TPU v7x, 32 devices: a whole 2x2x4 slice. The times are simulated.
32 devices in a mesh: groups: 2 (over y), dp: 16 (over z, x, core).
Axes of the slice: x: 2, y: 2, z: 4, core: 2. Of those that a mesh axis runs over, the one named last changes fastest.
Arguments:
- training_output_gradients: bfloat16 [64, 256, 4096], P(('groups', 'dp')), parts along dimension 0
- training_activations: bfloat16 [64, 256, 7168], P(('groups', 'dp')), parts along dimension 0
- train_ids: int32 [64, 256], P(('groups', 'dp')), parts along dimension 0, may hold values from 0 to 128255, as said below
- seq_index: int32 [64], P(('groups', 'dp')), parts along dimension 0, may hold values from 0 to 31, each once
- left_factor: bfloat16 [4096, 1024], P('dp', 'groups'), parts along dimension 1, may hold values from -0.09375 to 0.09375
- input_side_factor: bfloat16 [7168, 1024], P('dp', 'groups'), parts along dimension 1, may hold values from -0.0625 to 0.0625
- query_ids: int32 [32, 64], P('groups'), parts along dimension 0, may hold values from 0 to 128255, as said below
Outputs:
- influence: float32 [64, 16], P(('groups', 'dp')), parts along dimension 0
There are 2 independent parts, one for each index of `groups`. A program takes and returns all parts, laid end to end along the dimension named above; each array names one. Nothing has to cross between parts.
Inputs may be any that keep to these rules, and one draw needn't show every extreme that they name: `train_ids`: 0 marks padding and stands only at the end of a sequence; at least 128 leading tokens of every sequence are not 0. `query_ids`: 0 marks padding and stands only at the end of a completion; at least 32 leading tokens are not 0. `seq_index`: each position once.
All inputs are finite; a program needn't handle non-finite values.
Results may differ from a plain program's by a relative error of at most 0.0003.
Values may be sent and summed in bfloat16 or wider, within the bound.
No kernel may reach another device: no remote copies, remote signals or barrier semaphores. Data moves between devices by JAX's collectives and lax.ppermute only.
A program may use at most 64 MiB of HBM per device.

v0:
```python
import math

import jax
import jax.numpy as jnp
from jax import lax
from jax.sharding import PartitionSpec as P


def folder(features, piece):
    return jnp.dot(features, piece, preferred_element_type=jnp.float32)


def on_device(
    training_output_gradients,
    training_activations,
    train_ids,
    seq_index,
    left_factor,
    input_side_factor,
    query_ids,
):
    seq_count, length, width = training_output_gradients.shape
    hidden = training_activations.shape[2]
    columns = left_factor.shape[1]
    query_batch = query_ids.shape[0]
    rank = columns // query_batch
    grads_flat = training_output_gradients.reshape(seq_count * length, width)
    acts_flat = training_activations.reshape(seq_count * length, hidden)
    proj_out = folder(grads_flat, lax.all_gather(left_factor, "dp", axis=0, tiled=True))
    proj_in = folder(acts_flat, lax.all_gather(input_side_factor, "dp", axis=0, tiled=True))
    live = (train_ids != 0).astype(jnp.float32)
    product = (proj_out * proj_in).reshape(seq_count, length, columns) * live[:, :, None]
    raw = jnp.sum(jnp.sum(product, axis=1).reshape(seq_count, query_batch, rank), axis=2)
    output_covariance = jnp.einsum(
        "hcp,hqp->hcq",
        training_output_gradients,
        training_output_gradients,
        preferred_element_type=jnp.float32,
    )
    input_covariance = jnp.einsum(
        "hcp,hqp->hcq",
        training_activations,
        training_activations,
        preferred_element_type=jnp.float32,
    )
    grad_sq = jnp.sum(
        live[:, :, None] * live[:, None, :] * output_covariance * input_covariance, axis=(1, 2)
    )
    count = jnp.sum((query_ids != 0).astype(jnp.float32), axis=1)
    factor = query_ids.shape[1] * math.sqrt(width * hidden / rank)
    score = raw * factor / (count[None, :] * jnp.sqrt(grad_sq + 1e-06)[:, None])
    total_rows = seq_count * lax.axis_size("dp")
    slots = jnp.arange(total_rows, dtype=jnp.int32)
    onehot = (seq_index[:, None] == slots[None, :]).astype(jnp.float32)
    dense = jnp.einsum("rp,rq->pq", onehot, score, precision=lax.Precision.HIGHEST)
    influence = lax.psum_scatter(dense, "dp", scatter_dimension=0, tiled=True)
    return influence


def solution(mesh):
    in_specs = (
        P(("groups", "dp"), None, None),
        P(("groups", "dp"), None, None),
        P(("groups", "dp"), None),
        P(("groups", "dp")),
        P("dp", "groups"),
        P("dp", "groups"),
        P("groups", None),
    )
    out_specs = P(("groups", "dp"), None)
    return jax.shard_map(
        on_device, mesh=mesh, in_specs=in_specs, out_specs=out_specs, check_vma=False
    )
```

profile of v0, /device:TPU:0, one launch (start us, length us, event | category | flops | bytes accessed | tf_op | source)
XLA Modules:
  0.0 208.2 jit_solution(779440547868302542)
XLA Ops:
  6.5 0.0 all-gather.3.cloned.1.call-start
  6.5 0.7 all-gather.3.cloned.1.call-update
  7.3 0.0 all-gather.5.cloned.1.call-start
  7.3 0.7 all-gather.5.cloned.1.call-update
  8.0 1.2 dynamic-slice
  9.9 0.0 copy-start
  9.9 1.0 convert_reduce_fusion
  10.9 0.9 compare_convert_fusion
  11.7 5.0 %convolution_multiply_fusion.2 = f32[2,256,256]{2,1,0:T(8,128)S(1)} fusion(bf16[2,256,4096]{2,1,0:T(8,128)(2,1)} %param.7, f32[2,256]{1,0:T(2,128)S(1)} %compare_convert_fusion), kind=kOutput, calls=%fused_computation.2 | convolution fusion | flops 1074003968 | bytes 4720640 | tf_op jit(solution)/shard_map/hcp,hqp->hcq/dot_general | solution.py:34
  16.8 0.0 copy-done
  16.8 2.2 %fusion = f32[2]{0:T(128)S(1)} fusion(f32[2,256,256]{2,1,0:T(8,128)S(1)} %convolution_multiply_fusion.2, bf16[2,256,7168]{2,1,0:T(8,128)(2,1)S(1)} %copy-done), kind=kOutput, calls=%fused_computation.3 | convolution fusion | flops 1879310336 | bytes 7864328 | tf_op jit(solution)/shard_map/hcp,hqp->hcq/dot_general | solution.py:40
  19.0 44.0 %all-gather.3.cloned.1.call-done = bf16[4096,512]{1,0:T(8,128)(2,1)} async-done(((bf16[256,512]{1,0:T(8,128)(2,1)}), bf16[4096,512]{1,0:T(8,128)(2,1)}) %all-gather.3.cloned.1.call-update) | async-done | bytes 4194320 | tf_op jit(solution)/shard_map/all_gather | solution.py:29
  62.9 5.8 %fusion.12 = f32[512,512]{1,0:T(8,128)S(1)} fusion(bf16[512,4096]{1,0:T(8,128)(2,1)} %bitcast.14, bf16[4096,512]{1,0:T(8,128)(2,1)} %all-gather.3.cloned.1.call-done), kind=kOutput, calls=%fused_computation.20 | convolution fusion | flops 2147483648 | bytes 9437184 | tf_op jit(solution)/shard_map/dot_general | solution.py:10
  68.7 63.3 %all-gather.5.cloned.1.call-done = bf16[7168,512]{1,0:T(8,128)(2,1)} async-done(((bf16[448,512]{1,0:T(8,128)(2,1)}), bf16[7168,512]{1,0:T(8,128)(2,1)}) %all-gather.5.cloned.1.call-update) | async-done | bytes 7340048 | tf_op jit(solution)/shard_map/all_gather | solution.py:30
  132.0 0.0 copy-start.1
  132.0 9.2 %multiply_reduce_fusion = f32[2,512]{1,0:T(2,128)S(1)} fusion(f32[2,256]{1,0:T(2,128)S(1)} %compare_convert_fusion, f32[512,512]{1,0:T(8,128)S(1)} %fusion.12, bf16[512,7168]{1,0:T(8,128)(2,1)} %bitcast.13, bf16[7168,512]{1,0:T(8,128)(2,1)} %all-gather.5.cloned.1.call-done), kind=kOutput, calls=%fused_computation.4 | convolution fusion | flops 3758881792 | bytes 15734784 | tf_op jit(solution)/shard_map/dot_general | solution.py:10
  141.2 0.1 reshape.23
  141.3 0.1 reduce_sum.37
  141.4 0.0 copy-done.1
  141.4 0.3 fusion.1
  141.6 59.2 %all-reduce = f32[32,16]{1,0:T(8,128)S(1)} all-reduce(f32[32,16]{1,0:T(8,128)S(1)} %fusion.1), channel_id=2, replica_groups=mesh['groups'=2,'dp'=16] {'dp'}, use_global_device_ids=true, to_apply=%region_4.0.clone | all-reduce | flops 512 | bytes 4096
  200.8 0.6 constant_dynamic-slice_fusion
  (1 shorter events, 0.0 us)
Async XLA Ops:
  6.5 56.4 %all-gather.3.cloned.1.call-start = ((), (), s32[]{:S(2)}) async-start(), calls=%async_computation | async-start | bytes 4456448 | tf_op jit(solution)/shard_map/all_gather | solution.py:29
  7.3 124.8 %all-gather.5.cloned.1.call-start = ((), (), s32[]{:S(2)}) async-start(), calls=%async_computation.1 | async-start | bytes 7798784 | tf_op jit(solution)/shard_map/all_gather | solution.py:30
  9.9 6.9 %copy-start = (bf16[2,256,7168]{2,1,0:T(8,128)(2,1)S(1)}, bf16[2,256,7168]{2,1,0:T(8,128)(2,1)}, u32[]{:S(2)}) copy-start(bf16[2,256,7168]{2,1,0:T(8,128)(2,1)} %param.8) | copy-start | bytes 22020100
  132.0 9.3 %copy-start.1 = (s32[2]{0:T(128)S(1)}, s32[2]{0:T(128)}, u32[]{:S(2)}) copy-start(s32[2]{0:T(128)} %param.10) | copy-start | bytes 28
Sparse Core Ops, SparseCore 0:
  9.5 53.3 all-gather.2
  65.2 66.7 all-gather.4
where the time goes:
time: 208 us
  waiting for transfers between devices  109 us (52%)
  blocking collectives  59.2 us (28%)
  matrix products  22.4 us (11%)
  between operations  14.1 us (7%)
    all_gather x1, waiting for transfers between devices, on_device(): lax.all_gather(input_side_factor, 'dp', axis=0, tiled=True)  63.3 us
    unnamed x1, blocking collectives  59.2 us
    all_gather x1, waiting for transfers between devices, on_device(): lax.all_gather(left_factor, 'dp', axis=0, tiled=True)  44 us
    dot_general x2, matrix products, folder(): return jnp.dot(features, piece, preferred_element_type=jnp.float32)  14.9 us
    dot_general x1, matrix products, on_device(): jnp.einsum('hcp,hqp->hcq', training_output_gradients, training_output_gra...  5 us
  transfers between devices with their start and end apart: 2, of which 2 were waited for; matrix products, arithmetic and copies ran while one was open for 8% of the time, Pallas kernels for 0%

commit v1 on v0

v1 whole, which is shorter than its diff:
```python
import functools
import math

import jax
import jax.numpy as jnp
from jax import lax
from jax.experimental import pallas as pl
from jax.experimental.pallas import tpu as pltpu
from jax.sharding import PartitionSpec as P

AXIS = "dp"
MIB = 1 << 20


def ring_order(chips):
    return list(range(0, chips, 2)) + list(range(chips - 1, 0, -2))


def xor_pairs(devices, mask):
    return [(i, i ^ mask) for i in range(devices)]


def ring_pairs(order, shift):
    chips = len(order)
    return [
        (order[k] * 2 + core, order[(k + shift) % chips] * 2 + core)
        for k in range(chips)
        for core in range(2)
    ]


def send(x, pairs):
    return lax.ppermute(x, AXIS, pairs)


def in_order(*values):
    return lax.optimization_barrier(values)


def device_index():
    return lax.axis_index(AXIS)


def chip_on_ring(chips, chip, shift):
    place = jnp.where(chip % 2 == 0, chip // 2, chips - 1 - chip // 2)
    place = (place + shift + chips) % chips
    return jnp.where(place < chips // 2, 2 * place, 2 * (chips - 1 - place) + 1)


SMEM = pl.BlockSpec(memory_space=pltpu.SMEM)
VMEM = pl.BlockSpec(memory_space=pltpu.VMEM)
ANY = pl.BlockSpec(memory_space=pl.ANY)
FLOAT = jnp.float32


def params(limit=60):
    return pltpu.CompilerParams(vmem_limit_bytes=limit * MIB)


def small_cost():
    return pl.CostEstimate(flops=1, bytes_accessed=1, transcendentals=0)


def dot(a, b):
    return jnp.dot(a, b, preferred_element_type=FLOAT)


def dot_rows(a, b, precision=None):
    return lax.dot_general(
        a, b, (((1,), (1,)), ((), ())), precision=precision, preferred_element_type=FLOAT
    )


def exact_dot(a, b):
    return jnp.dot(a, b, precision=lax.Precision.HIGHEST, preferred_element_type=FLOAT)


class Rows:
    def __init__(self, chip, side, first, own, partner):
        self.chip, self.side, self.first = chip, side, first
        self.own, self.partner = own, partner

    def copies(self, per_device, own, partner, stacks, sems):
        core = device_index() % 2
        count = own.shape[0]
        result = []
        for j, (piece, place) in enumerate(((own, core), (partner, 1 - core))):
            base = place * per_device[self.side] + self.first
            target = stacks[self.side].at[self.chip, pl.ds(pl.multiple_of(base, 16), count), :]
            result.append(pltpu.make_async_copy(piece, target, sems.at[j]))
        return result


def project_kernel(per_device, shifts, chips, rows, fresh, *refs):
    grads, acts, refs = refs[0], refs[1], refs[2:]
    pieces, refs = refs[: 2 * len(rows)], refs[2 * len(rows) :]
    if not fresh:
        before, refs = refs[0], refs[1:]
    sums, left, right, lefts, rights, total, row_sems, block_sems, sum_sems = refs
    chip = device_index() // 2
    row_copies = [
        r.copies(per_device, pieces[2 * i], pieces[2 * i + 1], (lefts, rights), row_sems.at[i])
        for i, r in enumerate(rows)
    ]
    loads = []
    for k, shift in enumerate(shifts):
        there = chip_on_ring(chips, chip, shift)
        for j, (features, block) in enumerate(((grads, left), (acts, right))):
            width = block.shape[2]
            columns = pl.ds(pl.multiple_of(there * width, 128), width)
            loads.append(
                pltpu.make_async_copy(features.at[:, columns], block.at[k], block_sems.at[k, j])
            )
    old = [] if fresh else [
        pltpu.make_async_copy(before.at[j], total.at[j], sum_sems.at[0, j]) for j in range(2)
    ]
    new = [pltpu.make_async_copy(total.at[j], sums.at[j], sum_sems.at[1, j]) for j in range(2)]
    for j in range(2):
        for load in loads[j::2]:
            load.start()
        for r, copies in zip(rows, row_copies):
            if r.side == j:
                for copy in copies:
                    copy.start()
        if not fresh:
            old[j].start()
    for j, (block, stack) in enumerate(((left, lefts), (right, rights))):
        for load in loads[j::2]:
            load.wait()
        for r, copies in zip(rows, row_copies):
            if r.side == j:
                for copy in copies:
                    copy.wait()
        terms = [dot(block[k], stack[k]) for k in range(len(shifts))]
        if not fresh:
            old[j].wait()
            terms.append(total[j])
        total[j] = sum(terms)
        new[j].start()
    for copy in new:
        copy.wait()


def project(chips, shifts, grads, acts, per_device, rows, sums):
    count, tokens = len(shifts), grads.shape[0]
    columns = rows[0].own.shape[1]
    widths = [2 * n for n in per_device]
    sum_shape = (2, tokens, columns)
    before = [] if sums is None else [sums]
    pieces = [piece for r in rows for piece in (r.own, r.partner)]
    return pl.pallas_call(
        functools.partial(project_kernel, per_device, shifts, chips, rows, not before),
        in_specs=[ANY] * (2 + len(pieces) + len(before)),
        out_specs=ANY,
        out_shape=jax.ShapeDtypeStruct(sum_shape, FLOAT),
        scratch_shapes=[pltpu.VMEM((count, tokens, w), grads.dtype) for w in widths]
        + [pltpu.VMEM((count, w, columns), grads.dtype) for w in widths]
        + [
            pltpu.VMEM(sum_shape, FLOAT),
            pltpu.SemaphoreType.DMA((len(rows), 2)),
            pltpu.SemaphoreType.DMA((count, 2)),
            pltpu.SemaphoreType.DMA((2, 2)),
        ],
        compiler_params=params(),
        cost_estimate=small_cost(),
    )(grads, acts, *pieces, *before)


def fetch_kernel(chips, shift, grads, acts, left, right, left_held, right_held, sems):
    there = chip_on_ring(chips, device_index() // 2, shift)
    loads, stores = [], []
    for j, (features, held, block) in enumerate(
        ((grads, left_held, left), (acts, right_held, right))
    ):
        width = block.shape[1]
        columns = pl.ds(pl.multiple_of(there * width, 128), width)
        loads.append(pltpu.make_async_copy(features.at[:, columns], held, sems.at[j, 0]))
        stores.append(pltpu.make_async_copy(held, block, sems.at[j, 1]))
    for load in loads:
        load.start()
    for load, store in zip(loads, stores):
        load.wait()
        store.start()
    for store in stores:
        store.wait()


def fetch(chips, shift, grads, acts):
    shapes = [(x.shape[0], x.shape[1] // chips) for x in (grads, acts)]
    return pl.pallas_call(
        functools.partial(fetch_kernel, chips, shift),
        in_specs=[ANY, ANY],
        out_specs=[ANY, ANY],
        out_shape=[jax.ShapeDtypeStruct(s, grads.dtype) for s in shapes],
        scratch_shapes=[pltpu.VMEM(s, grads.dtype) for s in shapes]
        + [pltpu.SemaphoreType.DMA((2, 2))],
        compiler_params=params(),
        cost_estimate=small_cost(),
    )(grads, acts)


def finish_kernel(per_device, rows, rank, factor, *refs):
    pieces, refs = refs[: 2 * len(rows)], refs[2 * len(rows) :]
    left, right, sums, info, query_ids, dense, lefts, rights, sems = refs
    row_copies = [
        copy
        for i, r in enumerate(rows)
        for copy in r.copies(
            per_device, pieces[2 * i], pieces[2 * i + 1], (lefts, rights), sems.at[i]
        )
    ]
    for copy in row_copies:
        copy.start()
    columns = lefts.shape[2]
    queries = dense.shape[1]
    length = info.shape[2] - 128
    sequences = info.shape[0]
    column = lax.broadcasted_iota(jnp.int32, (columns, queries), 0)
    query = lax.broadcasted_iota(jnp.int32, (columns, queries), 1)
    member = (column // rank == query).astype(FLOAT)
    slot = lax.broadcasted_iota(jnp.int32, dense.shape, 0).astype(FLOAT)
    asked = (query_ids[...] != 0).astype(FLOAT)
    count = dot_rows(jnp.ones((8, asked.shape[1]), FLOAT), asked, lax.Precision.HIGHEST)
    placed = jnp.zeros(dense.shape, FLOAT)
    for copy in row_copies:
        copy.wait()
    for s in range(sequences):
        here = slice(s * length, (s + 1) * length)
        product = (sums[0, here, :] + dot(left[here, :], lefts[0])) * (
            sums[1, here, :] + dot(right[here, :], rights[0])
        )
        raw = exact_dot(exact_dot(info[s, :, 0:length], product), member)
        norm = jnp.sqrt(info[s, :, length : length + 1] + 1e-06)
        score = raw * factor / (count * norm)
        place = info[s, 0:1, length + 1 : length + 2]
        placed = placed + jnp.where(slot == place, score[0:1, :], 0.0)
    dense[...] = placed


def finish(per_device, rows, blocks, sums, info, query_ids, slots, rank, factor):
    columns = rows[0].own.shape[1]
    pieces = [piece for r in rows for piece in (r.own, r.partner)]
    return pl.pallas_call(
        functools.partial(finish_kernel, per_device, rows, rank, factor),
        in_specs=[ANY] * len(pieces) + [VMEM] * 5,
        out_specs=VMEM,
        out_shape=jax.ShapeDtypeStruct((slots, query_ids.shape[0]), FLOAT),
        scratch_shapes=[pltpu.VMEM((1, 2 * n, columns), pieces[0].dtype) for n in per_device]
        + [pltpu.SemaphoreType.DMA((len(rows), 2))],
        compiler_params=params(20),
        cost_estimate=small_cost(),
    )(*pieces, *blocks, sums, info, query_ids)


def info_kernel(steps, sequence, seq_index, grads, acts, ids, info, out_cov, in_cov):
    step = pl.program_id(0)

    @pl.when(step == 0)
    def _():
        out_cov[...] = dot_rows(grads[0], grads[0])

    for k in range(1, steps):

        @pl.when(step == k)
        def _(k=k):
            term = dot_rows(acts[0], acts[0])
            if k > 1:
                term = in_cov[...] + term
            if k < steps - 1:
                in_cov[...] = term
            else:
                length = out_cov.shape[0]
                live = jnp.broadcast_to((ids[0] != 0).astype(FLOAT), (8, length))
                rows = exact_dot(live, term * out_cov[...]) * live
                norm = jnp.sum(rows, axis=1, keepdims=True)
                lane = lax.broadcasted_iota(jnp.int32, (8, 128), 1)
                place = seq_index[sequence].astype(FLOAT)
                info[0, :, 0:length] = live
                info[0, :, length:] = jnp.where(lane == 0, norm, jnp.where(lane == 1, place, 0.0))


def sequence_info(sequence, seq_index, train_ids, grads, acts):
    length, width = grads.shape[1:]
    hidden = acts.shape[2]
    parts = 2 if hidden % 256 == 0 else 1
    steps = 1 + parts
    return pl.pallas_call(
        functools.partial(info_kernel, steps, sequence),
        grid=(steps,),
        in_specs=[
            SMEM,
            pl.BlockSpec((1, length, width), lambda k: (sequence, 0, 0)),
            pl.BlockSpec(
                (1, length, hidden // parts), lambda k: (sequence, 0, jnp.maximum(k - 1, 0))
            ),
            pl.BlockSpec((1, 1, length), lambda k: (sequence, 0, 0)),
        ],
        out_specs=pl.BlockSpec((1, 8, length + 128), lambda k: (0, 0, 0)),
        out_shape=jax.ShapeDtypeStruct((1, 8, length + 128), FLOAT),
        scratch_shapes=[pltpu.VMEM((length, length), FLOAT)] * 2,
        compiler_params=params(),
        cost_estimate=small_cost(),
    )(seq_index, grads, acts, train_ids[:, None, :])


def squared_norms(live, grads, acts):
    def covariance(x):
        return jnp.einsum("hcp,hqp->hcq", x, x, preferred_element_type=jnp.float32)

    return jnp.sum(
        live[:, :, None] * live[:, None, :] * covariance(grads) * covariance(acts), axis=(1, 2)
    )


def to_owners(dense, seq_count):
    devices = lax.axis_size(AXIS)
    if devices & (devices - 1):
        return lax.psum_scatter(dense, AXIS, scatter_dimension=0, tiled=True)
    mask = 1
    while mask < devices:
        dense = dense + send(dense, xor_pairs(devices, mask))
        mask *= 2
    return lax.dynamic_slice_in_dim(dense, lax.axis_index(AXIS) * seq_count, seq_count, axis=0)


def by_gathers(
    training_output_gradients, training_activations, train_ids, seq_index,
    left_factor, input_side_factor, query_ids,
):
    seq_count, length, width = training_output_gradients.shape
    hidden = training_activations.shape[2]
    columns = left_factor.shape[1]
    queries = query_ids.shape[0]
    rank = columns // queries
    grads = training_output_gradients.reshape(seq_count * length, width)
    acts = training_activations.reshape(seq_count * length, hidden)
    proj_out = dot(grads, lax.all_gather(left_factor, AXIS, axis=0, tiled=True))
    proj_in = dot(acts, lax.all_gather(input_side_factor, AXIS, axis=0, tiled=True))
    live = (train_ids != 0).astype(jnp.float32)
    product = (proj_out * proj_in).reshape(seq_count, length, columns) * live[:, :, None]
    raw = jnp.sum(jnp.sum(product, axis=1).reshape(seq_count, queries, rank), axis=2)
    grad_sq = squared_norms(live, training_output_gradients, training_activations)
    count = jnp.sum((query_ids != 0).astype(jnp.float32), axis=1)
    factor = query_ids.shape[1] * math.sqrt(width * hidden / rank)
    score = raw * factor / (count[None, :] * jnp.sqrt(grad_sq + 1e-06)[:, None])
    slots = jnp.arange(seq_count * lax.axis_size(AXIS), dtype=jnp.int32)
    dense = jnp.sum(
        jnp.where(seq_index[:, None, None] == slots[None, :, None], score[:, None, :], 0.0), axis=0
    )
    return to_owners(dense, seq_count)


def by_ring(
    training_output_gradients, training_activations, train_ids, seq_index,
    left_factor, input_side_factor, query_ids,
):
    seq_count, length, width = training_output_gradients.shape
    hidden = training_activations.shape[2]
    columns = left_factor.shape[1]
    queries = query_ids.shape[0]
    rank = columns // queries
    devices = lax.axis_size(AXIS)
    chips = devices // 2
    hops = chips // 2
    swap = xor_pairs(devices, 1)
    order = ring_order(chips)
    forward, backward = ring_pairs(order, 1), ring_pairs(order, -1)
    grads = training_output_gradients.reshape(seq_count * length, width)
    acts = training_activations.reshape(seq_count * length, hidden)
    per_device = (left_factor.shape[0], input_side_factor.shape[0])

    def with_partner(chip, side, first, piece):
        return Rows(chip, side, first, piece, send(piece, swap))

    lefts = [send(left_factor, forward), send(left_factor, backward)]
    rights = [send(input_side_factor, forward), send(input_side_factor, backward)]
    near = [with_partner(0, 0, 0, left_factor), with_partner(0, 1, 0, input_side_factor)]
    infos = [
        sequence_info(s, seq_index, train_ids, training_output_gradients, training_activations)
        for s in range(seq_count)
    ]
    sums = project(chips, [0], grads, acts, per_device, near, None)
    cut = (per_device[1] - per_device[0]) // 2 // 16 * 16
    for hop in range(1, hops):
        *lefts, sums = in_order(*lefts, sums)
        if hop <= len(infos):
            lefts[0], infos[hop - 1] = in_order(lefts[0], infos[hop - 1])
        behind = [with_partner(0, 0, 0, lefts[0])]
        ahead = [with_partner(1, 0, 0, lefts[1])]
        left_f, left_b = lefts
        lefts = [send(left_f, forward)]
        if hop + 1 < hops:
            lefts.append(send(left_b, backward))
        right_f, right_b = in_order(*rights)
        behind.append(with_partner(0, 1, 0, right_f))
        ahead.append(with_partner(1, 1, 0, right_b))
        if hop + 1 < hops:
            rights = [send(right_f, forward), send(right_b, backward)]
        else:
            rights = [send(right_f[:cut], forward), send(right_b[cut:], backward)]
        rows = [*behind, *ahead]
        sums = project(chips, [-hop, hop], grads, acts, per_device, rows, sums)
    rows = [
        with_partner(0, 0, 0, lefts[0]),
        with_partner(0, 1, 0, rights[0]),
        with_partner(0, 1, cut, rights[1]),
    ]
    blocks = fetch(chips, hops, grads, acts)
    info = jnp.concatenate(infos, axis=0)
    factor = query_ids.shape[1] * math.sqrt(width * hidden / rank)
    dense = finish(
        per_device, rows, blocks, sums, info, query_ids, seq_count * devices, rank, factor
    )
    return to_owners(dense, seq_count)


def on_device(*args):
    left_rows, right_rows = args[4].shape[0], args[5].shape[0]
    devices = lax.axis_size(AXIS)
    fits = (
        devices % 4 == 0
        and left_rows % 64 == 0
        and right_rows % 64 == 0
        and args[4].shape[1] % 256 == 0
        and args[6].shape[0] % 2 == 0
        and args[0].shape[1] % 128 == 0
        and (2 * left_rows) % 128 == 0
        and (2 * right_rows) % 128 == 0
    )
    return by_ring(*args) if fits else by_gathers(*args)


def solution(mesh):
    in_specs = (
        P(("groups", "dp"), None, None),
        P(("groups", "dp"), None, None),
        P(("groups", "dp"), None),
        P(("groups", "dp")),
        P("dp", "groups"),
        P("dp", "groups"),
        P("groups", None),
    )
    out_specs = P(("groups", "dp"), None)
    return jax.shard_map(
        on_device, mesh=mesh, in_specs=in_specs, out_specs=out_specs, check_vma=False
    )
```

time: 208 us -> 100 us (0.48)
  waiting for transfers between devices: 109 us -> 27.8 us
  blocking collectives: 59.2 us -> 0 us
  Pallas kernels: 0 us -> 38 us
  starting transfers between devices: 0.04 us -> 27.3 us
  matrix products: 22.4 us -> 0 us
  between operations: 14.1 us -> 0.4 us
  local copies, waits for them, and re-layouts: 1.9 us -> 5.96 us
    all_gather x2 -> x0, waiting for transfers between devices: 107 us -> none  [the longest x1 63.3 us: on_device(): lax.all_gather(input_side_factor, 'dp', axis=0, tiled=True)]
    unnamed x1 -> x0, blocking collectives: 59.2 us -> none
    pallas_call x0 -> x8, Pallas kernels: none -> 38 us  [the longest x4 20.3 us: project(): pl.pallas_call(functools.partial(project_kernel, per_device, shifts, chip...]
    ppermute x0 -> x36, waiting for transfers between devices: none -> 27.8 us  [send(): return lax.ppermute(x, AXIS, pairs)]
    ppermute x0 -> x36, starting transfers between devices: none -> 27.3 us  [send(): return lax.ppermute(x, AXIS, pairs)]
    dot_general x5 -> x0, matrix products: 22.4 us -> none  [the longest x2 14.9 us: folder(): return jnp.dot(features, piece, preferred_element_type=jnp.float32)]
    unnamed x6 -> x50, local copies, waits for them, and re-layouts: 1.82 us -> 4.65 us
  transfers between devices with their start and end apart: 2 -> 36, of which waited for: 2 -> 10; matrix products, arithmetic and copies ran while one was open for 8% -> 1% of each run, Pallas kernels for 0% -> 35%
where the time goes in v1:
time: 100 us
  Pallas kernels  38 us (38%)
  waiting for transfers between devices  27.8 us (28%)
  starting transfers between devices  27.3 us (27%)
  local copies, waits for them, and re-layouts  5.96 us (6%)
    ppermute x36, waiting for transfers between devices, send(): return lax.ppermute(x, AXIS, pairs)  27.8 us
    ppermute x36, starting transfers between devices, send(): return lax.ppermute(x, AXIS, pairs)  27.3 us
    pallas_call x4, Pallas kernels, project(): pl.pallas_call(functools.partial(project_kernel, per_device, shifts, chip...  20.3 us
    pallas_call x2, Pallas kernels, sequence_info(): pl.pallas_call(functools.partial(info_kernel, steps, sequence), grid=(ste...  12.4 us
    unnamed x50, local copies, waits for them, and re-layouts  4.65 us
    pallas_call x1, Pallas kernels, finish(): pl.pallas_call(functools.partial(finish_kernel, per_device, rows, rank, f...  2.92 us
    pallas_call x1, Pallas kernels, fetch(): pl.pallas_call(functools.partial(fetch_kernel, chips, shift), in_specs=[A...  2.33 us
  transfers between devices with their start and end apart: 36, of which 10 were waited for; matrix products, arithmetic and copies ran while one was open for 1% of the time, Pallas kernels for 35%

profile of v1, /device:TPU:0, one launch (start us, length us, event | category | flops | bytes accessed | tf_op | source)
XLA Modules:
  0.0 100.1 jit_solution(8533255332000836635)
XLA Ops:
  0.0 3.0 %collective-permute-start.7 = (bf16[448,512]{1,0:T(8,128)(2,1)}, bf16[448,512]{1,0:T(8,128)(2,1)S(1)}, u32[]{:S(2)}, u32[]{:S(2)}) collective-permute-start(bf16[448,512]{1,0:T(8,128)(2,1)} %refs_4_.1), channel_id=1, source_target_pairs={{0,4},{1,5},{4,8},{5,9},{8,12},{9,13},{12,14},{13,15},{14,10},{15,... | collective-permute-start | bytes 1376264 | tf_op jit(solution)/shard_map/ppermute | solution.py:33
  3.0 0.5 collective-permute-start.2
  3.5 2.0 %collective-permute-start = (bf16[256,512]{1,0:T(8,128)(2,1)}, bf16[256,512]{1,0:T(8,128)(2,1)S(1)}, u32[]{:S(2)}, u32[]{:S(2)}) collective-permute-start(bf16[256,512]{1,0:T(8,128)(2,1)} %refs_2_.1), channel_id=1, source_target_pairs={{0,4},{1,5},{4,8},{5,9},{8,12},{9,13},{12,14},{13,15},{14,10},{15,... | collective-permute-start | bytes 786440 | tf_op jit(solution)/shard_map/ppermute | solution.py:33
  5.6 8.9 %collective-permute-done.7.refs_4_ = bf16[448,512]{1,0:T(8,128)(2,1)S(1)} collective-permute-done((bf16[448,512]{1,0:T(8,128)(2,1)}, bf16[448,512]{1,0:T(8,128)(2,1)S(1)}, u32[]{:S(2)}, u32[]{:S(2)}) %collective-permute-start.7) | collective-permute-done | bytes 458784 | tf_op jit(solution)/shard_map/ppermute | solution.py:33
  14.5 2.1 %collective-permute-start.1 = (bf16[256,512]{1,0:T(8,128)(2,1)}, bf16[256,512]{1,0:T(8,128)(2,1)S(1)}, u32[]{:S(2)}, u32[]{:S(2)}) collective-permute-start(bf16[256,512]{1,0:T(8,128)(2,1)} %refs_2_.1), channel_id=1, source_target_pairs={{0,2},{1,3},{4,0},{5,1},{8,4},{9,5},{12,8},{13,9},{14,12},{15,13},... | collective-permute-start | bytes 786440 | tf_op jit(solution)/shard_map/ppermute | solution.py:33
  16.6 0.0 collective-permute-done.8.refs_8_
  16.6 0.2 collective-permute-start.15
  16.8 0.0 collective-permute-done.2.refs_3_
  16.8 1.8 %collective-permute-start.16 = (bf16[448,512]{1,0:T(8,128)(2,1)S(1)}, bf16[448,512]{1,0:T(8,128)(2,1)S(1)}, u32[]{:S(2)}, u32[]{:S(2)}) collective-permute-start(bf16[448,512]{1,0:T(8,128)(2,1)S(1)} %collective-permute-done.8.refs_8_), channel_id=1, source_target_pairs={{0,2},{1,3},{4,0},{5,1},{8,4},{9,5},{12,8},{13,9},{14,12},{15,13},... | collective-permute-start | bytes 1376264 | tf_op jit(solution)/shard_map/ppermute | solution.py:33
  18.6 1.3 %broadcast_in_dim.4.ids = s32[2,1,256]{2,1,0:T(1,128)} reshape(s32[2,256]{1,0:T(2,128)} %param.9) | data formatting | bytes 4096 | tf_op jit(solution)/shard_map/broadcast_in_dim | solution.py:303
  19.9 6.2 %shard_map.74 = f32[1,8,384]{2,1,0:T(8,128)} custom-call(s32[2]{0:T(128)} %seq_index.3, bf16[2,256,4096]{2,1,0:T(8,128)(2,1)} %grads.3, bf16[2,256,7168]{2,1,0:T(8,128)(2,1)} %acts.3, s32[2,1,256]{2,1,0:T(1,128)} %broadcast_in_dim.4.ids), custom_call_target="tpu_custom_call" | custom-call | flops 1 | bytes 1 | tf_op jit(solution)/shard_map/pallas_call | solution.py:287
  26.1 0.8 copy-done.13
  26.9 3.7 %shard_map.73.refs_10_ = f32[2,512,512]{2,1,0:T(8,128)} custom-call(bf16[512,4096]{1,0:T(8,128)(2,1)} %bitcast.7, bf16[512,7168]{1,0:T(8,128)(2,1)} %bitcast.2, bf16[256,512]{1,0:T(8,128)(2,1)} %refs_2_.1, bf16[256,512]{1,0:T(8,128)(2,1)} %copy-done.22, bf16[448,512]{1,0:T(8,128)(2,1)} %refs_4_.1, bf16[448,512]{1,0:T(8,128)(2,1)} %copy-done.13), custom_call_target="tpu_custom_call" | custom-call | flops 1 | bytes 1 | tf_op jit(solution)/shard_map/pallas_call | solution.py:151
  30.6 0.1 collective-permute-start.6
  30.7 0.5 collective-permute-start.11
  31.2 0.1 collective-permute-start.9
  31.3 0.9 collective-permute-done.6.refs_3_
  32.2 0.1 collective-permute-start.10
  32.4 0.3 collective-permute-start.4
  32.6 0.0 collective-permute-done.16.refs_8_
  32.6 1.8 %collective-permute-start.5 = (bf16[256,512]{1,0:T(8,128)(2,1)S(1)}, bf16[256,512]{1,0:T(8,128)(2,1)}, u32[]{:S(2)}, u32[]{:S(2)}) collective-permute-start(bf16[256,512]{1,0:T(8,128)(2,1)S(1)} %collective-permute-done.1.refs_6_), channel_id=1, source_target_pairs={{0,2},{1,3},{4,0},{5,1},{8,4},{9,5},{12,8},{13,9},{14,12},{15,13},... | collective-permute-start | bytes 786440 | tf_op jit(solution)/shard_map/ppermute | solution.py:33
  34.4 0.0 collective-permute-done.10.refs_7_
  34.4 0.3 collective-permute-start.22
  34.7 0.4 copy-done.21
  35.1 1.6 %collective-permute-start.23 = (bf16[448,512]{1,0:T(8,128)(2,1)S(1)}, bf16[448,512]{1,0:T(8,128)(2,1)S(1)}, u32[]{:S(2)}, u32[]{:S(2)}) collective-permute-start(bf16[448,512]{1,0:T(8,128)(2,1)S(1)} %collective-permute-done.16.refs_8_), channel_id=1, source_target_pairs={{0,2},{1,3},{4,0},{5,1},{8,4},{9,5},{12,8},{13,9},{14,12},{15,13},... | collective-permute-start | bytes 1376264 | tf_op jit(solution)/shard_map/ppermute | solution.py:33
  36.7 6.2 %shard_map.76 = f32[1,8,384]{2,1,0:T(8,128)} custom-call(s32[2]{0:T(128)} %seq_index.3, bf16[2,256,4096]{2,1,0:T(8,128)(2,1)} %grads.3, bf16[2,256,7168]{2,1,0:T(8,128)(2,1)} %acts.3, s32[2,1,256]{2,1,0:T(1,128)} %broadcast_in_dim.4.ids), custom_call_target="tpu_custom_call" | custom-call | flops 1 | bytes 1 | tf_op jit(solution)/shard_map/pallas_call | solution.py:287
  42.9 5.5 %shard_map.75.refs_10_ = f32[2,512,512]{2,1,0:T(8,128)} custom-call(bf16[512,4096]{1,0:T(8,128)(2,1)} %bitcast.8, bf16[512,7168]{1,0:T(8,128)(2,1)} %bitcast.3, bf16[256,512]{1,0:T(8,128)(2,1)} %copy-done.15, bf16[256,512]{1,0:T(8,128)(2,1)} %copy-done.18, bf16[448,512]{1,0:T(8,128)(2,1)} %copy-done.8, bf16[448,512]{1,0:T(8,128)(2,1)} %collective-permute-done.9.refs_5_, ...), custom_call_target="tpu_custom_call" | custom-call | flops 1 | bytes 1 | tf_op jit(solution)/shard_map/pallas_call | solution.py:151
  48.4 0.0 collective-permute-done.4.refs_2_
  48.4 0.1 collective-permute-start.14
  48.5 0.5 collective-permute-start.17
  49.0 0.1 collective-permute-start.19
  49.1 1.1 %collective-permute-done.14.refs_3_ = bf16[256,512]{1,0:T(8,128)(2,1)S(1)} collective-permute-done((bf16[256,512]{1,0:T(8,128)(2,1)}, bf16[256,512]{1,0:T(8,128)(2,1)S(1)}, u32[]{:S(2)}, u32[]{:S(2)}) %collective-permute-start.14) | collective-permute-done | bytes 262176 | tf_op jit(solution)/shard_map/ppermute | solution.py:33
  50.3 0.1 collective-permute-start.18
  50.4 0.4 collective-permute-done.22.refs_4_
  50.8 0.3 collective-permute-start.12
  51.1 1.8 %collective-permute-start.13 = (bf16[256,512]{1,0:T(8,128)(2,1)}, bf16[256,512]{1,0:T(8,128)(2,1)}, u32[]{:S(2)}, u32[]{:S(2)}) collective-permute-start(bf16[256,512]{1,0:T(8,128)(2,1)} %collective-permute-done.5.refs_6_), channel_id=1, source_target_pairs={{0,2},{1,3},{4,0},{5,1},{8,4},{9,5},{12,8},{13,9},{14,12},{15,13},... | collective-permute-start | bytes 786440 | tf_op jit(solution)/shard_map/ppermute | solution.py:33
  52.9 1.7 %collective-permute-start.26 = (bf16[352,512]{1,0:T(8,128)(2,1)S(1)}, bf16[352,512]{1,0:T(8,128)(2,1)S(1)}, u32[]{:S(2)}, u32[]{:S(2)}) collective-permute-start(bf16[352,512]{1,0:T(8,128)(2,1)S(1)} %slice.7), channel_id=1, source_target_pairs={{0,2},{1,3},{4,0},{5,1},{8,4},{9,5},{12,8},{13,9},{14,12},{15,13},... | collective-permute-start | bytes 1081352 | tf_op jit(solution)/shard_map/ppermute | solution.py:33
  54.6 0.8 copy-done.11
  55.3 0.8 copy-done.12
  56.1 5.6 %shard_map.77.refs_10_ = f32[2,512,512]{2,1,0:T(8,128)} custom-call(bf16[512,4096]{1,0:T(8,128)(2,1)} %bitcast.9, bf16[512,7168]{1,0:T(8,128)(2,1)} %bitcast.4, bf16[256,512]{1,0:T(8,128)(2,1)} %collective-permute-done.4.refs_2_, bf16[256,512]{1,0:T(8,128)(2,1)} %copy-done.19, bf16[448,512]{1,0:T(8,128)(2,1)} %copy-done.6, bf16[448,512]{1,0:T(8,128)(2,1)} %copy-done.11, ...), custom_call_target="tpu_custom_call" | custom-call | flops 1 | bytes 1 | tf_op jit(solution)/shard_map/pallas_call | solution.py:151
  61.7 0.1 collective-permute-start.28
  61.8 0.8 collective-permute-start.24
  62.6 1.6 %collective-permute-start.20 = (bf16[256,512]{1,0:T(8,128)(2,1)S(1)}, bf16[256,512]{1,0:T(8,128)(2,1)S(1)}, u32[]{:S(2)}, u32[]{:S(2)}) collective-permute-start(bf16[256,512]{1,0:T(8,128)(2,1)S(1)} %collective-permute-done.12.refs_2_), channel_id=1, source_target_pairs={{0,4},{1,5},{4,8},{5,9},{8,12},{9,13},{12,14},{13,15},{14,10},{15,... | collective-permute-start | bytes 786440 | tf_op jit(solution)/shard_map/ppermute | solution.py:33
  64.2 3.3 %collective-permute-done.24.refs_2_ = bf16[96,512]{1,0:T(8,128)(2,1)S(1)} collective-permute-done((bf16[96,512]{1,0:T(8,128)(2,1)S(1)}, bf16[96,512]{1,0:T(8,128)(2,1)S(1)}, u32[]{:S(2)}, u32[]{:S(2)}) %collective-permute-start.24) | collective-permute-done | bytes 98336 | tf_op jit(solution)/shard_map/ppermute | solution.py:33
  67.5 0.5 collective-permute-start.30
  68.0 0.1 collective-permute-start.27
  68.1 0.1 copy-done.17
  68.2 4.5 %collective-permute-done.20.refs_0_ = bf16[256,512]{1,0:T(8,128)(2,1)S(1)} collective-permute-done((bf16[256,512]{1,0:T(8,128)(2,1)S(1)}, bf16[256,512]{1,0:T(8,128)(2,1)S(1)}, u32[]{:S(2)}, u32[]{:S(2)}) %collective-permute-start.20) | collective-permute-done | bytes 262176 | tf_op jit(solution)/shard_map/ppermute | solution.py:33
  72.7 2.3 %shard_map.78 = (bf16[512,512]{1,0:T(8,128)(2,1)}, bf16[512,896]{1,0:T(8,128)(2,1)}) custom-call(bf16[512,4096]{1,0:T(8,128)(2,1)} %bitcast.10, bf16[512,7168]{1,0:T(8,128)(2,1)} %bitcast.5), custom_call_target="tpu_custom_call" | custom-call | flops 1 | bytes 1 | tf_op jit(solution)/shard_map/pallas_call | solution.py:190
  75.0 0.6 collective-permute-start.25
  75.6 0.1 copy-done.20
  75.8 0.0 copy-start.3
  75.8 5.6 %shard_map.79.refs_8_ = f32[2,512,512]{2,1,0:T(8,128)} custom-call(bf16[512,4096]{1,0:T(8,128)(2,1)} %bitcast.11, bf16[512,7168]{1,0:T(8,128)(2,1)} %bitcast.6, bf16[256,512]{1,0:T(8,128)(2,1)} %copy-done.14, bf16[256,512]{1,0:T(8,128)(2,1)} %copy-done.17, bf16[448,512]{1,0:T(8,128)(2,1)} %copy-done.5, bf16[448,512]{1,0:T(8,128)(2,1)} %collective-permute-done.29.refs_5_, ...), custom_call_target="tpu_custom_call" | custom-call | flops 1 | bytes 1 | tf_op jit(solution)/shard_map/pallas_call | solution.py:151
  81.5 1.6 %copy-done = f32[2,512,512]{2,1,0:T(8,128)S(1)} copy-done((f32[2,512,512]{2,1,0:T(8,128)S(1)}, f32[2,512,512]{2,1,0:T(8,128)}, u32[]{:S(2)}) %copy-start) | copy-done | bytes 2097176
  83.0 2.9 %shard_map.80 = f32[32,16]{1,0:T(8,128)S(1)} custom-call(bf16[256,512]{1,0:T(8,128)(2,1)S(1)} %collective-permute-done.20.refs_0_, bf16[256,512]{1,0:T(8,128)(2,1)S(1)} %collective-permute-done.21.refs_1_, bf16[96,512]{1,0:T(8,128)(2,1)S(1)} %collective-permute-done.24.refs_2_, bf16[96,512]{1,0:T(8,128)(2,1)S(1)} %collective-permute-done.25.refs_3_, ...), custom_call_target="tpu_custom_call" | custom-call | flops 1 | bytes 1 | tf_op jit(solution)/shard_map/pallas_call | solution.py:243
  86.0 0.6 collective-permute-start.32
  86.5 0.8 collective-permute-done.32
  87.4 1.6 %collective-permute-start.33 = (f32[32,16]{1,0:T(8,128)S(1)}, f32[32,16]{1,0:T(8,128)S(1)}, u32[]{:S(2)}, u32[]{:S(2)}) collective-permute-start(f32[32,16]{1,0:T(8,128)S(1)} %add.15), channel_id=1, source_target_pairs={{0,2},{1,3},{2,0},{3,1},{4,6},{5,7},{6,4},{7,5},{8,10},{9,11},{10,... | collective-permute-start | bytes 6152 | tf_op jit(solution)/shard_map/ppermute | solution.py:33
  89.0 2.2 %collective-permute-done.33 = f32[32,16]{1,0:T(8,128)S(1)} collective-permute-done((f32[32,16]{1,0:T(8,128)S(1)}, f32[32,16]{1,0:T(8,128)S(1)}, u32[]{:S(2)}, u32[]{:S(2)}) %collective-permute-start.33) | collective-permute-done | bytes 2080 | tf_op jit(solution)/shard_map/ppermute | solution.py:33
  91.1 1.0 %collective-permute-start.34 = (f32[32,16]{1,0:T(8,128)S(1)}, f32[32,16]{1,0:T(8,128)S(1)}, u32[]{:S(2)}, u32[]{:S(2)}) collective-permute-start(f32[32,16]{1,0:T(8,128)S(1)} %add.16), channel_id=1, source_target_pairs={{0,4},{1,5},{2,6},{3,7},{4,0},{5,1},{6,2},{7,3},{8,12},{9,13},{10,... | collective-permute-start | bytes 6152 | tf_op jit(solution)/shard_map/ppermute | solution.py:33
  92.2 2.7 %collective-permute-done.34 = f32[32,16]{1,0:T(8,128)S(1)} collective-permute-done((f32[32,16]{1,0:T(8,128)S(1)}, f32[32,16]{1,0:T(8,128)S(1)}, u32[]{:S(2)}, u32[]{:S(2)}) %collective-permute-start.34) | collective-permute-done | bytes 2080 | tf_op jit(solution)/shard_map/ppermute | solution.py:33
  94.9 1.7 %collective-permute-start.35 = (f32[32,16]{1,0:T(8,128)S(1)}, f32[32,16]{1,0:T(8,128)S(1)}, u32[]{:S(2)}, u32[]{:S(2)}) collective-permute-start(f32[32,16]{1,0:T(8,128)S(1)} %add.17), channel_id=1, source_target_pairs={{0,8},{1,9},{2,10},{3,11},{4,12},{5,13},{6,14},{7,15},{8,0},{9,1},... | collective-permute-start | bytes 6152 | tf_op jit(solution)/shard_map/ppermute | solution.py:33
  96.6 2.9 %collective-permute-done.35 = f32[32,16]{1,0:T(8,128)S(1)} collective-permute-done((f32[32,16]{1,0:T(8,128)S(1)}, f32[32,16]{1,0:T(8,128)S(1)}, u32[]{:S(2)}, u32[]{:S(2)}) %collective-permute-start.35) | collective-permute-done | bytes 2080 | tf_op jit(solution)/shard_map/ppermute | solution.py:33
  99.5 0.6 dynamic-slice_add_fusion
  (74 shorter events, 0.2 us)
Async XLA Ops:
  0.0 14.5 %collective-permute-start.7 = (bf16[448,512]{1,0:T(8,128)(2,1)}, bf16[448,512]{1,0:T(8,128)(2,1)S(1)}, u32[]{:S(2)}, u32[]{:S(2)}) collective-permute-start(bf16[448,512]{1,0:T(8,128)(2,1)} %refs_4_.1), channel_id=1, source_target_pairs={{0,4},{1,5},{4,8},{5,9},{8,12},{9,13},{12,14},{13,15},{14,10},{15,... | collective-permute-start | bytes 1376264 | tf_op jit(solution)/shard_map/ppermute | solution.py:33
  3.0 13.5 %collective-permute-start.8 = (bf16[448,512]{1,0:T(8,128)(2,1)}, bf16[448,512]{1,0:T(8,128)(2,1)S(1)}, u32[]{:S(2)}, u32[]{:S(2)}) collective-permute-start(bf16[448,512]{1,0:T(8,128)(2,1)} %refs_4_.1), channel_id=1, source_target_pairs={{0,2},{1,3},{4,0},{5,1},{8,4},{9,5},{12,8},{13,9},{14,12},{15,13},... | collective-permute-start | bytes 1376264 | tf_op jit(solution)/shard_map/ppermute | solution.py:33
  3.0 23.0 %collective-permute-start.3 = (bf16[448,512]{1,0:T(8,128)(2,1)}, bf16[448,512]{1,0:T(8,128)(2,1)S(1)}, u32[]{:S(2)}, u32[]{:S(2)}) collective-permute-start(bf16[448,512]{1,0:T(8,128)(2,1)} %refs_4_.1), channel_id=1, source_target_pairs={{0,1},{1,0},{2,3},{3,2},{4,5},{5,4},{6,7},{7,6},{8,9},{9,8},{10,11... | collective-permute-start | bytes 1376264 | tf_op jit(solution)/shard_map/ppermute | solution.py:33
  3.0 13.8 %collective-permute-start.2 = (bf16[256,512]{1,0:T(8,128)(2,1)}, bf16[256,512]{1,0:T(8,128)(2,1)S(1)}, u32[]{:S(2)}, u32[]{:S(2)}) collective-permute-start(bf16[256,512]{1,0:T(8,128)(2,1)} %refs_2_.1), channel_id=1, source_target_pairs={{0,1},{1,0},{2,3},{3,2},{4,5},{5,4},{6,7},{7,6},{8,9},{9,8},{10,11... | collective-permute-start | bytes 786440 | tf_op jit(solution)/shard_map/ppermute | solution.py:33
  3.5 27.0 %collective-permute-start = (bf16[256,512]{1,0:T(8,128)(2,1)}, bf16[256,512]{1,0:T(8,128)(2,1)S(1)}, u32[]{:S(2)}, u32[]{:S(2)}) collective-permute-start(bf16[256,512]{1,0:T(8,128)(2,1)} %refs_2_.1), channel_id=1, source_target_pairs={{0,4},{1,5},{4,8},{5,9},{8,12},{9,13},{12,14},{13,15},{14,10},{15,... | collective-permute-start | bytes 786440 | tf_op jit(solution)/shard_map/ppermute | solution.py:33
  14.5 16.7 %copy-start.8 = (bf16[448,512]{1,0:T(8,128)(2,1)}, bf16[448,512]{1,0:T(8,128)(2,1)S(1)}, u32[]{:S(2)}) copy-start(bf16[448,512]{1,0:T(8,128)(2,1)S(1)} %collective-permute-done.7.refs_4_) | copy-start | bytes 1376260
  14.5 16.1 %collective-permute-start.1 = (bf16[256,512]{1,0:T(8,128)(2,1)}, bf16[256,512]{1,0:T(8,128)(2,1)S(1)}, u32[]{:S(2)}, u32[]{:S(2)}) collective-permute-start(bf16[256,512]{1,0:T(8,128)(2,1)} %refs_2_.1), channel_id=1, source_target_pairs={{0,2},{1,3},{4,0},{5,1},{8,4},{9,5},{12,8},{13,9},{14,12},{15,13},... | collective-permute-start | bytes 786440 | tf_op jit(solution)/shard_map/ppermute | solution.py:33
  16.6 14.1 %copy-start.9 = (bf16[448,512]{1,0:T(8,128)(2,1)}, bf16[448,512]{1,0:T(8,128)(2,1)S(1)}, u32[]{:S(2)}) copy-start(bf16[448,512]{1,0:T(8,128)(2,1)S(1)} %collective-permute-done.8.refs_8_) | copy-start | bytes 1376260
  16.6 15.8 %collective-permute-start.15 = (bf16[448,512]{1,0:T(8,128)(2,1)S(1)}, bf16[448,512]{1,0:T(8,128)(2,1)S(1)}, u32[]{:S(2)}, u32[]{:S(2)}) collective-permute-start(bf16[448,512]{1,0:T(8,128)(2,1)S(1)} %collective-permute-done.7.refs_4_), channel_id=1, source_target_pairs={{0,4},{1,5},{4,8},{5,9},{8,12},{9,13},{12,14},{13,15},{14,10},{15,... | collective-permute-start | bytes 1376264 | tf_op jit(solution)/shard_map/ppermute | solution.py:33
  16.8 9.3 %copy-start.22 = (bf16[256,512]{1,0:T(8,128)(2,1)}, bf16[256,512]{1,0:T(8,128)(2,1)S(1)}, u32[]{:S(2)}) copy-start(bf16[256,512]{1,0:T(8,128)(2,1)S(1)} %collective-permute-done.2.refs_3_) | copy-start | bytes 786436
  16.8 15.8 %collective-permute-start.16 = (bf16[448,512]{1,0:T(8,128)(2,1)S(1)}, bf16[448,512]{1,0:T(8,128)(2,1)S(1)}, u32[]{:S(2)}, u32[]{:S(2)}) collective-permute-start(bf16[448,512]{1,0:T(8,128)(2,1)S(1)} %collective-permute-done.8.refs_8_), channel_id=1, source_target_pairs={{0,2},{1,3},{4,0},{5,1},{8,4},{9,5},{12,8},{13,9},{14,12},{15,13},... | collective-permute-start | bytes 1376264 | tf_op jit(solution)/shard_map/ppermute | solution.py:33
  26.1 0.8 copy-start.13
  30.6 12.3 %copy-start.15 = (bf16[256,512]{1,0:T(8,128)(2,1)}, bf16[256,512]{1,0:T(8,128)(2,1)S(1)}, u32[]{:S(2)}) copy-start(bf16[256,512]{1,0:T(8,128)(2,1)S(1)} %collective-permute-done.refs_2_) | copy-start | bytes 786436
  30.6 12.3 %copy-start.16 = (bf16[256,512]{1,0:T(8,128)(2,1)}, bf16[256,512]{1,0:T(8,128)(2,1)S(1)}, u32[]{:S(2)}) copy-start(bf16[256,512]{1,0:T(8,128)(2,1)S(1)} %collective-permute-done.1.refs_6_) | copy-start | bytes 786436
  30.6 1.6 %collective-permute-start.6 = (bf16[256,512]{1,0:T(8,128)(2,1)S(1)}, bf16[256,512]{1,0:T(8,128)(2,1)S(1)}, u32[]{:S(2)}, u32[]{:S(2)}) collective-permute-start(bf16[256,512]{1,0:T(8,128)(2,1)S(1)} %collective-permute-done.refs_2_), channel_id=1, source_target_pairs={{0,1},{1,0},{2,3},{3,2},{4,5},{5,4},{6,7},{7,6},{8,9},{9,8},{10,11... | collective-permute-start | bytes 786440 | tf_op jit(solution)/shard_map/ppermute | solution.py:33
  30.7 4.4 %collective-permute-start.11 = (bf16[448,512]{1,0:T(8,128)(2,1)S(1)}, bf16[448,512]{1,0:T(8,128)(2,1)S(1)}, u32[]{:S(2)}, u32[]{:S(2)}) collective-permute-start(bf16[448,512]{1,0:T(8,128)(2,1)S(1)} %collective-permute-done.8.refs_8_), channel_id=1, source_target_pairs={{0,1},{1,0},{2,3},{3,2},{4,5},{5,4},{6,7},{7,6},{8,9},{9,8},{10,11... | collective-permute-start | bytes 1376264 | tf_op jit(solution)/shard_map/ppermute | solution.py:33
  31.2 11.7 %collective-permute-start.9 = (bf16[448,512]{1,0:T(8,128)(2,1)S(1)}, bf16[448,512]{1,0:T(8,128)(2,1)}, u32[]{:S(2)}, u32[]{:S(2)}) collective-permute-start(bf16[448,512]{1,0:T(8,128)(2,1)S(1)} %collective-permute-done.7.refs_4_), channel_id=1, source_target_pairs={{0,1},{1,0},{2,3},{3,2},{4,5},{5,4},{6,7},{7,6},{8,9},{9,8},{10,11... | collective-permute-start | bytes 1376264 | tf_op jit(solution)/shard_map/ppermute | solution.py:33
  32.2 2.5 %copy-start.18 = (bf16[256,512]{1,0:T(8,128)(2,1)}, bf16[256,512]{1,0:T(8,128)(2,1)S(1)}, u32[]{:S(2)}) copy-start(bf16[256,512]{1,0:T(8,128)(2,1)S(1)} %collective-permute-done.6.refs_3_) | copy-start | bytes 786436
  32.2 2.2 %collective-permute-start.10 = (bf16[256,512]{1,0:T(8,128)(2,1)S(1)}, bf16[256,512]{1,0:T(8,128)(2,1)S(1)}, u32[]{:S(2)}, u32[]{:S(2)}) collective-permute-start(bf16[256,512]{1,0:T(8,128)(2,1)S(1)} %collective-permute-done.1.refs_6_), channel_id=1, source_target_pairs={{0,1},{1,0},{2,3},{3,2},{4,5},{5,4},{6,7},{7,6},{8,9},{9,8},{10,11... | collective-permute-start | bytes 786440 | tf_op jit(solution)/shard_map/ppermute | solution.py:33
  32.4 16.2 %copy-start.6 = (bf16[448,512]{1,0:T(8,128)(2,1)}, bf16[448,512]{1,0:T(8,128)(2,1)S(1)}, u32[]{:S(2)}) copy-start(bf16[448,512]{1,0:T(8,128)(2,1)S(1)} %collective-permute-done.15.refs_4_) | copy-start | bytes 1376260
  32.4 16.1 %collective-permute-start.4 = (bf16[256,512]{1,0:T(8,128)(2,1)S(1)}, bf16[256,512]{1,0:T(8,128)(2,1)}, u32[]{:S(2)}, u32[]{:S(2)}) collective-permute-start(bf16[256,512]{1,0:T(8,128)(2,1)S(1)} %collective-permute-done.refs_2_), channel_id=1, source_target_pairs={{0,4},{1,5},{4,8},{5,9},{8,12},{9,13},{12,14},{13,15},{14,10},{15,... | collective-permute-start | bytes 786440 | tf_op jit(solution)/shard_map/ppermute | solution.py:33
  32.6 16.4 %copy-start.7 = (bf16[448,512]{1,0:T(8,128)(2,1)}, bf16[448,512]{1,0:T(8,128)(2,1)S(1)}, u32[]{:S(2)}) copy-start(bf16[448,512]{1,0:T(8,128)(2,1)S(1)} %collective-permute-done.16.refs_8_) | copy-start | bytes 1376260
  32.6 15.8 %collective-permute-start.5 = (bf16[256,512]{1,0:T(8,128)(2,1)S(1)}, bf16[256,512]{1,0:T(8,128)(2,1)}, u32[]{:S(2)}, u32[]{:S(2)}) collective-permute-start(bf16[256,512]{1,0:T(8,128)(2,1)S(1)} %collective-permute-done.1.refs_6_), channel_id=1, source_target_pairs={{0,2},{1,3},{4,0},{5,1},{8,4},{9,5},{12,8},{13,9},{14,12},{15,13},... | collective-permute-start | bytes 786440 | tf_op jit(solution)/shard_map/ppermute | solution.py:33
  34.4 0.7 copy-start.21
  34.4 16.4 %collective-permute-start.22 = (bf16[448,512]{1,0:T(8,128)(2,1)S(1)}, bf16[448,512]{1,0:T(8,128)(2,1)S(1)}, u32[]{:S(2)}, u32[]{:S(2)}) collective-permute-start(bf16[448,512]{1,0:T(8,128)(2,1)S(1)} %collective-permute-done.15.refs_4_), channel_id=1, source_target_pairs={{0,4},{1,5},{4,8},{5,9},{8,12},{9,13},{12,14},{13,15},{14,10},{15,... | collective-permute-start | bytes 1376264 | tf_op jit(solution)/shard_map/ppermute | solution.py:33
  35.1 7.8 %copy-start.10 = (bf16[448,512]{1,0:T(8,128)(2,1)}, bf16[448,512]{1,0:T(8,128)(2,1)S(1)}, u32[]{:S(2)}) copy-start(bf16[448,512]{1,0:T(8,128)(2,1)S(1)} %collective-permute-done.11.refs_9_) | copy-start | bytes 1376260
  35.1 15.9 %collective-permute-start.23 = (bf16[448,512]{1,0:T(8,128)(2,1)S(1)}, bf16[448,512]{1,0:T(8,128)(2,1)S(1)}, u32[]{:S(2)}, u32[]{:S(2)}) collective-permute-start(bf16[448,512]{1,0:T(8,128)(2,1)S(1)} %collective-permute-done.16.refs_8_), channel_id=1, source_target_pairs={{0,2},{1,3},{4,0},{5,1},{8,4},{9,5},{12,8},{13,9},{14,12},{15,13},... | collective-permute-start | bytes 1376264 | tf_op jit(solution)/shard_map/ppermute | solution.py:33
  48.4 1.8 %collective-permute-start.14 = (bf16[256,512]{1,0:T(8,128)(2,1)}, bf16[256,512]{1,0:T(8,128)(2,1)S(1)}, u32[]{:S(2)}, u32[]{:S(2)}) collective-permute-start(bf16[256,512]{1,0:T(8,128)(2,1)} %collective-permute-done.4.refs_2_), channel_id=1, source_target_pairs={{0,1},{1,0},{2,3},{3,2},{4,5},{5,4},{6,7},{7,6},{8,9},{9,8},{10,11... | collective-permute-start | bytes 786440 | tf_op jit(solution)/shard_map/ppermute | solution.py:33
  48.5 6.0 %collective-permute-start.17 = (bf16[448,512]{1,0:T(8,128)(2,1)S(1)}, bf16[448,512]{1,0:T(8,128)(2,1)S(1)}, u32[]{:S(2)}, u32[]{:S(2)}) collective-permute-start(bf16[448,512]{1,0:T(8,128)(2,1)S(1)} %collective-permute-done.15.refs_4_), channel_id=1, source_target_pairs={{0,1},{1,0},{2,3},{3,2},{4,5},{5,4},{6,7},{7,6},{8,9},{9,8},{10,11... | collective-permute-start | bytes 1376264 | tf_op jit(solution)/shard_map/ppermute | solution.py:33
  49.0 5.5 %collective-permute-start.19 = (bf16[448,512]{1,0:T(8,128)(2,1)S(1)}, bf16[448,512]{1,0:T(8,128)(2,1)S(1)}, u32[]{:S(2)}, u32[]{:S(2)}) collective-permute-start(bf16[448,512]{1,0:T(8,128)(2,1)S(1)} %collective-permute-done.16.refs_8_), channel_id=1, source_target_pairs={{0,1},{1,0},{2,3},{3,2},{4,5},{5,4},{6,7},{7,6},{8,9},{9,8},{10,11... | collective-permute-start | bytes 1376264 | tf_op jit(solution)/shard_map/ppermute | solution.py:33
  50.2 0.8 copy-start.19
  50.3 2.6 %collective-permute-start.18 = (bf16[256,512]{1,0:T(8,128)(2,1)}, bf16[256,512]{1,0:T(8,128)(2,1)}, u32[]{:S(2)}, u32[]{:S(2)}) collective-permute-start(bf16[256,512]{1,0:T(8,128)(2,1)} %collective-permute-done.5.refs_6_), channel_id=1, source_target_pairs={{0,1},{1,0},{2,3},{3,2},{4,5},{5,4},{6,7},{7,6},{8,9},{9,8},{10,11... | collective-permute-start | bytes 786440 | tf_op jit(solution)/shard_map/ppermute | solution.py:33
  50.8 13.4 %copy-start.5 = (bf16[448,512]{1,0:T(8,128)(2,1)}, bf16[448,512]{1,0:T(8,128)(2,1)S(1)}, u32[]{:S(2)}) copy-start(bf16[448,512]{1,0:T(8,128)(2,1)S(1)} %collective-permute-done.22.refs_4_) | copy-start | bytes 1376260
  50.8 10.9 %collective-permute-start.12 = (bf16[256,512]{1,0:T(8,128)(2,1)}, bf16[256,512]{1,0:T(8,128)(2,1)S(1)}, u32[]{:S(2)}, u32[]{:S(2)}) collective-permute-start(bf16[256,512]{1,0:T(8,128)(2,1)} %collective-permute-done.4.refs_2_), channel_id=1, source_target_pairs={{0,4},{1,5},{4,8},{5,9},{8,12},{9,13},{12,14},{13,15},{14,10},{15,... | collective-permute-start | bytes 786440 | tf_op jit(solution)/shard_map/ppermute | solution.py:33
  51.1 16.4 %copy-start.4 = (bf16[448,512]{1,0:T(8,128)(2,1)}, bf16[448,512]{1,0:T(8,128)(2,1)S(1)}, u32[]{:S(2)}) copy-start(bf16[448,512]{1,0:T(8,128)(2,1)S(1)} %collective-permute-done.23.refs_8_) | copy-start | bytes 1376260
  51.1 10.6 %collective-permute-start.13 = (bf16[256,512]{1,0:T(8,128)(2,1)}, bf16[256,512]{1,0:T(8,128)(2,1)}, u32[]{:S(2)}, u32[]{:S(2)}) collective-permute-start(bf16[256,512]{1,0:T(8,128)(2,1)} %collective-permute-done.5.refs_6_), channel_id=1, source_target_pairs={{0,2},{1,3},{4,0},{5,1},{8,4},{9,5},{12,8},{13,9},{14,12},{15,13},... | collective-permute-start | bytes 786440 | tf_op jit(solution)/shard_map/ppermute | solution.py:33
  52.9 15.1 %collective-permute-start.26 = (bf16[352,512]{1,0:T(8,128)(2,1)S(1)}, bf16[352,512]{1,0:T(8,128)(2,1)S(1)}, u32[]{:S(2)}, u32[]{:S(2)}) collective-permute-start(bf16[352,512]{1,0:T(8,128)(2,1)S(1)} %slice.7), channel_id=1, source_target_pairs={{0,2},{1,3},{4,0},{5,1},{8,4},{9,5},{12,8},{13,9},{14,12},{15,13},... | collective-permute-start | bytes 1081352 | tf_op jit(solution)/shard_map/ppermute | solution.py:33
  54.6 0.8 copy-start.11
  55.3 0.8 copy-start.12
  61.7 13.3 %copy-start.14 = (bf16[256,512]{1,0:T(8,128)(2,1)}, bf16[256,512]{1,0:T(8,128)(2,1)S(1)}, u32[]{:S(2)}) copy-start(bf16[256,512]{1,0:T(8,128)(2,1)S(1)} %collective-permute-done.12.refs_2_) | copy-start | bytes 786436
  61.7 5.8 %collective-permute-start.28 = (bf16[256,512]{1,0:T(8,128)(2,1)S(1)}, bf16[256,512]{1,0:T(8,128)(2,1)S(1)}, u32[]{:S(2)}, u32[]{:S(2)}) collective-permute-start(bf16[256,512]{1,0:T(8,128)(2,1)S(1)} %collective-permute-done.12.refs_2_), channel_id=1, source_target_pairs={{0,1},{1,0},{2,3},{3,2},{4,5},{5,4},{6,7},{7,6},{8,9},{9,8},{10,11... | collective-permute-start | bytes 786440 | tf_op jit(solution)/shard_map/ppermute | solution.py:33
  61.8 13.9 %copy-start.23 = (f32[1,8,384]{2,1,0:T(8,128)S(1)}, f32[1,8,384]{2,1,0:T(8,128)}, u32[]{:S(2)}) copy-start(f32[1,8,384]{2,1,0:T(8,128)} %shard_map.74) | copy-start | bytes 36868
  61.8 13.9 %copy-start.24 = (f32[1,8,384]{2,1,0:T(8,128)S(1)}, f32[1,8,384]{2,1,0:T(8,128)}, u32[]{:S(2)}) copy-start(f32[1,8,384]{2,1,0:T(8,128)} %shard_map.76) | copy-start | bytes 36868
  61.8 5.6 %collective-permute-start.24 = (bf16[96,512]{1,0:T(8,128)(2,1)S(1)}, bf16[96,512]{1,0:T(8,128)(2,1)S(1)}, u32[]{:S(2)}, u32[]{:S(2)}) collective-permute-start(bf16[96,512]{1,0:T(8,128)(2,1)S(1)} %slice.6), channel_id=1, source_target_pairs={{0,4},{1,5},{4,8},{5,9},{8,12},{9,13},{12,14},{13,15},{14,10},{15,... | collective-permute-start | bytes 294920 | tf_op jit(solution)/shard_map/ppermute | solution.py:33
  62.6 10.1 %collective-permute-start.20 = (bf16[256,512]{1,0:T(8,128)(2,1)S(1)}, bf16[256,512]{1,0:T(8,128)(2,1)S(1)}, u32[]{:S(2)}, u32[]{:S(2)}) collective-permute-start(bf16[256,512]{1,0:T(8,128)(2,1)S(1)} %collective-permute-done.12.refs_2_), channel_id=1, source_target_pairs={{0,4},{1,5},{4,8},{5,9},{8,12},{9,13},{12,14},{13,15},{14,10},{15,... | collective-permute-start | bytes 786440 | tf_op jit(solution)/shard_map/ppermute | solution.py:33
  64.2 11.6 %collective-permute-start.29 = (bf16[448,512]{1,0:T(8,128)(2,1)S(1)}, bf16[448,512]{1,0:T(8,128)(2,1)}, u32[]{:S(2)}, u32[]{:S(2)}) collective-permute-start(bf16[448,512]{1,0:T(8,128)(2,1)S(1)} %collective-permute-done.22.refs_4_), channel_id=1, source_target_pairs={{0,1},{1,0},{2,3},{3,2},{4,5},{5,4},{6,7},{7,6},{8,9},{9,8},{10,11... | collective-permute-start | bytes 1376264 | tf_op jit(solution)/shard_map/ppermute | solution.py:33
  67.5 8.3 %collective-permute-start.31 = (bf16[448,512]{1,0:T(8,128)(2,1)S(1)}, bf16[448,512]{1,0:T(8,128)(2,1)}, u32[]{:S(2)}, u32[]{:S(2)}) collective-permute-start(bf16[448,512]{1,0:T(8,128)(2,1)S(1)} %collective-permute-done.23.refs_8_), channel_id=1, source_target_pairs={{0,1},{1,0},{2,3},{3,2},{4,5},{5,4},{6,7},{7,6},{8,9},{9,8},{10,11... | collective-permute-start | bytes 1376264 | tf_op jit(solution)/shard_map/ppermute | solution.py:33
  67.5 0.7 copy-start.17
  67.5 7.5 %collective-permute-start.30 = (bf16[256,512]{1,0:T(8,128)(2,1)}, bf16[256,512]{1,0:T(8,128)(2,1)S(1)}, u32[]{:S(2)}, u32[]{:S(2)}) collective-permute-start(bf16[256,512]{1,0:T(8,128)(2,1)} %collective-permute-done.13.refs_6_), channel_id=1, source_target_pairs={{0,1},{1,0},{2,3},{3,2},{4,5},{5,4},{6,7},{7,6},{8,9},{9,8},{10,11... | collective-permute-start | bytes 786440 | tf_op jit(solution)/shard_map/ppermute | solution.py:33
  68.0 13.4 %collective-permute-start.27 = (bf16[352,512]{1,0:T(8,128)(2,1)S(1)}, bf16[352,512]{1,0:T(8,128)(2,1)S(1)}, u32[]{:S(2)}, u32[]{:S(2)}) collective-permute-start(bf16[352,512]{1,0:T(8,128)(2,1)S(1)} %collective-permute-done.26.refs_4_), channel_id=1, source_target_pairs={{0,1},{1,0},{2,3},{3,2},{4,5},{5,4},{6,7},{7,6},{8,9},{9,8},{10,11... | collective-permute-start | bytes 1081352 | tf_op jit(solution)/shard_map/ppermute | solution.py:33
  72.7 8.7 %collective-permute-start.21 = (bf16[256,512]{1,0:T(8,128)(2,1)S(1)}, bf16[256,512]{1,0:T(8,128)(2,1)S(1)}, u32[]{:S(2)}, u32[]{:S(2)}) collective-permute-start(bf16[256,512]{1,0:T(8,128)(2,1)S(1)} %collective-permute-done.20.refs_0_), channel_id=1, source_target_pairs={{0,1},{1,0},{2,3},{3,2},{4,5},{5,4},{6,7},{7,6},{8,9},{9,8},{10,11... | collective-permute-start | bytes 786440 | tf_op jit(solution)/shard_map/ppermute | solution.py:33
  75.0 0.7 copy-start.20
  75.0 6.3 %collective-permute-start.25 = (bf16[96,512]{1,0:T(8,128)(2,1)S(1)}, bf16[96,512]{1,0:T(8,128)(2,1)S(1)}, u32[]{:S(2)}, u32[]{:S(2)}) collective-permute-start(bf16[96,512]{1,0:T(8,128)(2,1)S(1)} %collective-permute-done.24.refs_2_), channel_id=1, source_target_pairs={{0,1},{1,0},{2,3},{3,2},{4,5},{5,4},{6,7},{7,6},{8,9},{9,8},{10,11... | collective-permute-start | bytes 294920 | tf_op jit(solution)/shard_map/ppermute | solution.py:33
  75.7 5.7 %copy-start.1 = (bf16[512,896]{1,0:T(8,128)(2,1)S(1)}, bf16[512,896]{1,0:T(8,128)(2,1)}, u32[]{:S(2)}) copy-start(bf16[512,896]{1,0:T(8,128)(2,1)} %get-tuple-element.42.refs_7_) | copy-start | bytes 2752516
  75.8 5.7 %copy-start.2 = (bf16[512,512]{1,0:T(8,128)(2,1)S(1)}, bf16[512,512]{1,0:T(8,128)(2,1)}, u32[]{:S(2)}) copy-start(bf16[512,512]{1,0:T(8,128)(2,1)} %get-tuple-element.41.refs_6_) | copy-start | bytes 1572868
  75.8 5.7 %copy-start.3 = (s32[16,64]{1,0:T(8,128)S(1)}, s32[16,64]{1,0:T(8,128)}, u32[]{:S(2)}) copy-start(s32[16,64]{1,0:T(8,128)} %refs_10_.1) | copy-start | bytes 12292
  81.4 1.6 %copy-start = (f32[2,512,512]{2,1,0:T(8,128)S(1)}, f32[2,512,512]{2,1,0:T(8,128)}, u32[]{:S(2)}) copy-start(f32[2,512,512]{2,1,0:T(8,128)} %shard_map.79.refs_8_) | copy-start | bytes 6291460
  86.0 1.4 %collective-permute-start.32 = (f32[32,16]{1,0:T(8,128)S(1)}, f32[32,16]{1,0:T(8,128)S(1)}, u32[]{:S(2)}, u32[]{:S(2)}) collective-permute-start(f32[32,16]{1,0:T(8,128)S(1)} %shard_map.80), channel_id=1, source_target_pairs={{0,1},{1,0},{2,3},{3,2},{4,5},{5,4},{6,7},{7,6},{8,9},{9,8},{10,11... | collective-permute-start | bytes 6152 | tf_op jit(solution)/shard_map/ppermute | solution.py:33
  87.4 3.7 %collective-permute-start.33 = (f32[32,16]{1,0:T(8,128)S(1)}, f32[32,16]{1,0:T(8,128)S(1)}, u32[]{:S(2)}, u32[]{:S(2)}) collective-permute-start(f32[32,16]{1,0:T(8,128)S(1)} %add.15), channel_id=1, source_target_pairs={{0,2},{1,3},{2,0},{3,1},{4,6},{5,7},{6,4},{7,5},{8,10},{9,11},{10,... | collective-permute-start | bytes 6152 | tf_op jit(solution)/shard_map/ppermute | solution.py:33
  91.1 3.7 %collective-permute-start.34 = (f32[32,16]{1,0:T(8,128)S(1)}, f32[32,16]{1,0:T(8,128)S(1)}, u32[]{:S(2)}, u32[]{:S(2)}) collective-permute-start(f32[32,16]{1,0:T(8,128)S(1)} %add.16), channel_id=1, source_target_pairs={{0,4},{1,5},{2,6},{3,7},{4,0},{5,1},{6,2},{7,3},{8,12},{9,13},{10,... | collective-permute-start | bytes 6152 | tf_op jit(solution)/shard_map/ppermute | solution.py:33
  94.9 4.6 %collective-permute-start.35 = (f32[32,16]{1,0:T(8,128)S(1)}, f32[32,16]{1,0:T(8,128)S(1)}, u32[]{:S(2)}, u32[]{:S(2)}) collective-permute-start(f32[32,16]{1,0:T(8,128)S(1)} %add.17), channel_id=1, source_target_pairs={{0,8},{1,9},{2,10},{3,11},{4,12},{5,13},{6,14},{7,15},{8,0},{9,1},... | collective-permute-start | bytes 6152 | tf_op jit(solution)/shard_map/ppermute | solution.py:33

commit v2 on v0

v2 whole, which is shorter than its diff:
```python
import functools
import math

import jax
import jax.numpy as jnp
from jax import lax
from jax.experimental import pallas as pl
from jax.experimental.pallas import tpu as pltpu
from jax.sharding import PartitionSpec as P

AXIS = "dp"
MIB = 1 << 20
ROWS = 256


def ring_order(chips):
    return list(range(0, chips, 2)) + list(range(chips - 1, 0, -2))


def xor_pairs(devices, mask):
    return [(i, i ^ mask) for i in range(devices)]


def ring_pairs(order, shift):
    chips = len(order)
    return [
        (order[k] * 2 + core, order[(k + shift) % chips] * 2 + core)
        for k in range(chips)
        for core in range(2)
    ]


def send(x, pairs):
    return lax.ppermute(x, AXIS, pairs)


def in_order(*values):
    return lax.optimization_barrier(values)


def device_index():
    return lax.axis_index(AXIS)


def chip_on_ring(chips, chip, shift):
    place = jnp.where(chip % 2 == 0, chip // 2, chips - 1 - chip // 2)
    place = (place + shift + chips) % chips
    return jnp.where(place < chips // 2, 2 * place, 2 * (chips - 1 - place) + 1)


SMEM = pl.BlockSpec(memory_space=pltpu.SMEM)
VMEM = pl.BlockSpec(memory_space=pltpu.VMEM)
ANY = pl.BlockSpec(memory_space=pl.ANY)
FLOAT = jnp.float32


def params(limit=60):
    return pltpu.CompilerParams(vmem_limit_bytes=limit * MIB)


def small_cost():
    return pl.CostEstimate(flops=1, bytes_accessed=1, transcendentals=0)


def dot(a, b):
    return jnp.dot(a, b, preferred_element_type=FLOAT)


def dot_rows(a, b, precision=None):
    return lax.dot_general(
        a, b, (((1,), (1,)), ((), ())), precision=precision, preferred_element_type=FLOAT
    )


def exact_dot(a, b):
    return jnp.dot(a, b, precision=lax.Precision.HIGHEST, preferred_element_type=FLOAT)


def split_kernel(left, right, mine, other):
    core = device_index() % 2
    low = left.shape[0]
    half = mine.shape[1]

    def put(target, first):
        target[0:low, :] = left[:, first : first + half]
        target[low:, :] = right[:, first : first + half]

    @pl.when(core == 0)
    def _():
        put(mine, 0)
        put(other, half)

    @pl.when(core != 0)
    def _():
        put(mine, half)
        put(other, 0)


def split_columns(left, right):
    rows, half = left.shape[0] + right.shape[0], left.shape[1] // 2
    return pl.pallas_call(
        split_kernel,
        in_specs=[VMEM, VMEM],
        out_specs=[VMEM, VMEM],
        out_shape=[jax.ShapeDtypeStruct((rows, half), left.dtype)] * 2,
        compiler_params=params(8),
        cost_estimate=small_cost(),
    )(left, right)


def merge_kernel(low, mine, came, piece):
    core = device_index() % 2
    high = mine.shape[0] - low

    def put(first, second):
        piece[0:low, :] = first[0:low, :]
        piece[low : 2 * low, :] = second[0:low, :]
        piece[2 * low : 2 * low + high, :] = first[low:, :]
        piece[2 * low + high :, :] = second[low:, :]

    @pl.when(core == 0)
    def _():
        put(mine, came)

    @pl.when(core != 0)
    def _():
        put(came, mine)


def merge_rows(low, mine, came):
    rows, half = mine.shape
    return pl.pallas_call(
        functools.partial(merge_kernel, low),
        in_specs=[VMEM, VMEM],
        out_specs=VMEM,
        out_shape=jax.ShapeDtypeStruct((2 * rows, half), mine.dtype),
        compiler_params=params(8),
        cost_estimate=small_cost(),
    )(mine, came)


def block_of(chips, shift, features, rows=slice(None)):
    width = features.shape[1] // chips
    there = chip_on_ring(chips, device_index() // 2, shift)
    return features[rows, pl.ds(pl.multiple_of(there * width, 128), width)]


def project_kernel(shifts, chips, fresh, *refs):
    features, refs = refs[:2], refs[2:]
    pieces, refs = refs[: len(shifts)], refs[len(shifts) :]
    before, sums = (None, refs[0]) if fresh else refs
    split = features[0].shape[1] // chips

    @pl.loop(0, features[0].shape[0] // ROWS)
    def _(i):
        rows = pl.ds(pl.multiple_of(i * ROWS, ROWS), ROWS)
        for j, part in enumerate((slice(0, split), slice(split, None))):
            terms = [] if fresh else [before[j, rows, :]]
            for shift, piece in zip(shifts, pieces):
                terms.append(dot(block_of(chips, shift, features[j], rows), piece[part, :]))
            sums[j, rows, :] = sum(terms)


def project(chips, shifts, features, pieces, sums):
    tokens, columns = features[0].shape[0], pieces[0].shape[1]
    before = [] if sums is None else [sums]
    return pl.pallas_call(
        functools.partial(project_kernel, shifts, chips, not before),
        in_specs=[VMEM] * (2 + len(pieces) + len(before)),
        out_specs=VMEM,
        out_shape=jax.ShapeDtypeStruct((2, tokens, columns), FLOAT),
        input_output_aliases={2 + len(pieces): 0} if before else {},
        compiler_params=params(8),
        cost_estimate=small_cost(),
    )(*features, *pieces, *before)


def finish_kernel(
    shift, chips, rank, seq_index, seq_index_other, grads, acts, grads_other, acts_other,
    upper, lower, sums, sums_other, norms, dense, per_column,
):
    columns = upper.shape[1]
    queries = dense.shape[1] - 1
    sequences = seq_index.shape[0]
    length = grads.shape[0] // sequences
    middle, split = upper.shape[0], grads.shape[1] // chips
    core = device_index() % 2
    column = lax.broadcasted_iota(jnp.int32, (columns, queries + 1), 0)
    query = lax.broadcasted_iota(jnp.int32, (columns, queries + 1), 1)
    member = (column // rank + core * (columns // rank) == query).astype(FLOAT)
    for side, (left, right, total) in enumerate(
        ((grads, acts, sums), (grads_other, acts_other, sums_other))
    ):
        lefts, rights = block_of(chips, shift, left), block_of(chips, shift, right)
        rest = middle - split
        product = (total[0] + dot(lefts, upper[0:split, :])) * (
            total[1]
            + dot(rights[:, 0:rest], upper[split:, :])
            + dot(rights[:, rest:], lower[...])
        )
        for s in range(sequences):
            n = side * sequences + s
            per_column[n : n + 1, :] = jnp.sum(
                product[s * length : (s + 1) * length, :], axis=0, keepdims=True
            )
    raw = exact_dot(per_column[...], member)
    slot = lax.broadcasted_iota(jnp.int32, dense.shape, 0)
    lane = lax.broadcasted_iota(jnp.int32, (1, queries + 1), 1)
    placed = jnp.zeros(dense.shape, FLOAT)
    for side, places in enumerate((seq_index, seq_index_other)):
        for s in range(sequences):
            n = side * sequences + s
            row = raw[n : n + 1, :]
            if side == 0:
                row = row + jnp.where(lane == queries, norms[s, 0:1, 0:1], 0.0)
            placed = placed + jnp.where(slot == places[s], row, 0.0)
    dense[...] = placed


def finish(chips, shift, places, features, pieces, sums, norms, slots, queries, rank):
    columns = pieces[0].shape[1]
    return pl.pallas_call(
        functools.partial(finish_kernel, shift, chips, rank),
        in_specs=[SMEM] * 2 + [VMEM] * 9,
        out_specs=VMEM,
        out_shape=jax.ShapeDtypeStruct((slots, queries + 1), FLOAT),
        scratch_shapes=[pltpu.VMEM((2 * places[0].shape[0], columns), FLOAT)],
        compiler_params=params(12),
        cost_estimate=small_cost(),
    )(*places, *features, *pieces, *sums, norms)


def norms_kernel(sequences, grads, acts, norms):
    length = grads.shape[0] // sequences
    for s in range(sequences):
        rows = slice(s * length, (s + 1) * length)
        value = dot_rows(grads[rows, :], grads[rows, :]) * dot_rows(acts[rows, :], acts[rows, :])
        norms[s] = jnp.broadcast_to(jnp.sum(value, keepdims=True), norms.shape[1:])


def squared_norms_of(sequences, grads, acts):
    return pl.pallas_call(
        functools.partial(norms_kernel, sequences),
        in_specs=[VMEM, VMEM],
        out_specs=VMEM,
        out_shape=jax.ShapeDtypeStruct((sequences, 8, 128), FLOAT),
        compiler_params=params(8),
        cost_estimate=small_cost(),
    )(grads, acts)


def squared_norms(live, grads, acts):
    def covariance(x):
        return jnp.einsum("hcp,hqp->hcq", x, x, preferred_element_type=jnp.float32)

    return jnp.sum(
        live[:, :, None] * live[:, None, :] * covariance(grads) * covariance(acts), axis=(1, 2)
    )


def to_owners(dense, seq_count, mask=1):
    devices = lax.axis_size(AXIS)
    if devices & (devices - 1):
        return lax.psum_scatter(dense, AXIS, scatter_dimension=0, tiled=True)
    while mask < devices:
        masks = [mask] if mask < 4 or 2 * mask >= devices else [3 * mask, 2 * mask, mask]
        dense = sum([send(dense, xor_pairs(devices, m)) for m in masks], dense)
        mask *= len(masks) + 1
    return lax.dynamic_slice_in_dim(dense, lax.axis_index(AXIS) * seq_count, seq_count, axis=0)


def by_gathers(
    training_output_gradients, training_activations, train_ids, seq_index,
    left_factor, input_side_factor, query_ids,
):
    seq_count, length, width = training_output_gradients.shape
    hidden = training_activations.shape[2]
    columns = left_factor.shape[1]
    queries = query_ids.shape[0]
    rank = columns // queries
    grads = training_output_gradients.reshape(seq_count * length, width)
    acts = training_activations.reshape(seq_count * length, hidden)
    proj_out = dot(grads, lax.all_gather(left_factor, AXIS, axis=0, tiled=True))
    proj_in = dot(acts, lax.all_gather(input_side_factor, AXIS, axis=0, tiled=True))
    live = (train_ids != 0).astype(jnp.float32)
    product = (proj_out * proj_in).reshape(seq_count, length, columns) * live[:, :, None]
    raw = jnp.sum(jnp.sum(product, axis=1).reshape(seq_count, queries, rank), axis=2)
    grad_sq = squared_norms(live, training_output_gradients, training_activations)
    count = jnp.sum((query_ids != 0).astype(jnp.float32), axis=1)
    factor = query_ids.shape[1] * math.sqrt(width * hidden / rank)
    score = raw * factor / (count[None, :] * jnp.sqrt(grad_sq + 1e-06)[:, None])
    slots = jnp.arange(seq_count * lax.axis_size(AXIS), dtype=jnp.int32)
    dense = jnp.sum(
        jnp.where(seq_index[:, None, None] == slots[None, :, None], score[:, None, :], 0.0), axis=0
    )
    return to_owners(dense, seq_count)


def by_ring(
    training_output_gradients, training_activations, train_ids, seq_index,
    left_factor, input_side_factor, query_ids,
):
    seq_count, length, width = training_output_gradients.shape
    hidden = training_activations.shape[2]
    columns = left_factor.shape[1]
    queries = query_ids.shape[0]
    rank = columns // queries
    devices = lax.axis_size(AXIS)
    chips = devices // 2
    hops = chips // 2
    swap = xor_pairs(devices, 1)
    order = ring_order(chips)
    forward, backward = ring_pairs(order, 1), ring_pairs(order, -1)
    grads = training_output_gradients.reshape(seq_count * length, width)
    acts = training_activations.reshape(seq_count * length, hidden)
    low = left_factor.shape[0]

    mine, other = split_columns(left_factor, input_side_factor)
    came = send(other, swap)
    piece = merge_rows(low, mine, came)
    moving = [send(piece, forward), send(piece, backward)]
    grads_sent, _ = in_order(grads, came)
    acts = jnp.where((train_ids != 0).reshape(-1, 1), acts, jnp.zeros_like(acts))
    features = [grads, acts]
    features_other = [send(grads_sent, swap)]
    places = [seq_index, send(seq_index, swap)]
    norms = squared_norms_of(seq_count, grads, acts)
    shifts, pieces = [0], [piece]
    sums = sums_other = None
    middle = piece.shape[0] // 2
    for hop in range(1, hops):
        *new, norms, acts_sent, places, sums = in_order(*moving, norms, acts, places, sums)
        if hop + 1 < hops:
            moving = [send(new[0], forward), send(new[1], backward)]
        else:
            moving = [send(new[0][:middle], forward), send(new[1][middle:], backward)]
        shifts, pieces = shifts + [-hop, hop], pieces + new
        if hop == 1:
            features_other.append(send(acts_sent, swap))
            sums = project(chips, shifts, features, pieces, None)
        else:
            sums = project(chips, [-hop, hop], features, new, sums)
    sums_other = project(chips, shifts, features_other, pieces, None)
    *last, sums, sums_other = in_order(*moving, sums, sums_other)
    dense = finish(
        chips, hops, places, [*features, *features_other], last, [sums, sums_other], norms,
        seq_count * devices, queries, rank,
    )
    dense = dense + send(dense, swap)
    count = jnp.sum((query_ids != 0).astype(jnp.float32), axis=1)
    factor = query_ids.shape[1] * math.sqrt(width * hidden / rank)
    score = dense[:, :queries] * (factor / count)[None, :] / jnp.sqrt(dense[:, queries:] + 1e-06)
    return to_owners(score, seq_count, 2)


def on_device(*args):
    left_rows, right_rows = args[4].shape[0], args[5].shape[0]
    devices = lax.axis_size(AXIS)
    fits = (
        devices % 4 == 0
        and left_rows % 64 == 0
        and right_rows % 64 == 0
        and args[4].shape[1] % 256 == 0
        and args[6].shape[0] % 2 == 0
        and args[0].shape[1] % 128 == 0
        and (2 * left_rows) % 128 == 0
        and (2 * right_rows) % 128 == 0
    )
    return by_ring(*args) if fits else by_gathers(*args)


def solution(mesh):
    in_specs = (
        P(("groups", "dp"), None, None),
        P(("groups", "dp"), None, None),
        P(("groups", "dp"), None),
        P(("groups", "dp")),
        P("dp", "groups"),
        P("dp", "groups"),
        P("groups", None),
    )
    out_specs = P(("groups", "dp"), None)
    return jax.shard_map(
        on_device, mesh=mesh, in_specs=in_specs, out_specs=out_specs, check_vma=False
    )
```

time: 208 us -> 86.8 us (0.42)
  waiting for transfers between devices: 109 us -> 48.6 us
  blocking collectives: 59.2 us -> 0 us
  matrix products: 22.4 us -> 0 us
  starting transfers between devices: 0.04 us -> 15.4 us
  Pallas kernels: 0 us -> 14.9 us
  between operations: 14.1 us -> 0.17 us
  other arithmetic: 1.93 us -> 5.35 us
    all_gather x2 -> x0, waiting for transfers between devices: 107 us -> none  [the longest x1 63.3 us: on_device(): lax.all_gather(input_side_factor, 'dp', axis=0, tiled=True)]
    unnamed x1 -> x0, blocking collectives: 59.2 us -> none
    ppermute x0 -> x17, waiting for transfers between devices: none -> 48.6 us  [send(): return lax.ppermute(x, AXIS, pairs)]
    dot_general x5 -> x0, matrix products: 22.4 us -> none  [the longest x2 14.9 us: folder(): return jnp.dot(features, piece, preferred_element_type=jnp.float32)]
    ppermute x0 -> x17, starting transfers between devices: none -> 15.4 us  [send(): return lax.ppermute(x, AXIS, pairs)]
    pallas_call x0 -> x8, Pallas kernels: none -> 14.9 us  [the longest x4 9.6 us: project(): pl.pallas_call(functools.partial(project_kernel, shifts, chips, not befor...]
    select_n x0 -> x1, other arithmetic: none -> 3.63 us  [by_ring(): jnp.where((train_ids != 0).reshape(-1, 1), acts, jnp.zeros_like(acts))]
  transfers between devices with their start and end apart: 2 -> 17, of which waited for: 2 -> 12; matrix products, arithmetic and copies ran while one was open for 8% -> 5% of each run, Pallas kernels for 0% -> 15%
where the time goes in v2:
time: 86.8 us; the launch traced here: 86.4 us
  waiting for transfers between devices  48.6 us (56%)
  starting transfers between devices  15.4 us (18%)
  Pallas kernels  14.9 us (17%)
  other arithmetic  5.35 us (6%)
  local copies, waits for them, and re-layouts  2.05 us (2%)
    ppermute x17, waiting for transfers between devices, send(): return lax.ppermute(x, AXIS, pairs)  48.6 us
    ppermute x17, starting transfers between devices, send(): return lax.ppermute(x, AXIS, pairs)  15.4 us
    pallas_call x4, Pallas kernels, project(): pl.pallas_call(functools.partial(project_kernel, shifts, chips, not befor...  9.6 us
    select_n x1, other arithmetic, by_ring(): jnp.where((train_ids != 0).reshape(-1, 1), acts, jnp.zeros_like(acts))  3.63 us
    pallas_call x1, Pallas kernels, squared_norms_of(): pl.pallas_call(functools.partial(norms_kernel, sequences), in_specs=[VMEM...  3.3 us
    unnamed x10, local copies, waits for them, and re-layouts  1.99 us
    pallas_call x1, Pallas kernels, finish(): pl.pallas_call(functools.partial(finish_kernel, shift, chips, rank), in_s...  1.88 us
  transfers between devices with their start and end apart: 17, of which 12 were waited for; matrix products, arithmetic and copies ran while one was open for 5% of the time, Pallas kernels for 15%

profile of v2, /device:TPU:0, one launch (start us, length us, event | category | flops | bytes accessed | tf_op | source)
XLA Modules:
  0.0 86.4 jit_solution(5474148063910038529)
XLA Ops:
  0.0 0.0 copy-start.1
  0.0 1.0 %copy-done.1 = bf16[448,512]{1,0:T(8,128)(2,1)S(1)} copy-done((bf16[448,512]{1,0:T(8,128)(2,1)S(1)}, bf16[448,512]{1,0:T(8,128)(2,1)}, u32[]{:S(2)}) %copy-start.1) | copy-done | bytes 458776
  1.0 0.0 copy-start.2
  1.0 0.9 %copy-done.2 = bf16[256,512]{1,0:T(8,128)(2,1)S(1)} copy-done((bf16[256,512]{1,0:T(8,128)(2,1)S(1)}, bf16[256,512]{1,0:T(8,128)(2,1)}, u32[]{:S(2)}) %copy-start.2) | copy-done | bytes 262168
  2.0 0.5 collective-permute-start
  2.5 0.1 collective-permute-start.3
  2.6 0.7 broadcast_compare_fusion
  3.3 0.5 collective-permute-done.came
  3.9 0.0 copy-start
  3.9 3.0 %collective-permute-start.1 = (bf16[1408,256]{1,0:T(8,128)(2,1)S(1)}, bf16[1408,256]{1,0:T(8,128)(2,1)S(1)}, u32[]{:S(2)}, u32[]{:S(2)}) collective-permute-start(bf16[1408,256]{1,0:T(8,128)(2,1)S(1)} %shard_map.74.refs_2_), channel_id=1, source_target_pairs={{0,4},{1,5},{4,8},{5,9},{8,12},{9,13},{12,14},{13,15},{14,10},{15,... | collective-permute-start | bytes 2162696 | tf_op jit(solution)/shard_map/ppermute | solution.py:34
  6.9 0.0 collective-permute-start.2
  6.9 3.6 %bitcast_select_fusion.acts.refs_1_ = bf16[512,7168]{1,0:T(8,128)(2,1)S(1)} fusion(bf16[2,256,7168]{2,1,0:T(8,128)(2,1)} %param.8, pred[512]{0:T(512)(128)(4,1)S(1)} %broadcast_in_dim.14), kind=kLoop, calls=%fused_computation | loop fusion | flops 3670016 | bytes 14680576 | tf_op jit(solution)/shard_map/jit(_where)/select_n | solution.py:323
  10.6 0.0 copy-done
  10.6 3.3 %shard_map.75.norms = f32[2,8,128]{2,1,0:T(8,128)S(1)} custom-call(bf16[512,4096]{1,0:T(8,128)(2,1)S(1)} %bitcast.3, bf16[512,7168]{1,0:T(8,128)(2,1)S(1)} %bitcast_select_fusion.acts.refs_1_), custom_call_target="tpu_custom_call" | custom-call | flops 1 | bytes 1 | tf_op jit(solution)/shard_map/pallas_call | solution.py:242
  13.9 0.0 collective-permute-done.3.seq_index_other
  13.9 9.4 %collective-permute-done.1.refs_3_ = bf16[1408,256]{1,0:T(8,128)(2,1)S(1)} collective-permute-done((bf16[1408,256]{1,0:T(8,128)(2,1)S(1)}, bf16[1408,256]{1,0:T(8,128)(2,1)S(1)}, u32[]{:S(2)}, u32[]{:S(2)}) %collective-permute-start.1) | collective-permute-done | bytes 720928 | tf_op jit(solution)/shard_map/ppermute | solution.py:34
  23.3 1.7 %collective-permute-done.2.refs_4_ = bf16[1408,256]{1,0:T(8,128)(2,1)} collective-permute-done((bf16[1408,256]{1,0:T(8,128)(2,1)S(1)}, bf16[1408,256]{1,0:T(8,128)(2,1)}, u32[]{:S(2)}, u32[]{:S(2)}) %collective-permute-start.2) | collective-permute-done | bytes 720928 | tf_op jit(solution)/shard_map/ppermute | solution.py:34
  24.9 0.0 collective-permute-start.9
  24.9 0.5 collective-permute-start.8
  25.4 1.6 %collective-permute-start.4 = (bf16[1408,256]{1,0:T(8,128)(2,1)S(1)}, bf16[1408,256]{1,0:T(8,128)(2,1)S(1)}, u32[]{:S(2)}, u32[]{:S(2)}) collective-permute-start(bf16[1408,256]{1,0:T(8,128)(2,1)S(1)} %collective-permute-done.1.refs_3_), channel_id=1, source_target_pairs={{0,4},{1,5},{4,8},{5,9},{8,12},{9,13},{12,14},{13,15},{14,10},{15,... | collective-permute-start | bytes 2162696 | tf_op jit(solution)/shard_map/ppermute | solution.py:34
  27.0 0.4 collective-permute-start.5
  27.4 2.7 %shard_map.76.refs_4_ = f32[2,512,256]{2,1,0:T(8,128)S(1)} custom-call(bf16[512,4096]{1,0:T(8,128)(2,1)S(1)} %bitcast.5, bf16[512,7168]{1,0:T(8,128)(2,1)S(1)} %bitcast_select_fusion.acts.refs_1_, bf16[1408,256]{1,0:T(8,128)(2,1)S(1)} %shard_map.74.refs_2_, bf16[1408,256]{1,0:T(8,128)(2,1)S(1)} %collective-permute-done.1.refs_3_, ...), custom_call_target="tpu_custom_call" | custom-call | flops 1 | bytes 1 | tf_op jit(solution)/shard_map/pallas_call | solution.py:167
  30.2 0.0 copy-start.4
  30.2 13.3 %collective-permute-done.4.refs_2_.refs_5_ = bf16[1408,256]{1,0:T(8,128)(2,1)S(1)} collective-permute-done((bf16[1408,256]{1,0:T(8,128)(2,1)S(1)}, bf16[1408,256]{1,0:T(8,128)(2,1)S(1)}, u32[]{:S(2)}, u32[]{:S(2)}) %collective-permute-start.4) | collective-permute-done | bytes 720928 | tf_op jit(solution)/shard_map/ppermute | solution.py:34
  43.5 1.5 %collective-permute-done.5.refs_3_.refs_6_ = bf16[1408,256]{1,0:T(8,128)(2,1)S(1)} collective-permute-done((bf16[1408,256]{1,0:T(8,128)(2,1)}, bf16[1408,256]{1,0:T(8,128)(2,1)S(1)}, u32[]{:S(2)}, u32[]{:S(2)}) %collective-permute-start.5) | collective-permute-done | bytes 720928 | tf_op jit(solution)/shard_map/ppermute | solution.py:34
  45.0 1.6 %collective-permute-start.6 = (bf16[1408,256]{1,0:T(8,128)(2,1)S(1)}, bf16[1408,256]{1,0:T(8,128)(2,1)S(1)}, u32[]{:S(2)}, u32[]{:S(2)}) collective-permute-start(bf16[1408,256]{1,0:T(8,128)(2,1)S(1)} %collective-permute-done.4.refs_2_.refs_5_), channel_id=1, source_target_pairs={{0,4},{1,5},{4,8},{5,9},{8,12},{9,13},{12,14},{13,15},{14,10},{15,... | collective-permute-start | bytes 2162696 | tf_op jit(solution)/shard_map/ppermute | solution.py:34
  46.6 0.4 collective-permute-start.7
  47.0 1.2 %shard_map.77.refs_4_ = f32[2,512,256]{2,1,0:T(8,128)S(1)} custom-call(bf16[512,4096]{1,0:T(8,128)(2,1)S(1)} %bitcast.6, bf16[512,7168]{1,0:T(8,128)(2,1)S(1)} %bitcast_select_fusion.acts.refs_1_, bf16[1408,256]{1,0:T(8,128)(2,1)S(1)} %collective-permute-done.4.refs_2_.refs_5_, ...), custom_call_target="tpu_custom_call", output_to_operand_aliasing={{}: (4, {})} | custom-call | flops 1 | bytes 1 | tf_op jit(solution)/shard_map/pallas_call | solution.py:167
  48.2 13.6 %collective-permute-done.6.refs_2_.refs_7_ = bf16[1408,256]{1,0:T(8,128)(2,1)S(1)} collective-permute-done((bf16[1408,256]{1,0:T(8,128)(2,1)S(1)}, bf16[1408,256]{1,0:T(8,128)(2,1)S(1)}, u32[]{:S(2)}, u32[]{:S(2)}) %collective-permute-start.6) | collective-permute-done | bytes 720928 | tf_op jit(solution)/shard_map/ppermute | solution.py:34
  61.9 1.3 %collective-permute-done.7.refs_3_.refs_8_ = bf16[1408,256]{1,0:T(8,128)(2,1)S(1)} collective-permute-done((bf16[1408,256]{1,0:T(8,128)(2,1)S(1)}, bf16[1408,256]{1,0:T(8,128)(2,1)S(1)}, u32[]{:S(2)}, u32[]{:S(2)}) %collective-permute-start.7) | collective-permute-done | bytes 720928 | tf_op jit(solution)/shard_map/ppermute | solution.py:34
  63.2 1.5 %collective-permute-start.10 = (bf16[704,256]{1,0:T(8,128)(2,1)S(1)}, bf16[704,256]{1,0:T(8,128)(2,1)S(1)}, u32[]{:S(2)}, u32[]{:S(2)}) collective-permute-start(bf16[704,256]{1,0:T(8,128)(2,1)S(1)} %slice.12), channel_id=1, source_target_pairs={{0,4},{1,5},{4,8},{5,9},{8,12},{9,13},{12,14},{13,15},{14,10},{15,... | collective-permute-start | bytes 1081352 | tf_op jit(solution)/shard_map/ppermute | solution.py:34
  64.7 0.6 collective-permute-start.11
  65.3 0.0 copy-done.4
  65.3 0.1 convert_reduce_fusion
  65.5 1.2 %shard_map.78.sums = f32[2,512,256]{2,1,0:T(8,128)S(1)} custom-call(bf16[512,4096]{1,0:T(8,128)(2,1)S(1)} %bitcast.7, bf16[512,7168]{1,0:T(8,128)(2,1)S(1)} %bitcast_select_fusion.acts.refs_1_, bf16[1408,256]{1,0:T(8,128)(2,1)S(1)} %collective-permute-done.6.refs_2_.refs_7_, ...), custom_call_target="tpu_custom_call", output_to_operand_aliasing={{}: (4, {})} | custom-call | flops 1 | bytes 1 | tf_op jit(solution)/shard_map/pallas_call | solution.py:167
  66.7 0.0 copy-start.3
  66.7 0.0 collective-permute-done.8.refs_0_.grads_other
  66.7 0.0 collective-permute-done.9.refs_1_.acts_other
  66.7 4.5 %shard_map.79.sums_other = f32[2,512,256]{2,1,0:T(8,128)S(1)} custom-call(bf16[512,4096]{1,0:T(8,128)(2,1)S(1)} %collective-permute-done.8.refs_0_.grads_other, bf16[512,7168]{1,0:T(8,128)(2,1)S(1)} %collective-permute-done.9.refs_1_.acts_other, bf16[1408,256]{1,0:T(8,128)(2,1)S(1)} %shard_map.74.refs_2_, ...), custom_call_target="tpu_custom_call" | custom-call | flops 1 | bytes 1 | tf_op jit(solution)/shard_map/pallas_call | solution.py:167
  71.1 0.0 collective-permute-done.10.upper
  71.2 1.3 %collective-permute-done.11.lower = bf16[704,256]{1,0:T(8,128)(2,1)S(1)} collective-permute-done((bf16[704,256]{1,0:T(8,128)(2,1)S(1)}, bf16[704,256]{1,0:T(8,128)(2,1)S(1)}, u32[]{:S(2)}, u32[]{:S(2)}) %collective-permute-start.11) | collective-permute-done | bytes 360480 | tf_op jit(solution)/shard_map/ppermute | solution.py:34
  72.5 0.0 copy-done.3
  72.5 1.9 %shard_map.80 = f32[32,17]{1,0:T(8,128)S(1)} custom-call(s32[2]{0:T(128)S(1)} %copy-done.3, s32[2]{0:T(128)S(1)} %collective-permute-done.3.seq_index_other, bf16[512,4096]{1,0:T(8,128)(2,1)S(1)} %bitcast.8, bf16[512,7168]{1,0:T(8,128)(2,1)S(1)} %bitcast_select_fusion.acts.refs_1_, bf16[512,4096]{1,0:T(8,128)(2,1)S(1)} %collective-permute-done.8.refs_0_.grads_other, ...), custom_call_target="tpu_custom_call" | custom-call | flops 1 | bytes 1 | tf_op jit(solution)/shard_map/pallas_call | solution.py:222
  74.4 0.1 collective-permute-start.12
  74.4 1.2 %collective-permute-done.12 = f32[32,17]{1,0:T(8,128)S(1)} collective-permute-done((f32[32,17]{1,0:T(8,128)S(1)}, f32[32,17]{1,0:T(8,128)S(1)}, u32[]{:S(2)}, u32[]{:S(2)}) %collective-permute-start.12) | collective-permute-done | bytes 2208 | tf_op jit(solution)/shard_map/ppermute | solution.py:34
  75.6 0.2 fusion.1
  75.8 0.1 fusion.2
  75.9 0.6 collective-permute-start.13
  76.5 3.2 %collective-permute-done.13 = f32[32,16]{1,0:T(8,128)S(1)} collective-permute-done((f32[32,16]{1,0:T(8,128)S(1)}, f32[32,16]{1,0:T(8,128)S(1)}, u32[]{:S(2)}, u32[]{:S(2)}) %collective-permute-start.13) | collective-permute-done | bytes 2080 | tf_op jit(solution)/shard_map/ppermute | solution.py:34
  79.6 0.1 fusion.3
  79.7 0.4 collective-permute-start.14
  80.2 1.7 %collective-permute-start.15 = (f32[32,16]{1,0:T(8,128)S(1)}, f32[32,16]{1,0:T(8,128)S(1)}, u32[]{:S(2)}, u32[]{:S(2)}) collective-permute-start(f32[32,16]{1,0:T(8,128)S(1)} %fusion.3), channel_id=1, source_target_pairs={{0,8},{1,9},{2,10},{3,11},{4,12},{5,13},{6,14},{7,15},{8,0},{9,1},... | collective-permute-start | bytes 6152 | tf_op jit(solution)/shard_map/ppermute | solution.py:34
  81.8 2.3 %collective-permute-start.16 = (f32[32,16]{1,0:T(8,128)S(1)}, f32[32,16]{1,0:T(8,128)S(1)}, u32[]{:S(2)}, u32[]{:S(2)}) collective-permute-start(f32[32,16]{1,0:T(8,128)S(1)} %fusion.3), channel_id=1, source_target_pairs={{0,4},{1,5},{2,6},{3,7},{4,0},{5,1},{6,2},{7,3},{8,12},{9,13},{10,... | collective-permute-start | bytes 6152 | tf_op jit(solution)/shard_map/ppermute | solution.py:34
  84.2 1.1 %collective-permute-done.14 = f32[32,16]{1,0:T(8,128)S(1)} collective-permute-done((f32[32,16]{1,0:T(8,128)S(1)}, f32[32,16]{1,0:T(8,128)S(1)}, u32[]{:S(2)}, u32[]{:S(2)}) %collective-permute-start.14) | collective-permute-done | bytes 2080 | tf_op jit(solution)/shard_map/ppermute | solution.py:34
  85.3 0.0 collective-permute-done.15
  85.3 0.6 collective-permute-done.16
  85.9 0.6 dynamic-slice_add_fusion
  (7 shorter events, 0.2 us)
Async XLA Ops:
  0.0 1.0 %copy-start.1 = (bf16[448,512]{1,0:T(8,128)(2,1)S(1)}, bf16[448,512]{1,0:T(8,128)(2,1)}, u32[]{:S(2)}) copy-start(bf16[448,512]{1,0:T(8,128)(2,1)} %right.1) | copy-start | bytes 1376260
  1.0 0.9 %copy-start.2 = (bf16[256,512]{1,0:T(8,128)(2,1)S(1)}, bf16[256,512]{1,0:T(8,128)(2,1)}, u32[]{:S(2)}) copy-start(bf16[256,512]{1,0:T(8,128)(2,1)} %left.1) | copy-start | bytes 786436
  2.0 1.8 %collective-permute-start = (bf16[704,256]{1,0:T(8,128)(2,1)S(1)}, bf16[704,256]{1,0:T(8,128)(2,1)S(1)}, u32[]{:S(2)}, u32[]{:S(2)}) collective-permute-start(bf16[704,256]{1,0:T(8,128)(2,1)S(1)} %get-tuple-element.31), channel_id=1, source_target_pairs={{0,1},{1,0},{2,3},{3,2},{4,5},{5,4},{6,7},{7,6},{8,9},{9,8},{10,11... | collective-permute-start | bytes 1081352 | tf_op jit(solution)/shard_map/ppermute | solution.py:34
  2.5 11.3 %collective-permute-start.3 = (s32[2]{0:T(128)}, s32[2]{0:T(128)S(1)}, u32[]{:S(2)}, u32[]{:S(2)}) collective-permute-start(s32[2]{0:T(128)} %seq_index), channel_id=1, source_target_pairs={{0,1},{1,0},{2,3},{3,2},{4,5},{5,4},{6,7},{7,6},{8,9},{9,8},{10,11... | collective-permute-start | bytes 32 | tf_op jit(solution)/shard_map/ppermute | solution.py:34
  3.9 6.7 %copy-start = (bf16[2,256,4096]{2,1,0:T(8,128)(2,1)S(1)}, bf16[2,256,4096]{2,1,0:T(8,128)(2,1)}, u32[]{:S(2)}) copy-start(bf16[2,256,4096]{2,1,0:T(8,128)(2,1)} %param.7) | copy-start | bytes 12582916
  3.9 19.4 %collective-permute-start.1 = (bf16[1408,256]{1,0:T(8,128)(2,1)S(1)}, bf16[1408,256]{1,0:T(8,128)(2,1)S(1)}, u32[]{:S(2)}, u32[]{:S(2)}) collective-permute-start(bf16[1408,256]{1,0:T(8,128)(2,1)S(1)} %shard_map.74.refs_2_), channel_id=1, source_target_pairs={{0,4},{1,5},{4,8},{5,9},{8,12},{9,13},{12,14},{13,15},{14,10},{15,... | collective-permute-start | bytes 2162696 | tf_op jit(solution)/shard_map/ppermute | solution.py:34
  6.9 18.0 %collective-permute-start.2 = (bf16[1408,256]{1,0:T(8,128)(2,1)S(1)}, bf16[1408,256]{1,0:T(8,128)(2,1)}, u32[]{:S(2)}, u32[]{:S(2)}) collective-permute-start(bf16[1408,256]{1,0:T(8,128)(2,1)S(1)} %shard_map.74.refs_2_), channel_id=1, source_target_pairs={{0,2},{1,3},{4,0},{5,1},{8,4},{9,5},{12,8},{13,9},{14,12},{15,13},... | collective-permute-start | bytes 2162696 | tf_op jit(solution)/shard_map/ppermute | solution.py:34
  24.9 41.8 %collective-permute-start.9 = (bf16[512,7168]{1,0:T(8,128)(2,1)S(1)}, bf16[512,7168]{1,0:T(8,128)(2,1)S(1)}, u32[]{:S(2)}, u32[]{:S(2)}) collective-permute-start(bf16[512,7168]{1,0:T(8,128)(2,1)S(1)} %bitcast_select_fusion.acts.refs_1_), channel_id=1, source_target_pairs={{0,1},{1,0},{2,3},{3,2},{4,5},{5,4},{6,7},{7,6},{8,9},{9,8},{10,11... | collective-permute-start | bytes 22020104 | tf_op jit(solution)/shard_map/ppermute | solution.py:34
  24.9 41.8 %collective-permute-start.8 = (bf16[512,4096]{1,0:T(8,128)(2,1)S(1)}, bf16[512,4096]{1,0:T(8,128)(2,1)S(1)}, u32[]{:S(2)}, u32[]{:S(2)}) collective-permute-start(bf16[512,4096]{1,0:T(8,128)(2,1)S(1)} %bitcast.4), channel_id=1, source_target_pairs={{0,1},{1,0},{2,3},{3,2},{4,5},{5,4},{6,7},{7,6},{8,9},{9,8},{10,11... | collective-permute-start | bytes 12582920 | tf_op jit(solution)/shard_map/ppermute | solution.py:34
  25.4 18.0 %collective-permute-start.4 = (bf16[1408,256]{1,0:T(8,128)(2,1)S(1)}, bf16[1408,256]{1,0:T(8,128)(2,1)S(1)}, u32[]{:S(2)}, u32[]{:S(2)}) collective-permute-start(bf16[1408,256]{1,0:T(8,128)(2,1)S(1)} %collective-permute-done.1.refs_3_), channel_id=1, source_target_pairs={{0,4},{1,5},{4,8},{5,9},{8,12},{9,13},{12,14},{13,15},{14,10},{15,... | collective-permute-start | bytes 2162696 | tf_op jit(solution)/shard_map/ppermute | solution.py:34
  27.0 18.0 %collective-permute-start.5 = (bf16[1408,256]{1,0:T(8,128)(2,1)}, bf16[1408,256]{1,0:T(8,128)(2,1)S(1)}, u32[]{:S(2)}, u32[]{:S(2)}) collective-permute-start(bf16[1408,256]{1,0:T(8,128)(2,1)} %collective-permute-done.2.refs_4_), channel_id=1, source_target_pairs={{0,2},{1,3},{4,0},{5,1},{8,4},{9,5},{12,8},{13,9},{14,12},{15,13},... | collective-permute-start | bytes 2162696 | tf_op jit(solution)/shard_map/ppermute | solution.py:34
  30.2 35.1 %copy-start.4 = (s32[16,64]{1,0:T(8,128)S(1)}, s32[16,64]{1,0:T(8,128)}, u32[]{:S(2)}) copy-start(s32[16,64]{1,0:T(8,128)} %param.13) | copy-start | bytes 12292
  45.0 16.9 %collective-permute-start.6 = (bf16[1408,256]{1,0:T(8,128)(2,1)S(1)}, bf16[1408,256]{1,0:T(8,128)(2,1)S(1)}, u32[]{:S(2)}, u32[]{:S(2)}) collective-permute-start(bf16[1408,256]{1,0:T(8,128)(2,1)S(1)} %collective-permute-done.4.refs_2_.refs_5_), channel_id=1, source_target_pairs={{0,4},{1,5},{4,8},{5,9},{8,12},{9,13},{12,14},{13,15},{14,10},{15,... | collective-permute-start | bytes 2162696 | tf_op jit(solution)/shard_map/ppermute | solution.py:34
  46.6 16.6 %collective-permute-start.7 = (bf16[1408,256]{1,0:T(8,128)(2,1)S(1)}, bf16[1408,256]{1,0:T(8,128)(2,1)S(1)}, u32[]{:S(2)}, u32[]{:S(2)}) collective-permute-start(bf16[1408,256]{1,0:T(8,128)(2,1)S(1)} %collective-permute-done.5.refs_3_.refs_6_), channel_id=1, source_target_pairs={{0,2},{1,3},{4,0},{5,1},{8,4},{9,5},{12,8},{13,9},{14,12},{15,13},... | collective-permute-start | bytes 2162696 | tf_op jit(solution)/shard_map/ppermute | solution.py:34
  63.2 8.0 %collective-permute-start.10 = (bf16[704,256]{1,0:T(8,128)(2,1)S(1)}, bf16[704,256]{1,0:T(8,128)(2,1)S(1)}, u32[]{:S(2)}, u32[]{:S(2)}) collective-permute-start(bf16[704,256]{1,0:T(8,128)(2,1)S(1)} %slice.12), channel_id=1, source_target_pairs={{0,4},{1,5},{4,8},{5,9},{8,12},{9,13},{12,14},{13,15},{14,10},{15,... | collective-permute-start | bytes 1081352 | tf_op jit(solution)/shard_map/ppermute | solution.py:34
  64.7 7.7 %collective-permute-start.11 = (bf16[704,256]{1,0:T(8,128)(2,1)S(1)}, bf16[704,256]{1,0:T(8,128)(2,1)S(1)}, u32[]{:S(2)}, u32[]{:S(2)}) collective-permute-start(bf16[704,256]{1,0:T(8,128)(2,1)S(1)} %slice.13), channel_id=1, source_target_pairs={{0,2},{1,3},{4,0},{5,1},{8,4},{9,5},{12,8},{13,9},{14,12},{15,13},... | collective-permute-start | bytes 1081352 | tf_op jit(solution)/shard_map/ppermute | solution.py:34
  66.7 5.8 %copy-start.3 = (s32[2]{0:T(128)S(1)}, s32[2]{0:T(128)}, u32[]{:S(2)}) copy-start(s32[2]{0:T(128)} %seq_index) | copy-start | bytes 28
  74.4 1.2 %collective-permute-start.12 = (f32[32,17]{1,0:T(8,128)S(1)}, f32[32,17]{1,0:T(8,128)S(1)}, u32[]{:S(2)}, u32[]{:S(2)}) collective-permute-start(f32[32,17]{1,0:T(8,128)S(1)} %shard_map.80), channel_id=1, source_target_pairs={{0,1},{1,0},{2,3},{3,2},{4,5},{5,4},{6,7},{7,6},{8,9},{9,8},{10,11... | collective-permute-start | bytes 6536 | tf_op jit(solution)/shard_map/ppermute | solution.py:34
  75.9 3.8 %collective-permute-start.13 = (f32[32,16]{1,0:T(8,128)S(1)}, f32[32,16]{1,0:T(8,128)S(1)}, u32[]{:S(2)}, u32[]{:S(2)}) collective-permute-start(f32[32,16]{1,0:T(8,128)S(1)} %fusion.2), channel_id=1, source_target_pairs={{0,2},{1,3},{2,0},{3,1},{4,6},{5,7},{6,4},{7,5},{8,10},{9,11},{10,... | collective-permute-start | bytes 6152 | tf_op jit(solution)/shard_map/ppermute | solution.py:34
  79.7 5.6 %collective-permute-start.14 = (f32[32,16]{1,0:T(8,128)S(1)}, f32[32,16]{1,0:T(8,128)S(1)}, u32[]{:S(2)}, u32[]{:S(2)}) collective-permute-start(f32[32,16]{1,0:T(8,128)S(1)} %fusion.3), channel_id=1, source_target_pairs={{0,12},{1,13},{2,14},{3,15},{4,8},{5,9},{6,10},{7,11},{8,4},{9,5},... | collective-permute-start | bytes 6152 | tf_op jit(solution)/shard_map/ppermute | solution.py:34
  80.2 5.2 %collective-permute-start.15 = (f32[32,16]{1,0:T(8,128)S(1)}, f32[32,16]{1,0:T(8,128)S(1)}, u32[]{:S(2)}, u32[]{:S(2)}) collective-permute-start(f32[32,16]{1,0:T(8,128)S(1)} %fusion.3), channel_id=1, source_target_pairs={{0,8},{1,9},{2,10},{3,11},{4,12},{5,13},{6,14},{7,15},{8,0},{9,1},... | collective-permute-start | bytes 6152 | tf_op jit(solution)/shard_map/ppermute | solution.py:34
  81.8 4.1 %collective-permute-start.16 = (f32[32,16]{1,0:T(8,128)S(1)}, f32[32,16]{1,0:T(8,128)S(1)}, u32[]{:S(2)}, u32[]{:S(2)}) collective-permute-start(f32[32,16]{1,0:T(8,128)S(1)} %fusion.3), channel_id=1, source_target_pairs={{0,4},{1,5},{2,6},{3,7},{4,0},{5,1},{6,2},{7,3},{8,12},{9,13},{10,... | collective-permute-start | bytes 6152 | tf_op jit(solution)/shard_map/ppermute | solution.py:34

commit v3 on v2

--- a/solution.py
+++ b/solution.py
@@ -108,15 +108,20 @@
     )(left, right)
 
 
-def merge_kernel(low, mine, came, piece):
+def merge_kernel(low, mine, came, upper, lower):
     core = device_index() % 2
+    middle, total = upper.shape[0], upper.shape[0] + lower.shape[0]
     high = mine.shape[0] - low
 
     def put(first, second):
-        piece[0:low, :] = first[0:low, :]
-        piece[low : 2 * low, :] = second[0:low, :]
-        piece[2 * low : 2 * low + high, :] = first[low:, :]
-        piece[2 * low + high :, :] = second[low:, :]
+        parts = ((first, 0, low), (second, 0, low), (first, low, high), (second, low, high))
+        at = 0
+        for source, begin, count in parts:
+            for target, start, stop in ((upper, 0, middle), (lower, middle, total)):
+                lo, hi = max(at, start), min(at + count, stop)
+                if lo < hi:
+                    target[lo - start : hi - start, :] = source[begin + lo - at : begin + hi - at, :]
+            at += count
 
     @pl.when(core == 0)
     def _():
@@ -128,12 +133,11 @@
 
 
 def merge_rows(low, mine, came):
-    rows, half = mine.shape
     return pl.pallas_call(
         functools.partial(merge_kernel, low),
         in_specs=[VMEM, VMEM],
-        out_specs=VMEM,
-        out_shape=jax.ShapeDtypeStruct((2 * rows, half), mine.dtype),
+        out_specs=[VMEM, VMEM],
+        out_shape=[jax.ShapeDtypeStruct(mine.shape, mine.dtype)] * 2,
         compiler_params=params(8),
         cost_estimate=small_cost(),
     )(mine, came)
@@ -145,58 +149,108 @@
     return features[rows, pl.ds(pl.multiple_of(there * width, 128), width)]
 
 
-def project_kernel(shifts, chips, fresh, *refs):
-    features, refs = refs[:2], refs[2:]
-    pieces, refs = refs[: len(shifts)], refs[len(shifts) :]
-    before, sums = (None, refs[0]) if fresh else refs
-    split = features[0].shape[1] // chips
-
-    @pl.loop(0, features[0].shape[0] // ROWS)
+LEFT, RIGHT = 0, 1
+
+
+class Job:
+    def __init__(self, side, features, shifts, pieces, before=None):
+        self.side, self.features, self.shifts, self.before = side, features, shifts, before
+        self.pieces = pieces if side == RIGHT else pieces[::2]
+
+    def operands(self):
+        return [self.features, *self.pieces, *([] if self.before is None else [self.before])]
+
+
+def project_kernel(jobs, split, chips, keep, *refs):
+    rights = sum(len(job.shifts) for job in jobs if job.side == RIGHT)
+    stacks, refs = (refs[-1], refs[:-1]) if rights else (None, refs)
+    count = sum(len(job.operands()) for job in jobs)
+    refs, outs = list(refs[:count]), list(refs[count:])
+    work, used = [], 0
+    for job in jobs:
+        taken = [refs.pop(0) for _ in job.operands()]
+        features, before = taken[0], None if job.before is None else taken.pop()
+        factors = taken[1:]
+        if job.side == RIGHT:
+            for k in range(len(job.shifts)):
+                upper, lower = factors[2 * k : 2 * k + 2]
+                rest = upper.shape[0] - split
+                stacks[used + k, 0:rest, :] = upper[split:, :]
+                stacks[used + k, rest:, :] = lower[...]
+            factors = [stacks.at[used + k] for k in range(len(job.shifts))]
+            used += len(job.shifts)
+        else:
+            factors = [upper.at[0:split, :] for upper in factors]
+        work.append((job, features, factors, before, outs.pop(0)))
+
+    @pl.loop(0, work[0][1].shape[0] // ROWS)
     def _(i):
         rows = pl.ds(pl.multiple_of(i * ROWS, ROWS), ROWS)
-        for j, part in enumerate((slice(0, split), slice(split, None))):
-            terms = [] if fresh else [before[j, rows, :]]
-            for shift, piece in zip(shifts, pieces):
-                terms.append(dot(block_of(chips, shift, features[j], rows), piece[part, :]))
-            sums[j, rows, :] = sum(terms)
-
-
-def project(chips, shifts, features, pieces, sums):
-    tokens, columns = features[0].shape[0], pieces[0].shape[1]
-    before = [] if sums is None else [sums]
+        for job, features, factors, before, total in work:
+            terms = [] if before is None else [before[rows, :]]
+            for shift, factor in zip(job.shifts, factors):
+                terms.append(dot(block_of(chips, shift, features, rows), factor[...]))
+            total[rows, :] = sum(terms)
+        if keep:
+            outs[0][rows, :] = work[0][1][rows, :]
+
+
+def project(chips, split, jobs, keep=False):
+    first = jobs[0]
+    tokens, columns = first.features.shape[0], first.pieces[0].shape[1]
+    rights = [job for job in jobs if job.side == RIGHT]
+    shapes = [jax.ShapeDtypeStruct((tokens, columns), FLOAT) for _ in jobs]
+    if keep:
+        shapes.append(jax.ShapeDtypeStruct(first.features.shape, first.features.dtype))
+    aliases, place = {}, 0
+    for k, job in enumerate(jobs):
+        place += len(job.operands())
+        if job.before is not None:
+            aliases[place - 1] = k
+    scratch = []
+    if rights:
+        total = sum(len(job.shifts) for job in rights)
+        width = rights[0].features.shape[1] // chips
+        scratch = [pltpu.VMEM((total, width, columns), first.features.dtype)]
     return pl.pallas_call(
-        functools.partial(project_kernel, shifts, chips, not before),
-        in_specs=[VMEM] * (2 + len(pieces) + len(before)),
-        out_specs=VMEM,
-        out_shape=jax.ShapeDtypeStruct((2, tokens, columns), FLOAT),
-        input_output_aliases={2 + len(pieces): 0} if before else {},
-        compiler_params=params(8),
+        functools.partial(project_kernel, jobs, split, chips, keep),
+        in_specs=[VMEM] * place,
+        out_specs=[VMEM] * len(shapes),
+        out_shape=shapes,
+        scratch_shapes=scratch,
+        input_output_aliases=aliases,
+        compiler_params=params(14),
         cost_estimate=small_cost(),
-    )(*features, *pieces, *before)
+    )(*[x for job in jobs for x in job.operands()])
 
 
 def finish_kernel(
     shift, chips, rank, seq_index, seq_index_other, grads, acts, grads_other, acts_other,
-    upper, lower, sums, sums_other, norms, dense, per_column,
+    *refs,
 ):
-    columns = upper.shape[1]
+    pieces, refs = refs[:-8], refs[-8:]
+    sums, sums_other = refs[0:2], refs[2:4]
+    norms, dense, per_column, stack = refs[4:]
+    columns = stack.shape[1]
     queries = dense.shape[1] - 1
     sequences = seq_index.shape[0]
     length = grads.shape[0] // sequences
-    middle, split = upper.shape[0], grads.shape[1] // chips
+    split = grads.shape[1] // chips
     core = device_index() % 2
     column = lax.broadcasted_iota(jnp.int32, (columns, queries + 1), 0)
     query = lax.broadcasted_iota(jnp.int32, (columns, queries + 1), 1)
     member = (column // rank + core * (columns // rank) == query).astype(FLOAT)
-    for side, (left, right, total) in enumerate(
-        ((grads, acts, sums), (grads_other, acts_other, sums_other))
-    ):
-        lefts, rights = block_of(chips, shift, left), block_of(chips, shift, right)
-        rest = middle - split
-        product = (total[0] + dot(lefts, upper[0:split, :])) * (
-            total[1]
-            + dot(rights[:, 0:rest], upper[split:, :])
-            + dot(rights[:, rest:], lower[...])
+    first = 0
+    for piece in pieces:
+        stack[first : first + piece.shape[0], :] = piece[...]
+        first += piece.shape[0]
+    sides = (
+        (block_of(chips, shift, grads), block_of(chips, shift, acts), sums),
+        (block_of(chips, shift, grads_other), block_of(chips, shift, acts_other), sums_other),
+    )
+    for side, (lefts, rights, total) in enumerate(sides):
+        product = (total[0][...] + dot(lefts, stack[0:split, :])) * (
+            total[1][...] + dot(rights, stack[split:, :])
         )
         for s in range(sequences):
             n = side * sequences + s
@@ -221,10 +275,13 @@
     columns = pieces[0].shape[1]
     return pl.pallas_call(
         functools.partial(finish_kernel, shift, chips, rank),
-        in_specs=[SMEM] * 2 + [VMEM] * 9,
+        in_specs=[SMEM] * 2 + [VMEM] * (9 + len(pieces)),
         out_specs=VMEM,
         out_shape=jax.ShapeDtypeStruct((slots, queries + 1), FLOAT),
-        scratch_shapes=[pltpu.VMEM((2 * places[0].shape[0], columns), FLOAT)],
+        scratch_shapes=[
+            pltpu.VMEM((2 * places[0].shape[0], columns), FLOAT),
+            pltpu.VMEM((sum(p.shape[0] for p in pieces), columns), pieces[0].dtype),
+        ],
         compiler_params=params(12),
         cost_estimate=small_cost(),
     )(*places, *features, *pieces, *sums, norms)
@@ -317,33 +374,60 @@
 
     mine, other = split_columns(left_factor, input_side_factor)
     came = send(other, swap)
-    piece = merge_rows(low, mine, came)
-    moving = [send(piece, forward), send(piece, backward)]
+    pieces = list(merge_rows(low, mine, came))
+    moving = [[send(x, forward), send(x, backward)] for x in pieces]
     grads_sent, _ = in_order(grads, came)
     acts = jnp.where((train_ids != 0).reshape(-1, 1), acts, jnp.zeros_like(acts))
     features = [grads, acts]
-    features_other = [send(grads_sent, swap)]
+    grads_other = send(grads_sent, swap)
     places = [seq_index, send(seq_index, swap)]
     norms = squared_norms_of(seq_count, grads, acts)
-    shifts, pieces = [0], [piece]
-    sums = sums_other = None
-    middle = piece.shape[0] // 2
+    middle = pieces[0].shape[0] // 2
+    split = width // chips
+    shifts = [0]
+    own = [None, None]
+    other = [None, None]
     for hop in range(1, hops):
-        *new, norms, acts_sent, places, sums = in_order(*moving, norms, acts, places, sums)
-        if hop + 1 < hops:
-            moving = [send(new[0], forward), send(new[1], backward)]
+        if hop == 1:
+            moving, norms, places, acts_sent, grads_other = in_order(
+                moving, norms, places, acts, grads_other
+            )
+            acts_other = send(acts_sent, swap)
+            new = moving
         else:
-            moving = [send(new[0][:middle], forward), send(new[1][middle:], backward)]
-        shifts, pieces = shifts + [-hop, hop], pieces + new
+            upper, own, other[LEFT] = in_order(moving[0], own, other[LEFT])
+            lower = moving[1]
+            if hop + 1 == hops:
+                (other[RIGHT],) = project(
+                    chips, split, [Job(RIGHT, acts_other, shifts, pieces)]
+                )
+                *lower, other[RIGHT] = in_order(*lower, other[RIGHT])
+            new = [upper, lower]
+        arrived = [new[0][0], new[1][0], new[0][1], new[1][1]]
+        if hop + 1 == hops:
+            new = [[x[0][:middle], x[1][middle:]] for x in new]
+        moving = [[send(x[0], forward), send(x[1], backward)] for x in new]
+        step = [-hop, hop]
+        shifts, pieces = shifts + step, pieces + arrived
         if hop == 1:
-            features_other.append(send(acts_sent, swap))
-            sums = project(chips, shifts, features, pieces, None)
+            jobs = [Job(LEFT, grads_other, shifts, pieces)]
+            jobs += [Job(j, features[j], shifts, pieces) for j in (LEFT, RIGHT)]
+            other[LEFT], *own, grads_other = project(chips, split, jobs, True)
         else:
-            sums = project(chips, [-hop, hop], features, new, sums)
-    sums_other = project(chips, shifts, features_other, pieces, None)
-    *last, sums, sums_other = in_order(*moving, sums, sums_other)
+            jobs = [Job(LEFT, grads_other, step, arrived, other[LEFT])]
+            jobs += [Job(j, features[j], step, arrived, own[j]) for j in (LEFT, RIGHT)]
+            if hop + 1 == hops:
+                jobs.append(Job(RIGHT, acts_other, step, arrived, other[RIGHT]))
+            if hop + 1 < hops:
+                other[LEFT], *own = project(chips, split, jobs)
+            else:
+                own = project(chips, split, jobs[1:3])
+                other = project(chips, split, jobs[:1] + jobs[3:])
+    upper, lower = moving
+    upper, own, other = in_order(upper, own, other)
+    last = [*upper, *lower]
     dense = finish(
-        chips, hops, places, [*features, *features_other], last, [sums, sums_other], norms,
+        chips, hops, places, [*features, grads_other, acts_other], last, [*own, *other], norms,
         seq_count * devices, queries, rank,
     )
     dense = dense + send(dense, swap)

time: 86.8 us -> 84.3 us (0.971)
  waiting for transfers between devices: 48.6 us -> 34.6 us
  starting transfers between devices: 15.4 us -> 24.8 us
  Pallas kernels: 14.9 us -> 17.1 us
    ppermute x17 -> x25, waiting for transfers between devices: 48.6 us -> 34.6 us  [send(): return lax.ppermute(x, AXIS, pairs)]
    ppermute x17 -> x25, starting transfers between devices: 15.4 us -> 24.8 us  [send(): return lax.ppermute(x, AXIS, pairs)]
    pallas_call x4 -> x5, Pallas kernels: 9.6 us -> 11.9 us  [project(): pl.pallas_call(functools.partial(project_kernel, jobs, split, chips, keep...]
  transfers between devices with their start and end apart: 17 -> 25, of which waited for: 12 -> 17; matrix products, arithmetic and copies ran while one was open for 5% -> 5% of each run, Pallas kernels for 15% -> 18%
where the time goes in v3:
time: 84.3 us; the launch traced here: 84 us
  waiting for transfers between devices  34.6 us (41%)
  starting transfers between devices  24.8 us (29%)
  Pallas kernels  17.1 us (20%)
  other arithmetic  5.36 us (6%)
  local copies, waits for them, and re-layouts  2.05 us (2%)
    ppermute x25, waiting for transfers between devices, send(): return lax.ppermute(x, AXIS, pairs)  34.6 us
    ppermute x25, starting transfers between devices, send(): return lax.ppermute(x, AXIS, pairs)  24.8 us
    pallas_call x5, Pallas kernels, project(): pl.pallas_call(functools.partial(project_kernel, jobs, split, chips, keep...  11.9 us
    select_n x1, other arithmetic, by_ring(): jnp.where((train_ids != 0).reshape(-1, 1), acts, jnp.zeros_like(acts))  3.63 us
    pallas_call x1, Pallas kernels, squared_norms_of(): pl.pallas_call(functools.partial(norms_kernel, sequences), in_specs=[VMEM...  3.3 us
    unnamed x10, local copies, waits for them, and re-layouts  1.98 us
    pallas_call x1, Pallas kernels, finish(): pl.pallas_call(functools.partial(finish_kernel, shift, chips, rank), in_s...  1.8 us
  transfers between devices with their start and end apart: 25, of which 17 were waited for; matrix products, arithmetic and copies ran while one was open for 5% of the time, Pallas kernels for 18%

profile of v3, /device:TPU:0, one launch (start us, length us, event | category | flops | bytes accessed | tf_op | source)
XLA Modules:
  0.0 84.0 jit_solution(15092794622372788001)
XLA Ops:
  0.0 1.0 %copy-done.1 = bf16[448,512]{1,0:T(8,128)(2,1)S(1)} copy-done((bf16[448,512]{1,0:T(8,128)(2,1)S(1)}, bf16[448,512]{1,0:T(8,128)(2,1)}, u32[]{:S(2)}) %copy-start.1) | copy-done | bytes 458776
  1.0 0.9 %copy-done.2 = bf16[256,512]{1,0:T(8,128)(2,1)S(1)} copy-done((bf16[256,512]{1,0:T(8,128)(2,1)S(1)}, bf16[256,512]{1,0:T(8,128)(2,1)}, u32[]{:S(2)}) %copy-start.2) | copy-done | bytes 262168
  2.0 0.5 collective-permute-start
  2.5 1.3 %collective-permute-done.came = bf16[704,256]{1,0:T(8,128)(2,1)S(1)} collective-permute-done((bf16[704,256]{1,0:T(8,128)(2,1)S(1)}, bf16[704,256]{1,0:T(8,128)(2,1)S(1)}, u32[]{:S(2)}, u32[]{:S(2)}) %collective-permute-start) | collective-permute-done | bytes 360480 | tf_op jit(solution)/shard_map/ppermute | solution.py:34
  3.8 0.4 collective-permute-start.6
  4.2 0.1 collective-permute-start.5
  4.4 0.7 broadcast_compare_fusion
  5.1 0.1 shard_map.74
  5.1 3.0 %collective-permute-start.1 = (bf16[704,256]{1,0:T(8,128)(2,1)S(1)}, bf16[704,256]{1,0:T(8,128)(2,1)S(1)}, u32[]{:S(2)}, u32[]{:S(2)}) collective-permute-start(bf16[704,256]{1,0:T(8,128)(2,1)S(1)} %get-tuple-element.51.refs_1_.refs_5_.refs_9_), channel_id=1, source_target_pairs={{0,4},{1,5},{4,8},{5,9},{8,12},{9,13},{12,14},{13,15},{14,10},{15,... | collective-permute-start | bytes 1081352 | tf_op jit(solution)/shard_map/ppermute | solution.py:34
  8.1 2.0 %collective-permute-start.3 = (bf16[704,256]{1,0:T(8,128)(2,1)S(1)}, bf16[704,256]{1,0:T(8,128)(2,1)}, u32[]{:S(2)}, u32[]{:S(2)}) collective-permute-start(bf16[704,256]{1,0:T(8,128)(2,1)S(1)} %get-tuple-element.52.refs_10_.refs_2_), channel_id=1, source_target_pairs={{0,4},{1,5},{4,8},{5,9},{8,12},{9,13},{12,14},{13,15},{14,10},{15,... | collective-permute-start | bytes 1081352 | tf_op jit(solution)/shard_map/ppermute | solution.py:34
  10.2 0.0 collective-permute-done.5.seq_index_other
  10.2 1.3 %collective-permute-start.4 = (bf16[704,256]{1,0:T(8,128)(2,1)S(1)}, bf16[704,256]{1,0:T(8,128)(2,1)}, u32[]{:S(2)}, u32[]{:S(2)}) collective-permute-start(bf16[704,256]{1,0:T(8,128)(2,1)S(1)} %get-tuple-element.52.refs_10_.refs_2_), channel_id=1, source_target_pairs={{0,2},{1,3},{4,0},{5,1},{8,4},{9,5},{12,8},{13,9},{14,12},{15,13},... | collective-permute-start | bytes 1081352 | tf_op jit(solution)/shard_map/ppermute | solution.py:34
  11.5 3.6 %bitcast_select_fusion.acts.refs_8_.refs_4_ = bf16[512,7168]{1,0:T(8,128)(2,1)S(1)} fusion(bf16[2,256,7168]{2,1,0:T(8,128)(2,1)} %param.8, pred[512]{0:T(512)(128)(4,1)S(1)} %broadcast_in_dim.14), kind=kLoop, calls=%fused_computation | loop fusion | flops 3670016 | bytes 14680576 | tf_op jit(solution)/shard_map/jit(_where)/select_n | solution.py:380
  15.2 3.3 %shard_map.75.refs_8_ = f32[2,8,128]{2,1,0:T(8,128)S(1)} custom-call(bf16[512,4096]{1,0:T(8,128)(2,1)S(1)} %bitcast.4, bf16[512,7168]{1,0:T(8,128)(2,1)S(1)} %bitcast_select_fusion.acts.refs_8_.refs_4_), custom_call_target="tpu_custom_call" | custom-call | flops 1 | bytes 1 | tf_op jit(solution)/shard_map/pallas_call | solution.py:299
  18.5 0.0 collective-permute-done.1.refs_2_.refs_6_.refs_11_.refs_3_
  18.5 0.9 %collective-permute-done.2.refs_3_.refs_7_.refs_13_.refs_5_ = bf16[704,256]{1,0:T(8,128)(2,1)S(1)} collective-permute-done((bf16[704,256]{1,0:T(8,128)(2,1)S(1)}, bf16[704,256]{1,0:T(8,128)(2,1)S(1)}, u32[]{:S(2)}, u32[]{:S(2)}) %collective-permute-start.2) | collective-permute-done | bytes 360480 | tf_op jit(solution)/shard_map/ppermute | solution.py:34
  19.4 5.2 %collective-permute-done.3.refs_12_.refs_4_ = bf16[704,256]{1,0:T(8,128)(2,1)} collective-permute-done((bf16[704,256]{1,0:T(8,128)(2,1)S(1)}, bf16[704,256]{1,0:T(8,128)(2,1)}, u32[]{:S(2)}, u32[]{:S(2)}) %collective-permute-start.3) | collective-permute-done | bytes 360480 | tf_op jit(solution)/shard_map/ppermute | solution.py:34
  24.6 1.5 %collective-permute-done.4.refs_14_.refs_6_ = bf16[704,256]{1,0:T(8,128)(2,1)} collective-permute-done((bf16[704,256]{1,0:T(8,128)(2,1)S(1)}, bf16[704,256]{1,0:T(8,128)(2,1)}, u32[]{:S(2)}, u32[]{:S(2)}) %collective-permute-start.4) | collective-permute-done | bytes 360480 | tf_op jit(solution)/shard_map/ppermute | solution.py:34
  26.1 0.0 collective-permute-start.7
  26.1 1.6 %collective-permute-start.8 = (bf16[704,256]{1,0:T(8,128)(2,1)S(1)}, bf16[704,256]{1,0:T(8,128)(2,1)S(1)}, u32[]{:S(2)}, u32[]{:S(2)}) collective-permute-start(bf16[704,256]{1,0:T(8,128)(2,1)S(1)} %collective-permute-done.1.refs_2_.refs_6_.refs_11_.refs_3_), channel_id=1, source_target_pairs={{0,4},{1,5},{4,8},{5,9},{8,12},{9,13},{12,14},{13,15},{14,10},{15,... | collective-permute-start | bytes 1081352 | tf_op jit(solution)/shard_map/ppermute | solution.py:34
  27.7 0.4 collective-permute-start.9
  28.2 1.6 %collective-permute-start.12 = (bf16[704,256]{1,0:T(8,128)(2,1)}, bf16[704,256]{1,0:T(8,128)(2,1)S(1)}, u32[]{:S(2)}, u32[]{:S(2)}) collective-permute-start(bf16[704,256]{1,0:T(8,128)(2,1)} %collective-permute-done.3.refs_12_.refs_4_), channel_id=1, source_target_pairs={{0,4},{1,5},{4,8},{5,9},{8,12},{9,13},{12,14},{13,15},{14,10},{15,... | collective-permute-start | bytes 1081352 | tf_op jit(solution)/shard_map/ppermute | solution.py:34
  29.7 0.4 collective-permute-start.13
  30.2 4.8 %shard_map.76 = (f32[512,256]{1,0:T(8,128)S(1)}, f32[512,256]{1,0:T(8,128)S(1)}, f32[512,256]{1,0:T(8,128)S(1)}, bf16[512,4096]{1,0:T(8,128)(2,1)S(1)}) custom-call(bf16[512,4096]{1,0:T(8,128)(2,1)} %collective-permute-done.6.refs_0_, bf16[704,256]{1,0:T(8,128)(2,1)S(1)} %get-tuple-element.51.refs_1_.refs_5_.refs_9_, ...), custom_call_target="tpu_custom_call" | custom-call | flops 1 | bytes 1 | tf_op jit(solution)/shard_map/pallas_call | solution.py:215
  35.0 2.4 %collective-permute-done.8.refs_1_.refs_5_.refs_9_.refs_7_ = bf16[704,256]{1,0:T(8,128)(2,1)S(1)} collective-permute-done((bf16[704,256]{1,0:T(8,128)(2,1)S(1)}, bf16[704,256]{1,0:T(8,128)(2,1)S(1)}, u32[]{:S(2)}, u32[]{:S(2)}) %collective-permute-start.8) | collective-permute-done | bytes 360480 | tf_op jit(solution)/shard_map/ppermute | solution.py:34
  37.3 1.6 %collective-permute-done.9.refs_2_.refs_6_.refs_11_.refs_9_ = bf16[704,256]{1,0:T(8,128)(2,1)S(1)} collective-permute-done((bf16[704,256]{1,0:T(8,128)(2,1)S(1)}, bf16[704,256]{1,0:T(8,128)(2,1)S(1)}, u32[]{:S(2)}, u32[]{:S(2)}) %collective-permute-start.9) | collective-permute-done | bytes 360480 | tf_op jit(solution)/shard_map/ppermute | solution.py:34
  39.0 1.6 %collective-permute-start.10 = (bf16[704,256]{1,0:T(8,128)(2,1)S(1)}, bf16[704,256]{1,0:T(8,128)(2,1)S(1)}, u32[]{:S(2)}, u32[]{:S(2)}) collective-permute-start(bf16[704,256]{1,0:T(8,128)(2,1)S(1)} %collective-permute-done.8.refs_1_.refs_5_.refs_9_.refs_7_), channel_id=1, source_target_pairs={{0,4},{1,5},{4,8},{5,9},{8,12},{9,13},{12,14},{13,15},{14,10},{15,... | collective-permute-start | bytes 1081352 | tf_op jit(solution)/shard_map/ppermute | solution.py:34
  40.5 0.4 collective-permute-start.11
  41.0 4.1 %collective-permute-done.12.refs_10_.refs_8_ = bf16[704,256]{1,0:T(8,128)(2,1)S(1)} collective-permute-done((bf16[704,256]{1,0:T(8,128)(2,1)}, bf16[704,256]{1,0:T(8,128)(2,1)S(1)}, u32[]{:S(2)}, u32[]{:S(2)}) %collective-permute-start.12) | collective-permute-done | bytes 360480 | tf_op jit(solution)/shard_map/ppermute | solution.py:34
  45.1 1.6 %collective-permute-start.16 = (bf16[704,256]{1,0:T(8,128)(2,1)S(1)}, bf16[704,256]{1,0:T(8,128)(2,1)S(1)}, u32[]{:S(2)}, u32[]{:S(2)}) collective-permute-start(bf16[704,256]{1,0:T(8,128)(2,1)S(1)} %collective-permute-done.12.refs_10_.refs_8_), channel_id=1, source_target_pairs={{0,4},{1,5},{4,8},{5,9},{8,12},{9,13},{12,14},{13,15},{14,10},{15,... | collective-permute-start | bytes 1081352 | tf_op jit(solution)/shard_map/ppermute | solution.py:34
  46.6 0.0 collective-permute-done.13.refs_12_.refs_10_
  46.7 0.4 collective-permute-start.17
  47.1 1.6 %shard_map.77 = (f32[512,256]{1,0:T(8,128)S(1)}, f32[512,256]{1,0:T(8,128)S(1)}, f32[512,256]{1,0:T(8,128)S(1)}) custom-call(bf16[512,4096]{1,0:T(8,128)(2,1)S(1)} %get-tuple-element.61.refs_0_.grads_other, bf16[704,256]{1,0:T(8,128)(2,1)S(1)} %collective-permute-done.8.refs_1_.refs_5_.refs_9_.refs_7_, ...), custom_call_target="tpu_custom_call", output_to_operand_aliasing={{0}: (3, {}), {1}: (7, {}), {2}: (13, {})} | custom-call | flops 1 | bytes 1 | tf_op jit(solution)/shard_map/pallas_call | solution.py:215
  48.7 0.0 copy-start.4
  48.7 4.1 %collective-permute-done.10.refs_1_.refs_5_ = bf16[704,256]{1,0:T(8,128)(2,1)S(1)} collective-permute-done((bf16[704,256]{1,0:T(8,128)(2,1)S(1)}, bf16[704,256]{1,0:T(8,128)(2,1)S(1)}, u32[]{:S(2)}, u32[]{:S(2)}) %collective-permute-start.10) | collective-permute-done | bytes 360480 | tf_op jit(solution)/shard_map/ppermute | solution.py:34
  52.8 1.6 %collective-permute-done.11.refs_2_.refs_7_ = bf16[704,256]{1,0:T(8,128)(2,1)S(1)} collective-permute-done((bf16[704,256]{1,0:T(8,128)(2,1)S(1)}, bf16[704,256]{1,0:T(8,128)(2,1)S(1)}, u32[]{:S(2)}, u32[]{:S(2)}) %collective-permute-start.11) | collective-permute-done | bytes 360480 | tf_op jit(solution)/shard_map/ppermute | solution.py:34
  54.4 1.6 %collective-permute-start.14 = (bf16[352,256]{1,0:T(8,128)(2,1)S(1)}, bf16[352,256]{1,0:T(8,128)(2,1)S(1)}, u32[]{:S(2)}, u32[]{:S(2)}) collective-permute-start(bf16[352,256]{1,0:T(8,128)(2,1)S(1)} %slice.18), channel_id=1, source_target_pairs={{0,4},{1,5},{4,8},{5,9},{8,12},{9,13},{12,14},{13,15},{14,10},{15,... | collective-permute-start | bytes 540680 | tf_op jit(solution)/shard_map/ppermute | solution.py:34
  56.1 0.5 collective-permute-start.15
  56.6 0.0 collective-permute-done.7.refs_0_.refs_4_.acts_other
  56.6 3.0 %shard_map.78.refs_9_ = f32[512,256]{1,0:T(8,128)S(1)} custom-call(bf16[512,7168]{1,0:T(8,128)(2,1)S(1)} %collective-permute-done.7.refs_0_.refs_4_.acts_other, bf16[704,256]{1,0:T(8,128)(2,1)S(1)} %get-tuple-element.51.refs_1_.refs_5_.refs_9_, bf16[704,256]{1,0:T(8,128)(2,1)S(1)} %get-tuple-element.52.refs_10_.refs_2_, ...), custom_call_target="tpu_custom_call" | custom-call | flops 1 | bytes 1 | tf_op jit(solution)/shard_map/pallas_call | solution.py:215
  59.6 0.9 %collective-permute-done.16.refs_6_ = bf16[704,256]{1,0:T(8,128)(2,1)S(1)} collective-permute-done((bf16[704,256]{1,0:T(8,128)(2,1)S(1)}, bf16[704,256]{1,0:T(8,128)(2,1)S(1)}, u32[]{:S(2)}, u32[]{:S(2)}) %collective-permute-start.16) | collective-permute-done | bytes 360480 | tf_op jit(solution)/shard_map/ppermute | solution.py:34
  60.5 1.6 %collective-permute-done.17.refs_8_ = bf16[704,256]{1,0:T(8,128)(2,1)S(1)} collective-permute-done((bf16[704,256]{1,0:T(8,128)(2,1)S(1)}, bf16[704,256]{1,0:T(8,128)(2,1)S(1)}, u32[]{:S(2)}, u32[]{:S(2)}) %collective-permute-start.17) | collective-permute-done | bytes 360480 | tf_op jit(solution)/shard_map/ppermute | solution.py:34
  62.1 1.6 %collective-permute-start.18 = (bf16[352,256]{1,0:T(8,128)(2,1)S(1)}, bf16[352,256]{1,0:T(8,128)(2,1)S(1)}, u32[]{:S(2)}, u32[]{:S(2)}) collective-permute-start(bf16[352,256]{1,0:T(8,128)(2,1)S(1)} %slice.20), channel_id=1, source_target_pairs={{0,4},{1,5},{4,8},{5,9},{8,12},{9,13},{12,14},{13,15},{14,10},{15,... | collective-permute-start | bytes 540680 | tf_op jit(solution)/shard_map/ppermute | solution.py:34
  63.8 0.5 collective-permute-start.19
  64.3 0.1 convert_reduce_fusion
  64.4 1.3 %shard_map.79 = (f32[512,256]{1,0:T(8,128)S(1)}, f32[512,256]{1,0:T(8,128)S(1)}) custom-call(bf16[512,4096]{1,0:T(8,128)(2,1)S(1)} %bitcast.7, bf16[704,256]{1,0:T(8,128)(2,1)S(1)} %collective-permute-done.10.refs_1_.refs_5_, bf16[704,256]{1,0:T(8,128)(2,1)S(1)} %collective-permute-done.11.refs_2_.refs_7_, ...), custom_call_target="tpu_custom_call", output_to_operand_aliasing={{0}: (3, {}), {1}: (9, {})} | custom-call | flops 1 | bytes 1 | tf_op jit(solution)/shard_map/pallas_call | solution.py:215
  65.7 0.0 copy-start.3
  65.7 1.3 %shard_map.80 = (f32[512,256]{1,0:T(8,128)S(1)}, f32[512,256]{1,0:T(8,128)S(1)}) custom-call(bf16[512,4096]{1,0:T(8,128)(2,1)S(1)} %get-tuple-element.61.refs_0_.grads_other, bf16[704,256]{1,0:T(8,128)(2,1)S(1)} %collective-permute-done.10.refs_1_.refs_5_, ...), custom_call_target="tpu_custom_call", output_to_operand_aliasing={{0}: (3, {}), {1}: (9, {})} | custom-call | flops 1 | bytes 1 | tf_op jit(solution)/shard_map/pallas_call | solution.py:215
  67.0 0.9 %collective-permute-done.18.refs_2_ = bf16[352,256]{1,0:T(8,128)(2,1)S(1)} collective-permute-done((bf16[352,256]{1,0:T(8,128)(2,1)S(1)}, bf16[352,256]{1,0:T(8,128)(2,1)S(1)}, u32[]{:S(2)}, u32[]{:S(2)}) %collective-permute-start.18) | collective-permute-done | bytes 180256 | tf_op jit(solution)/shard_map/ppermute | solution.py:34
  67.9 1.5 %collective-permute-done.19.refs_3_ = bf16[352,256]{1,0:T(8,128)(2,1)S(1)} collective-permute-done((bf16[352,256]{1,0:T(8,128)(2,1)S(1)}, bf16[352,256]{1,0:T(8,128)(2,1)S(1)}, u32[]{:S(2)}, u32[]{:S(2)}) %collective-permute-start.19) | collective-permute-done | bytes 180256 | tf_op jit(solution)/shard_map/ppermute | solution.py:34
  69.3 1.8 %shard_map.81 = f32[32,17]{1,0:T(8,128)S(1)} custom-call(s32[2]{0:T(128)S(1)} %copy-done.3, s32[2]{0:T(128)S(1)} %collective-permute-done.5.seq_index_other, bf16[512,4096]{1,0:T(8,128)(2,1)S(1)} %bitcast.8, bf16[512,7168]{1,0:T(8,128)(2,1)S(1)} %bitcast_select_fusion.acts.refs_8_.refs_4_, bf16[512,4096]{1,0:T(8,128)(2,1)S(1)} %get-tuple-element.61.refs_0_.grads_other, ...), custom_call_target="tpu_custom_call" | custom-call | flops 1 | bytes 1 | tf_op jit(solution)/shard_map/pallas_call | solution.py:276
  71.2 0.1 collective-permute-start.20
  71.2 1.2 %collective-permute-done.20 = f32[32,17]{1,0:T(8,128)S(1)} collective-permute-done((f32[32,17]{1,0:T(8,128)S(1)}, f32[32,17]{1,0:T(8,128)S(1)}, u32[]{:S(2)}, u32[]{:S(2)}) %collective-permute-start.20) | collective-permute-done | bytes 2208 | tf_op jit(solution)/shard_map/ppermute | solution.py:34
  72.4 0.2 fusion.1
  72.6 0.1 fusion.2
  72.7 0.5 collective-permute-start.21
  73.2 3.3 %collective-permute-done.21 = f32[32,16]{1,0:T(8,128)S(1)} collective-permute-done((f32[32,16]{1,0:T(8,128)S(1)}, f32[32,16]{1,0:T(8,128)S(1)}, u32[]{:S(2)}, u32[]{:S(2)}) %collective-permute-start.21) | collective-permute-done | bytes 2080 | tf_op jit(solution)/shard_map/ppermute | solution.py:34
  76.4 0.1 fusion.3
  76.5 2.3 %collective-permute-start.22 = (f32[32,16]{1,0:T(8,128)S(1)}, f32[32,16]{1,0:T(8,128)S(1)}, u32[]{:S(2)}, u32[]{:S(2)}) collective-permute-start(f32[32,16]{1,0:T(8,128)S(1)} %fusion.3), channel_id=1, source_target_pairs={{0,12},{1,13},{2,14},{3,15},{4,8},{5,9},{6,10},{7,11},{8,4},{9,5},... | collective-permute-start | bytes 6152 | tf_op jit(solution)/shard_map/ppermute | solution.py:34
  78.8 0.8 collective-permute-start.23
  79.5 1.4 %collective-permute-start.24 = (f32[32,16]{1,0:T(8,128)S(1)}, f32[32,16]{1,0:T(8,128)S(1)}, u32[]{:S(2)}, u32[]{:S(2)}) collective-permute-start(f32[32,16]{1,0:T(8,128)S(1)} %fusion.3), channel_id=1, source_target_pairs={{0,4},{1,5},{2,6},{3,7},{4,0},{5,1},{6,2},{7,3},{8,12},{9,13},{10,... | collective-permute-start | bytes 6152 | tf_op jit(solution)/shard_map/ppermute | solution.py:34
  81.0 1.1 %collective-permute-done.22 = f32[32,16]{1,0:T(8,128)S(1)} collective-permute-done((f32[32,16]{1,0:T(8,128)S(1)}, f32[32,16]{1,0:T(8,128)S(1)}, u32[]{:S(2)}, u32[]{:S(2)}) %collective-permute-start.22) | collective-permute-done | bytes 2080 | tf_op jit(solution)/shard_map/ppermute | solution.py:34
  82.1 1.3 %collective-permute-done.23 = f32[32,16]{1,0:T(8,128)S(1)} collective-permute-done((f32[32,16]{1,0:T(8,128)S(1)}, f32[32,16]{1,0:T(8,128)S(1)}, u32[]{:S(2)}, u32[]{:S(2)}) %collective-permute-start.23) | collective-permute-done | bytes 2080 | tf_op jit(solution)/shard_map/ppermute | solution.py:34
  83.5 0.6 dynamic-slice_add_fusion
  (19 shorter events, 0.2 us)
Async XLA Ops:
  0.0 1.0 %copy-start.1 = (bf16[448,512]{1,0:T(8,128)(2,1)S(1)}, bf16[448,512]{1,0:T(8,128)(2,1)}, u32[]{:S(2)}) copy-start(bf16[448,512]{1,0:T(8,128)(2,1)} %right.1) | copy-start | bytes 1376260
  1.0 0.9 %copy-start.2 = (bf16[256,512]{1,0:T(8,128)(2,1)S(1)}, bf16[256,512]{1,0:T(8,128)(2,1)}, u32[]{:S(2)}) copy-start(bf16[256,512]{1,0:T(8,128)(2,1)} %left.1) | copy-start | bytes 786436
  2.0 1.8 %collective-permute-start = (bf16[704,256]{1,0:T(8,128)(2,1)S(1)}, bf16[704,256]{1,0:T(8,128)(2,1)S(1)}, u32[]{:S(2)}, u32[]{:S(2)}) collective-permute-start(bf16[704,256]{1,0:T(8,128)(2,1)S(1)} %get-tuple-element.50), channel_id=1, source_target_pairs={{0,1},{1,0},{2,3},{3,2},{4,5},{5,4},{6,7},{7,6},{8,9},{9,8},{10,11... | collective-permute-start | bytes 1081352 | tf_op jit(solution)/shard_map/ppermute | solution.py:34
  3.8 22.3 %collective-permute-start.6 = (bf16[512,4096]{1,0:T(8,128)(2,1)}, bf16[512,4096]{1,0:T(8,128)(2,1)}, u32[]{:S(2)}, u32[]{:S(2)}) collective-permute-start(bf16[512,4096]{1,0:T(8,128)(2,1)} %bitcast.3), channel_id=1, source_target_pairs={{0,1},{1,0},{2,3},{3,2},{4,5},{5,4},{6,7},{7,6},{8,9},{9,8},{10,11... | collective-permute-start | bytes 12582920 | tf_op jit(solution)/shard_map/ppermute | solution.py:34
  4.2 5.9 %collective-permute-start.5 = (s32[2]{0:T(128)}, s32[2]{0:T(128)S(1)}, u32[]{:S(2)}, u32[]{:S(2)}) collective-permute-start(s32[2]{0:T(128)} %seq_index), channel_id=1, source_target_pairs={{0,1},{1,0},{2,3},{3,2},{4,5},{5,4},{6,7},{7,6},{8,9},{9,8},{10,11... | collective-permute-start | bytes 32 | tf_op jit(solution)/shard_map/ppermute | solution.py:34
  5.1 13.3 %collective-permute-start.1 = (bf16[704,256]{1,0:T(8,128)(2,1)S(1)}, bf16[704,256]{1,0:T(8,128)(2,1)S(1)}, u32[]{:S(2)}, u32[]{:S(2)}) collective-permute-start(bf16[704,256]{1,0:T(8,128)(2,1)S(1)} %get-tuple-element.51.refs_1_.refs_5_.refs_9_), channel_id=1, source_target_pairs={{0,4},{1,5},{4,8},{5,9},{8,12},{9,13},{12,14},{13,15},{14,10},{15,... | collective-permute-start | bytes 1081352 | tf_op jit(solution)/shard_map/ppermute | solution.py:34
  8.1 11.3 %collective-permute-start.2 = (bf16[704,256]{1,0:T(8,128)(2,1)S(1)}, bf16[704,256]{1,0:T(8,128)(2,1)S(1)}, u32[]{:S(2)}, u32[]{:S(2)}) collective-permute-start(bf16[704,256]{1,0:T(8,128)(2,1)S(1)} %get-tuple-element.51.refs_1_.refs_5_.refs_9_), channel_id=1, source_target_pairs={{0,2},{1,3},{4,0},{5,1},{8,4},{9,5},{12,8},{13,9},{14,12},{15,13},... | collective-permute-start | bytes 1081352 | tf_op jit(solution)/shard_map/ppermute | solution.py:34
  8.1 7.0 %copy-start = (bf16[2,256,4096]{2,1,0:T(8,128)(2,1)S(1)}, bf16[2,256,4096]{2,1,0:T(8,128)(2,1)}, u32[]{:S(2)}) copy-start(bf16[2,256,4096]{2,1,0:T(8,128)(2,1)} %param.7) | copy-start | bytes 12582916
  8.1 16.5 %collective-permute-start.3 = (bf16[704,256]{1,0:T(8,128)(2,1)S(1)}, bf16[704,256]{1,0:T(8,128)(2,1)}, u32[]{:S(2)}, u32[]{:S(2)}) collective-permute-start(bf16[704,256]{1,0:T(8,128)(2,1)S(1)} %get-tuple-element.52.refs_10_.refs_2_), channel_id=1, source_target_pairs={{0,4},{1,5},{4,8},{5,9},{8,12},{9,13},{12,14},{13,15},{14,10},{15,... | collective-permute-start | bytes 1081352 | tf_op jit(solution)/shard_map/ppermute | solution.py:34
  10.2 16.0 %collective-permute-start.4 = (bf16[704,256]{1,0:T(8,128)(2,1)S(1)}, bf16[704,256]{1,0:T(8,128)(2,1)}, u32[]{:S(2)}, u32[]{:S(2)}) collective-permute-start(bf16[704,256]{1,0:T(8,128)(2,1)S(1)} %get-tuple-element.52.refs_10_.refs_2_), channel_id=1, source_target_pairs={{0,2},{1,3},{4,0},{5,1},{8,4},{9,5},{12,8},{13,9},{14,12},{15,13},... | collective-permute-start | bytes 1081352 | tf_op jit(solution)/shard_map/ppermute | solution.py:34
  26.1 30.4 %collective-permute-start.7 = (bf16[512,7168]{1,0:T(8,128)(2,1)S(1)}, bf16[512,7168]{1,0:T(8,128)(2,1)S(1)}, u32[]{:S(2)}, u32[]{:S(2)}) collective-permute-start(bf16[512,7168]{1,0:T(8,128)(2,1)S(1)} %bitcast_select_fusion.acts.refs_8_.refs_4_), channel_id=1, source_target_pairs={{0,1},{1,0},{2,3},{3,2},{4,5},{5,4},{6,7},{7,6},{8,9},{9,8},{10,11... | collective-permute-start | bytes 22020104 | tf_op jit(solution)/shard_map/ppermute | solution.py:34
  26.1 11.2 %collective-permute-start.8 = (bf16[704,256]{1,0:T(8,128)(2,1)S(1)}, bf16[704,256]{1,0:T(8,128)(2,1)S(1)}, u32[]{:S(2)}, u32[]{:S(2)}) collective-permute-start(bf16[704,256]{1,0:T(8,128)(2,1)S(1)} %collective-permute-done.1.refs_2_.refs_6_.refs_11_.refs_3_), channel_id=1, source_target_pairs={{0,4},{1,5},{4,8},{5,9},{8,12},{9,13},{12,14},{13,15},{14,10},{15,... | collective-permute-start | bytes 1081352 | tf_op jit(solution)/shard_map/ppermute | solution.py:34
  27.7 11.2 %collective-permute-start.9 = (bf16[704,256]{1,0:T(8,128)(2,1)S(1)}, bf16[704,256]{1,0:T(8,128)(2,1)S(1)}, u32[]{:S(2)}, u32[]{:S(2)}) collective-permute-start(bf16[704,256]{1,0:T(8,128)(2,1)S(1)} %collective-permute-done.2.refs_3_.refs_7_.refs_13_.refs_5_), channel_id=1, source_target_pairs={{0,2},{1,3},{4,0},{5,1},{8,4},{9,5},{12,8},{13,9},{14,12},{15,13},... | collective-permute-start | bytes 1081352 | tf_op jit(solution)/shard_map/ppermute | solution.py:34
  28.2 16.9 %collective-permute-start.12 = (bf16[704,256]{1,0:T(8,128)(2,1)}, bf16[704,256]{1,0:T(8,128)(2,1)S(1)}, u32[]{:S(2)}, u32[]{:S(2)}) collective-permute-start(bf16[704,256]{1,0:T(8,128)(2,1)} %collective-permute-done.3.refs_12_.refs_4_), channel_id=1, source_target_pairs={{0,4},{1,5},{4,8},{5,9},{8,12},{9,13},{12,14},{13,15},{14,10},{15,... | collective-permute-start | bytes 1081352 | tf_op jit(solution)/shard_map/ppermute | solution.py:34
  29.7 16.9 %collective-permute-start.13 = (bf16[704,256]{1,0:T(8,128)(2,1)}, bf16[704,256]{1,0:T(8,128)(2,1)S(1)}, u32[]{:S(2)}, u32[]{:S(2)}) collective-permute-start(bf16[704,256]{1,0:T(8,128)(2,1)} %collective-permute-done.4.refs_14_.refs_6_), channel_id=1, source_target_pairs={{0,2},{1,3},{4,0},{5,1},{8,4},{9,5},{12,8},{13,9},{14,12},{15,13},... | collective-permute-start | bytes 1081352 | tf_op jit(solution)/shard_map/ppermute | solution.py:34
  39.0 13.8 %collective-permute-start.10 = (bf16[704,256]{1,0:T(8,128)(2,1)S(1)}, bf16[704,256]{1,0:T(8,128)(2,1)S(1)}, u32[]{:S(2)}, u32[]{:S(2)}) collective-permute-start(bf16[704,256]{1,0:T(8,128)(2,1)S(1)} %collective-permute-done.8.refs_1_.refs_5_.refs_9_.refs_7_), channel_id=1, source_target_pairs={{0,4},{1,5},{4,8},{5,9},{8,12},{9,13},{12,14},{13,15},{14,10},{15,... | collective-permute-start | bytes 1081352 | tf_op jit(solution)/shard_map/ppermute | solution.py:34
  40.5 13.9 %collective-permute-start.11 = (bf16[704,256]{1,0:T(8,128)(2,1)S(1)}, bf16[704,256]{1,0:T(8,128)(2,1)S(1)}, u32[]{:S(2)}, u32[]{:S(2)}) collective-permute-start(bf16[704,256]{1,0:T(8,128)(2,1)S(1)} %collective-permute-done.9.refs_2_.refs_6_.refs_11_.refs_9_), channel_id=1, source_target_pairs={{0,2},{1,3},{4,0},{5,1},{8,4},{9,5},{12,8},{13,9},{14,12},{15,13},... | collective-permute-start | bytes 1081352 | tf_op jit(solution)/shard_map/ppermute | solution.py:34
  45.1 15.4 %collective-permute-start.16 = (bf16[704,256]{1,0:T(8,128)(2,1)S(1)}, bf16[704,256]{1,0:T(8,128)(2,1)S(1)}, u32[]{:S(2)}, u32[]{:S(2)}) collective-permute-start(bf16[704,256]{1,0:T(8,128)(2,1)S(1)} %collective-permute-done.12.refs_10_.refs_8_), channel_id=1, source_target_pairs={{0,4},{1,5},{4,8},{5,9},{8,12},{9,13},{12,14},{13,15},{14,10},{15,... | collective-permute-start | bytes 1081352 | tf_op jit(solution)/shard_map/ppermute | solution.py:34
  46.7 15.4 %collective-permute-start.17 = (bf16[704,256]{1,0:T(8,128)(2,1)S(1)}, bf16[704,256]{1,0:T(8,128)(2,1)S(1)}, u32[]{:S(2)}, u32[]{:S(2)}) collective-permute-start(bf16[704,256]{1,0:T(8,128)(2,1)S(1)} %collective-permute-done.13.refs_12_.refs_10_), channel_id=1, source_target_pairs={{0,2},{1,3},{4,0},{5,1},{8,4},{9,5},{12,8},{13,9},{14,12},{15,13},... | collective-permute-start | bytes 1081352 | tf_op jit(solution)/shard_map/ppermute | solution.py:34
  48.7 15.6 %copy-start.4 = (s32[16,64]{1,0:T(8,128)S(1)}, s32[16,64]{1,0:T(8,128)}, u32[]{:S(2)}) copy-start(s32[16,64]{1,0:T(8,128)} %param.13) | copy-start | bytes 12292
  54.4 12.5 %collective-permute-start.14 = (bf16[352,256]{1,0:T(8,128)(2,1)S(1)}, bf16[352,256]{1,0:T(8,128)(2,1)S(1)}, u32[]{:S(2)}, u32[]{:S(2)}) collective-permute-start(bf16[352,256]{1,0:T(8,128)(2,1)S(1)} %slice.18), channel_id=1, source_target_pairs={{0,4},{1,5},{4,8},{5,9},{8,12},{9,13},{12,14},{13,15},{14,10},{15,... | collective-permute-start | bytes 540680 | tf_op jit(solution)/shard_map/ppermute | solution.py:34
  56.1 10.9 %collective-permute-start.15 = (bf16[352,256]{1,0:T(8,128)(2,1)S(1)}, bf16[352,256]{1,0:T(8,128)(2,1)S(1)}, u32[]{:S(2)}, u32[]{:S(2)}) collective-permute-start(bf16[352,256]{1,0:T(8,128)(2,1)S(1)} %slice.19), channel_id=1, source_target_pairs={{0,2},{1,3},{4,0},{5,1},{8,4},{9,5},{12,8},{13,9},{14,12},{15,13},... | collective-permute-start | bytes 540680 | tf_op jit(solution)/shard_map/ppermute | solution.py:34
  62.1 5.7 %collective-permute-start.18 = (bf16[352,256]{1,0:T(8,128)(2,1)S(1)}, bf16[352,256]{1,0:T(8,128)(2,1)S(1)}, u32[]{:S(2)}, u32[]{:S(2)}) collective-permute-start(bf16[352,256]{1,0:T(8,128)(2,1)S(1)} %slice.20), channel_id=1, source_target_pairs={{0,4},{1,5},{4,8},{5,9},{8,12},{9,13},{12,14},{13,15},{14,10},{15,... | collective-permute-start | bytes 540680 | tf_op jit(solution)/shard_map/ppermute | solution.py:34
  63.8 5.5 %collective-permute-start.19 = (bf16[352,256]{1,0:T(8,128)(2,1)S(1)}, bf16[352,256]{1,0:T(8,128)(2,1)S(1)}, u32[]{:S(2)}, u32[]{:S(2)}) collective-permute-start(bf16[352,256]{1,0:T(8,128)(2,1)S(1)} %slice.21), channel_id=1, source_target_pairs={{0,2},{1,3},{4,0},{5,1},{8,4},{9,5},{12,8},{13,9},{14,12},{15,13},... | collective-permute-start | bytes 540680 | tf_op jit(solution)/shard_map/ppermute | solution.py:34
  65.7 3.7 %copy-start.3 = (s32[2]{0:T(128)S(1)}, s32[2]{0:T(128)}, u32[]{:S(2)}) copy-start(s32[2]{0:T(128)} %seq_index) | copy-start | bytes 28
  71.2 1.2 %collective-permute-start.20 = (f32[32,17]{1,0:T(8,128)S(1)}, f32[32,17]{1,0:T(8,128)S(1)}, u32[]{:S(2)}, u32[]{:S(2)}) collective-permute-start(f32[32,17]{1,0:T(8,128)S(1)} %shard_map.81), channel_id=1, source_target_pairs={{0,1},{1,0},{2,3},{3,2},{4,5},{5,4},{6,7},{7,6},{8,9},{9,8},{10,11... | collective-permute-start | bytes 6536 | tf_op jit(solution)/shard_map/ppermute | solution.py:34
  72.7 3.8 %collective-permute-start.21 = (f32[32,16]{1,0:T(8,128)S(1)}, f32[32,16]{1,0:T(8,128)S(1)}, u32[]{:S(2)}, u32[]{:S(2)}) collective-permute-start(f32[32,16]{1,0:T(8,128)S(1)} %fusion.2), channel_id=1, source_target_pairs={{0,2},{1,3},{2,0},{3,1},{4,6},{5,7},{6,4},{7,5},{8,10},{9,11},{10,... | collective-permute-start | bytes 6152 | tf_op jit(solution)/shard_map/ppermute | solution.py:34
  76.5 5.6 %collective-permute-start.22 = (f32[32,16]{1,0:T(8,128)S(1)}, f32[32,16]{1,0:T(8,128)S(1)}, u32[]{:S(2)}, u32[]{:S(2)}) collective-permute-start(f32[32,16]{1,0:T(8,128)S(1)} %fusion.3), channel_id=1, source_target_pairs={{0,12},{1,13},{2,14},{3,15},{4,8},{5,9},{6,10},{7,11},{8,4},{9,5},... | collective-permute-start | bytes 6152 | tf_op jit(solution)/shard_map/ppermute | solution.py:34
  78.8 4.7 %collective-permute-start.23 = (f32[32,16]{1,0:T(8,128)S(1)}, f32[32,16]{1,0:T(8,128)S(1)}, u32[]{:S(2)}, u32[]{:S(2)}) collective-permute-start(f32[32,16]{1,0:T(8,128)S(1)} %fusion.3), channel_id=1, source_target_pairs={{0,8},{1,9},{2,10},{3,11},{4,12},{5,13},{6,14},{7,15},{8,0},{9,1},... | collective-permute-start | bytes 6152 | tf_op jit(solution)/shard_map/ppermute | solution.py:34
  79.5 3.9 %collective-permute-start.24 = (f32[32,16]{1,0:T(8,128)S(1)}, f32[32,16]{1,0:T(8,128)S(1)}, u32[]{:S(2)}, u32[]{:S(2)}) collective-permute-start(f32[32,16]{1,0:T(8,128)S(1)} %fusion.3), channel_id=1, source_target_pairs={{0,4},{1,5},{2,6},{3,7},{4,0},{5,1},{6,2},{7,3},{8,12},{9,13},{10,... | collective-permute-start | bytes 6152 | tf_op jit(solution)/shard_map/ppermute | solution.py:34

commit v4 on v3

--- a/solution.py
+++ b/solution.py
@@ -225,20 +225,20 @@
 
 
 def finish_kernel(
-    shift, chips, rank, seq_index, seq_index_other, grads, acts, grads_other, acts_other,
-    *refs,
+    shift, chips, rank, queries, seq_index, seq_index_other, grads, acts, grads_other,
+    acts_other, *refs,
 ):
     pieces, refs = refs[:-8], refs[-8:]
     sums, sums_other = refs[0:2], refs[2:4]
     norms, dense, per_column, stack = refs[4:]
     columns = stack.shape[1]
-    queries = dense.shape[1] - 1
     sequences = seq_index.shape[0]
     length = grads.shape[0] // sequences
+    lanes = dense.shape[2] // sequences
     split = grads.shape[1] // chips
     core = device_index() % 2
-    column = lax.broadcasted_iota(jnp.int32, (columns, queries + 1), 0)
-    query = lax.broadcasted_iota(jnp.int32, (columns, queries + 1), 1)
+    column = lax.broadcasted_iota(jnp.int32, (columns, dense.shape[2]), 0)
+    query = lax.broadcasted_iota(jnp.int32, (columns, dense.shape[2]), 1) % lanes
     member = (column // rank + core * (columns // rank) == query).astype(FLOAT)
     first = 0
     for piece in pieces:
@@ -258,26 +258,51 @@
                 product[s * length : (s + 1) * length, :], axis=0, keepdims=True
             )
     raw = exact_dot(per_column[...], member)
-    slot = lax.broadcasted_iota(jnp.int32, dense.shape, 0)
-    lane = lax.broadcasted_iota(jnp.int32, (1, queries + 1), 1)
+    lane = lax.broadcasted_iota(jnp.int32, dense.shape, 2)
+    slot = lax.broadcasted_iota(jnp.int32, dense.shape, 0) * sequences + lane // lanes
+    last = lane[0] % lanes == queries
     placed = jnp.zeros(dense.shape, FLOAT)
     for side, places in enumerate((seq_index, seq_index_other)):
         for s in range(sequences):
             n = side * sequences + s
             row = raw[n : n + 1, :]
             if side == 0:
-                row = row + jnp.where(lane == queries, norms[s, 0:1, 0:1], 0.0)
-            placed = placed + jnp.where(slot == places[s], row, 0.0)
+                row = row + jnp.where(last, norms[s, 0:1, 0:1], 0.0)
+            placed = placed + jnp.where(slot == places[s], row[None], 0.0)
     dense[...] = placed
 
 
-def finish(chips, shift, places, features, pieces, sums, norms, slots, queries, rank):
+def settle_kernel(factor, parts, query_ids, influence):
+    sequences, queries = influence.shape
+    lanes = parts.shape[2] // sequences
+    total = jnp.sum(parts[...], axis=0)
+    asked = (query_ids[...] != 0).astype(FLOAT)
+    count = dot_rows(jnp.ones((8, asked.shape[1]), FLOAT), asked, lax.Precision.HIGHEST)[0:1, :]
+    for s in range(sequences):
+        at = s * lanes
+        norm = jnp.sqrt(total[:, at + queries : at + queries + 1] + 1e-06)
+        influence[s : s + 1, :] = total[:, at : at + queries] * factor / (count * norm)
+
+
+def settle(parts, query_ids, sequences, factor):
+    return pl.pallas_call(
+        functools.partial(settle_kernel, factor),
+        in_specs=[VMEM, VMEM],
+        out_specs=VMEM,
+        out_shape=jax.ShapeDtypeStruct((sequences, query_ids.shape[0]), FLOAT),
+        compiler_params=params(4),
+        cost_estimate=small_cost(),
+    )(parts, query_ids)
+
+
+def finish(chips, shift, places, features, pieces, sums, norms, queries, rank):
     columns = pieces[0].shape[1]
-    return pl.pallas_call(
-        functools.partial(finish_kernel, shift, chips, rank),
+    lanes = -(-places[0].shape[0] * (queries + 1) // 128) * 128
+    return pl.pallas_call(
+        functools.partial(finish_kernel, shift, chips, rank, queries),
         in_specs=[SMEM] * 2 + [VMEM] * (9 + len(pieces)),
         out_specs=VMEM,
-        out_shape=jax.ShapeDtypeStruct((slots, queries + 1), FLOAT),
+        out_shape=jax.ShapeDtypeStruct((2 * chips, 1, lanes), FLOAT),
         scratch_shapes=[
             pltpu.VMEM((2 * places[0].shape[0], columns), FLOAT),
             pltpu.VMEM((sum(p.shape[0] for p in pieces), columns), pieces[0].dtype),
@@ -375,8 +400,8 @@
     mine, other = split_columns(left_factor, input_side_factor)
     came = send(other, swap)
     pieces = list(merge_rows(low, mine, came))
+    pieces, grads_sent, train_ids, seq_index = in_order(pieces, grads, train_ids, seq_index)
     moving = [[send(x, forward), send(x, backward)] for x in pieces]
-    grads_sent, _ = in_order(grads, came)
     acts = jnp.where((train_ids != 0).reshape(-1, 1), acts, jnp.zeros_like(acts))
     features = [grads, acts]
     grads_other = send(grads_sent, swap)
@@ -428,13 +453,10 @@
     last = [*upper, *lower]
     dense = finish(
         chips, hops, places, [*features, grads_other, acts_other], last, [*own, *other], norms,
-        seq_count * devices, queries, rank,
-    )
-    dense = dense + send(dense, swap)
-    count = jnp.sum((query_ids != 0).astype(jnp.float32), axis=1)
+        queries, rank,
+    )
     factor = query_ids.shape[1] * math.sqrt(width * hidden / rank)
-    score = dense[:, :queries] * (factor / count)[None, :] / jnp.sqrt(dense[:, queries:] + 1e-06)
-    return to_owners(score, seq_count, 2)
+    return settle(lax.all_to_all(dense, AXIS, 0, 0), query_ids, seq_count, factor)
 
 
 def on_device(*args):

time: 84.3 us -> 81.5 us (0.967)
  blocking collectives: 0 us -> 9.9 us
  waiting for transfers between devices: 34.6 us -> 25.7 us
  starting transfers between devices: 24.8 us -> 20.9 us
  other arithmetic: 5.36 us -> 4.32 us
  Pallas kernels: 17.1 us -> 18.1 us
    all_to_all x0 -> x1, blocking collectives: none -> 9.9 us  [by_ring(): lax.all_to_all(dense, AXIS, 0, 0)]
    ppermute x25 -> x20, waiting for transfers between devices: 34.6 us -> 25.7 us  [send(): return lax.ppermute(x, AXIS, pairs)]
    ppermute x25 -> x20, starting transfers between devices: 24.8 us -> 20.9 us  [send(): return lax.ppermute(x, AXIS, pairs)]
    pallas_call x1 -> x2, Pallas kernels: 1.8 us -> 2.76 us  [the longest x1 1.92 us: finish(): pl.pallas_call(functools.partial(finish_kernel, shift, chips, rank, queri...]
  transfers between devices with their start and end apart: 25 -> 20, of which waited for: 17 -> 13; matrix products, arithmetic and copies ran while one was open for 5% -> 5% of each run, Pallas kernels for 18% -> 19%
where the time goes in v4:
time: 81.5 us; the launch traced here: 81.2 us
  waiting for transfers between devices  25.7 us (32%)
  starting transfers between devices  20.9 us (26%)
  Pallas kernels  18.1 us (22%)
  blocking collectives  9.9 us (12%)
  other arithmetic  4.32 us (5%)
  local copies, waits for them, and re-layouts  2.05 us (3%)
    ppermute x20, waiting for transfers between devices, send(): return lax.ppermute(x, AXIS, pairs)  25.7 us
    ppermute x20, starting transfers between devices, send(): return lax.ppermute(x, AXIS, pairs)  20.9 us
    pallas_call x5, Pallas kernels, project(): pl.pallas_call(functools.partial(project_kernel, jobs, split, chips, keep...  11.9 us
    all_to_all x1, blocking collectives, by_ring(): lax.all_to_all(dense, AXIS, 0, 0)  9.9 us
    select_n x1, other arithmetic, by_ring(): jnp.where((train_ids != 0).reshape(-1, 1), acts, jnp.zeros_like(acts))  3.63 us
    pallas_call x1, Pallas kernels, squared_norms_of(): pl.pallas_call(functools.partial(norms_kernel, sequences), in_specs=[VMEM...  3.3 us
    unnamed x10, local copies, waits for them, and re-layouts  1.98 us
    pallas_call x1, Pallas kernels, finish(): pl.pallas_call(functools.partial(finish_kernel, shift, chips, rank, queri...  1.92 us
  transfers between devices with their start and end apart: 20, of which 13 were waited for; matrix products, arithmetic and copies ran while one was open for 5% of the time, Pallas kernels for 19%

profile of v4, /device:TPU:0, one launch (start us, length us, event | category | flops | bytes accessed | tf_op | source)
XLA Modules:
  0.0 81.2 jit_solution(7449215268069371916)
XLA Ops:
  0.0 0.0 copy-start.1
  0.0 1.0 %copy-done.1 = bf16[448,512]{1,0:T(8,128)(2,1)S(1)} copy-done((bf16[448,512]{1,0:T(8,128)(2,1)S(1)}, bf16[448,512]{1,0:T(8,128)(2,1)}, u32[]{:S(2)}) %copy-start.1) | copy-done | bytes 458776
  1.0 0.0 copy-start.2
  1.0 0.9 %copy-done.2 = bf16[256,512]{1,0:T(8,128)(2,1)S(1)} copy-done((bf16[256,512]{1,0:T(8,128)(2,1)S(1)}, bf16[256,512]{1,0:T(8,128)(2,1)}, u32[]{:S(2)}) %copy-start.2) | copy-done | bytes 262168
  2.0 0.5 collective-permute-start
  2.5 1.3 %collective-permute-done.came = bf16[704,256]{1,0:T(8,128)(2,1)S(1)} collective-permute-done((bf16[704,256]{1,0:T(8,128)(2,1)S(1)}, bf16[704,256]{1,0:T(8,128)(2,1)S(1)}, u32[]{:S(2)}, u32[]{:S(2)}) %collective-permute-start) | collective-permute-done | bytes 360480 | tf_op jit(solution)/shard_map/ppermute | solution.py:34
  3.9 0.4 collective-permute-start.6
  4.3 2.7 %collective-permute-start.1 = (bf16[704,256]{1,0:T(8,128)(2,1)S(1)}, bf16[704,256]{1,0:T(8,128)(2,1)S(1)}, u32[]{:S(2)}, u32[]{:S(2)}) collective-permute-start(bf16[704,256]{1,0:T(8,128)(2,1)S(1)} %get-tuple-element.57.refs_1_.refs_5_.refs_9_), channel_id=1, source_target_pairs={{0,4},{1,5},{4,8},{5,9},{8,12},{9,13},{12,14},{13,15},{14,10},{15,... | collective-permute-start | bytes 1081352 | tf_op jit(solution)/shard_map/ppermute | solution.py:34
  7.1 0.0 collective-permute-start.2
  7.1 0.7 broadcast_compare_fusion
  7.8 0.0 copy-start
  7.8 2.1 %collective-permute-start.3 = (bf16[704,256]{1,0:T(8,128)(2,1)S(1)}, bf16[704,256]{1,0:T(8,128)(2,1)}, u32[]{:S(2)}, u32[]{:S(2)}) collective-permute-start(bf16[704,256]{1,0:T(8,128)(2,1)S(1)} %get-tuple-element.58.refs_10_.refs_2_), channel_id=1, source_target_pairs={{0,4},{1,5},{4,8},{5,9},{8,12},{9,13},{12,14},{13,15},{14,10},{15,... | collective-permute-start | bytes 1081352 | tf_op jit(solution)/shard_map/ppermute | solution.py:34
  9.8 0.0 collective-permute-start.5
  9.9 1.4 %collective-permute-done.5.seq_index_other = s32[2]{0:T(128)S(1)} collective-permute-done((s32[2]{0:T(128)}, s32[2]{0:T(128)S(1)}, u32[]{:S(2)}, u32[]{:S(2)}) %collective-permute-start.5) | collective-permute-done | bytes 40 | tf_op jit(solution)/shard_map/ppermute | solution.py:34
  11.3 2.8 %collective-permute-start.4 = (bf16[704,256]{1,0:T(8,128)(2,1)S(1)}, bf16[704,256]{1,0:T(8,128)(2,1)}, u32[]{:S(2)}, u32[]{:S(2)}) collective-permute-start(bf16[704,256]{1,0:T(8,128)(2,1)S(1)} %get-tuple-element.58.refs_10_.refs_2_), channel_id=1, source_target_pairs={{0,2},{1,3},{4,0},{5,1},{8,4},{9,5},{12,8},{13,9},{14,12},{15,13},... | collective-permute-start | bytes 1081352 | tf_op jit(solution)/shard_map/ppermute | solution.py:34
  14.1 3.6 %bitcast_select_fusion.acts.refs_8_.refs_4_ = bf16[512,7168]{1,0:T(8,128)(2,1)S(1)} fusion(bf16[2,256,7168]{2,1,0:T(8,128)(2,1)} %param.8, pred[512]{0:T(512)(128)(4,1)S(1)} %broadcast_in_dim.13), kind=kLoop, calls=%fused_computation | loop fusion | flops 3670016 | bytes 14680576 | tf_op jit(solution)/shard_map/jit(_where)/select_n | solution.py:405
  17.7 0.0 copy-done
  17.7 3.3 %shard_map.75.refs_8_ = f32[2,8,128]{2,1,0:T(8,128)S(1)} custom-call(bf16[512,4096]{1,0:T(8,128)(2,1)S(1)} %bitcast.4, bf16[512,7168]{1,0:T(8,128)(2,1)S(1)} %bitcast_select_fusion.acts.refs_8_.refs_4_), custom_call_target="tpu_custom_call" | custom-call | flops 1 | bytes 1 | tf_op jit(solution)/shard_map/pallas_call | solution.py:324
  21.0 0.0 collective-permute-done.1.refs_2_.refs_6_.refs_11_.refs_3_
  21.1 0.0 collective-permute-done.2.refs_3_.refs_7_.refs_13_.refs_5_
  21.1 2.7 %collective-permute-done.3.refs_12_.refs_4_ = bf16[704,256]{1,0:T(8,128)(2,1)} collective-permute-done((bf16[704,256]{1,0:T(8,128)(2,1)S(1)}, bf16[704,256]{1,0:T(8,128)(2,1)}, u32[]{:S(2)}, u32[]{:S(2)}) %collective-permute-start.3) | collective-permute-done | bytes 360480 | tf_op jit(solution)/shard_map/ppermute | solution.py:34
  23.7 1.5 %collective-permute-done.4.refs_14_.refs_6_ = bf16[704,256]{1,0:T(8,128)(2,1)} collective-permute-done((bf16[704,256]{1,0:T(8,128)(2,1)S(1)}, bf16[704,256]{1,0:T(8,128)(2,1)}, u32[]{:S(2)}, u32[]{:S(2)}) %collective-permute-start.4) | collective-permute-done | bytes 360480 | tf_op jit(solution)/shard_map/ppermute | solution.py:34
  25.3 0.0 collective-permute-done.6.refs_0_
  25.3 0.0 collective-permute-start.7
  25.3 1.6 %collective-permute-start.8 = (bf16[704,256]{1,0:T(8,128)(2,1)S(1)}, bf16[704,256]{1,0:T(8,128)(2,1)S(1)}, u32[]{:S(2)}, u32[]{:S(2)}) collective-permute-start(bf16[704,256]{1,0:T(8,128)(2,1)S(1)} %collective-permute-done.1.refs_2_.refs_6_.refs_11_.refs_3_), channel_id=1, source_target_pairs={{0,4},{1,5},{4,8},{5,9},{8,12},{9,13},{12,14},{13,15},{14,10},{15,... | collective-permute-start | bytes 1081352 | tf_op jit(solution)/shard_map/ppermute | solution.py:34
  26.9 0.4 collective-permute-start.9
  27.3 1.6 %collective-permute-start.12 = (bf16[704,256]{1,0:T(8,128)(2,1)}, bf16[704,256]{1,0:T(8,128)(2,1)S(1)}, u32[]{:S(2)}, u32[]{:S(2)}) collective-permute-start(bf16[704,256]{1,0:T(8,128)(2,1)} %collective-permute-done.3.refs_12_.refs_4_), channel_id=1, source_target_pairs={{0,4},{1,5},{4,8},{5,9},{8,12},{9,13},{12,14},{13,15},{14,10},{15,... | collective-permute-start | bytes 1081352 | tf_op jit(solution)/shard_map/ppermute | solution.py:34
  28.9 0.4 collective-permute-start.13
  29.4 4.8 %shard_map.76 = (f32[512,256]{1,0:T(8,128)S(1)}, f32[512,256]{1,0:T(8,128)S(1)}, f32[512,256]{1,0:T(8,128)S(1)}, bf16[512,4096]{1,0:T(8,128)(2,1)S(1)}) custom-call(bf16[512,4096]{1,0:T(8,128)(2,1)} %collective-permute-done.6.refs_0_, bf16[704,256]{1,0:T(8,128)(2,1)S(1)} %get-tuple-element.57.refs_1_.refs_5_.refs_9_, ...), custom_call_target="tpu_custom_call" | custom-call | flops 1 | bytes 1 | tf_op jit(solution)/shard_map/pallas_call | solution.py:215
  34.2 2.4 %collective-permute-done.8.refs_1_.refs_5_.refs_9_.refs_7_ = bf16[704,256]{1,0:T(8,128)(2,1)S(1)} collective-permute-done((bf16[704,256]{1,0:T(8,128)(2,1)S(1)}, bf16[704,256]{1,0:T(8,128)(2,1)S(1)}, u32[]{:S(2)}, u32[]{:S(2)}) %collective-permute-start.8) | collective-permute-done | bytes 360480 | tf_op jit(solution)/shard_map/ppermute | solution.py:34
  36.5 1.6 %collective-permute-done.9.refs_2_.refs_6_.refs_11_.refs_9_ = bf16[704,256]{1,0:T(8,128)(2,1)S(1)} collective-permute-done((bf16[704,256]{1,0:T(8,128)(2,1)S(1)}, bf16[704,256]{1,0:T(8,128)(2,1)S(1)}, u32[]{:S(2)}, u32[]{:S(2)}) %collective-permute-start.9) | collective-permute-done | bytes 360480 | tf_op jit(solution)/shard_map/ppermute | solution.py:34
  38.1 1.6 %collective-permute-start.10 = (bf16[704,256]{1,0:T(8,128)(2,1)S(1)}, bf16[704,256]{1,0:T(8,128)(2,1)S(1)}, u32[]{:S(2)}, u32[]{:S(2)}) collective-permute-start(bf16[704,256]{1,0:T(8,128)(2,1)S(1)} %collective-permute-done.8.refs_1_.refs_5_.refs_9_.refs_7_), channel_id=1, source_target_pairs={{0,4},{1,5},{4,8},{5,9},{8,12},{9,13},{12,14},{13,15},{14,10},{15,... | collective-permute-start | bytes 1081352 | tf_op jit(solution)/shard_map/ppermute | solution.py:34
  39.7 0.4 collective-permute-start.11
  40.2 4.1 %collective-permute-done.12.refs_10_.refs_8_ = bf16[704,256]{1,0:T(8,128)(2,1)S(1)} collective-permute-done((bf16[704,256]{1,0:T(8,128)(2,1)}, bf16[704,256]{1,0:T(8,128)(2,1)S(1)}, u32[]{:S(2)}, u32[]{:S(2)}) %collective-permute-start.12) | collective-permute-done | bytes 360480 | tf_op jit(solution)/shard_map/ppermute | solution.py:34
  44.2 1.6 %collective-permute-start.16 = (bf16[704,256]{1,0:T(8,128)(2,1)S(1)}, bf16[704,256]{1,0:T(8,128)(2,1)S(1)}, u32[]{:S(2)}, u32[]{:S(2)}) collective-permute-start(bf16[704,256]{1,0:T(8,128)(2,1)S(1)} %collective-permute-done.12.refs_10_.refs_8_), channel_id=1, source_target_pairs={{0,4},{1,5},{4,8},{5,9},{8,12},{9,13},{12,14},{13,15},{14,10},{15,... | collective-permute-start | bytes 1081352 | tf_op jit(solution)/shard_map/ppermute | solution.py:34
  45.8 0.0 collective-permute-done.13.refs_12_.refs_10_
  45.8 0.4 collective-permute-start.17
  46.3 1.6 %shard_map.77 = (f32[512,256]{1,0:T(8,128)S(1)}, f32[512,256]{1,0:T(8,128)S(1)}, f32[512,256]{1,0:T(8,128)S(1)}) custom-call(bf16[512,4096]{1,0:T(8,128)(2,1)S(1)} %get-tuple-element.69.refs_0_.grads_other, bf16[704,256]{1,0:T(8,128)(2,1)S(1)} %collective-permute-done.8.refs_1_.refs_5_.refs_9_.refs_7_, ...), custom_call_target="tpu_custom_call", output_to_operand_aliasing={{0}: (3, {}), {1}: (7, {}), {2}: (13, {})} | custom-call | flops 1 | bytes 1 | tf_op jit(solution)/shard_map/pallas_call | solution.py:215
  47.9 4.1 %collective-permute-done.10.refs_1_.refs_5_ = bf16[704,256]{1,0:T(8,128)(2,1)S(1)} collective-permute-done((bf16[704,256]{1,0:T(8,128)(2,1)S(1)}, bf16[704,256]{1,0:T(8,128)(2,1)S(1)}, u32[]{:S(2)}, u32[]{:S(2)}) %collective-permute-start.10) | collective-permute-done | bytes 360480 | tf_op jit(solution)/shard_map/ppermute | solution.py:34
  52.0 1.6 %collective-permute-done.11.refs_2_.refs_7_ = bf16[704,256]{1,0:T(8,128)(2,1)S(1)} collective-permute-done((bf16[704,256]{1,0:T(8,128)(2,1)S(1)}, bf16[704,256]{1,0:T(8,128)(2,1)S(1)}, u32[]{:S(2)}, u32[]{:S(2)}) %collective-permute-start.11) | collective-permute-done | bytes 360480 | tf_op jit(solution)/shard_map/ppermute | solution.py:34
  53.6 1.6 %collective-permute-start.14 = (bf16[352,256]{1,0:T(8,128)(2,1)S(1)}, bf16[352,256]{1,0:T(8,128)(2,1)S(1)}, u32[]{:S(2)}, u32[]{:S(2)}) collective-permute-start(bf16[352,256]{1,0:T(8,128)(2,1)S(1)} %slice.12), channel_id=1, source_target_pairs={{0,4},{1,5},{4,8},{5,9},{8,12},{9,13},{12,14},{13,15},{14,10},{15,... | collective-permute-start | bytes 540680 | tf_op jit(solution)/shard_map/ppermute | solution.py:34
  55.2 0.5 collective-permute-start.15
  55.7 0.0 collective-permute-done.7.refs_0_.refs_4_.acts_other
  55.7 3.0 %shard_map.78.refs_9_ = f32[512,256]{1,0:T(8,128)S(1)} custom-call(bf16[512,7168]{1,0:T(8,128)(2,1)S(1)} %collective-permute-done.7.refs_0_.refs_4_.acts_other, bf16[704,256]{1,0:T(8,128)(2,1)S(1)} %get-tuple-element.57.refs_1_.refs_5_.refs_9_, bf16[704,256]{1,0:T(8,128)(2,1)S(1)} %get-tuple-element.58.refs_10_.refs_2_, ...), custom_call_target="tpu_custom_call" | custom-call | flops 1 | bytes 1 | tf_op jit(solution)/shard_map/pallas_call | solution.py:215
  58.7 0.9 %collective-permute-done.16.refs_6_ = bf16[704,256]{1,0:T(8,128)(2,1)S(1)} collective-permute-done((bf16[704,256]{1,0:T(8,128)(2,1)S(1)}, bf16[704,256]{1,0:T(8,128)(2,1)S(1)}, u32[]{:S(2)}, u32[]{:S(2)}) %collective-permute-start.16) | collective-permute-done | bytes 360480 | tf_op jit(solution)/shard_map/ppermute | solution.py:34
  59.7 1.6 %collective-permute-done.17.refs_8_ = bf16[704,256]{1,0:T(8,128)(2,1)S(1)} collective-permute-done((bf16[704,256]{1,0:T(8,128)(2,1)S(1)}, bf16[704,256]{1,0:T(8,128)(2,1)S(1)}, u32[]{:S(2)}, u32[]{:S(2)}) %collective-permute-start.17) | collective-permute-done | bytes 360480 | tf_op jit(solution)/shard_map/ppermute | solution.py:34
  61.3 1.6 %collective-permute-start.18 = (bf16[352,256]{1,0:T(8,128)(2,1)S(1)}, bf16[352,256]{1,0:T(8,128)(2,1)S(1)}, u32[]{:S(2)}, u32[]{:S(2)}) collective-permute-start(bf16[352,256]{1,0:T(8,128)(2,1)S(1)} %slice.14), channel_id=1, source_target_pairs={{0,4},{1,5},{4,8},{5,9},{8,12},{9,13},{12,14},{13,15},{14,10},{15,... | collective-permute-start | bytes 540680 | tf_op jit(solution)/shard_map/ppermute | solution.py:34
  63.0 0.5 collective-permute-start.19
  63.5 1.3 %shard_map.79 = (f32[512,256]{1,0:T(8,128)S(1)}, f32[512,256]{1,0:T(8,128)S(1)}) custom-call(bf16[512,4096]{1,0:T(8,128)(2,1)S(1)} %bitcast.7, bf16[704,256]{1,0:T(8,128)(2,1)S(1)} %collective-permute-done.10.refs_1_.refs_5_, bf16[704,256]{1,0:T(8,128)(2,1)S(1)} %collective-permute-done.11.refs_2_.refs_7_, ...), custom_call_target="tpu_custom_call", output_to_operand_aliasing={{0}: (3, {}), {1}: (9, {})} | custom-call | flops 1 | bytes 1 | tf_op jit(solution)/shard_map/pallas_call | solution.py:215
  64.7 0.0 copy-start.4
  64.7 1.3 %shard_map.80 = (f32[512,256]{1,0:T(8,128)S(1)}, f32[512,256]{1,0:T(8,128)S(1)}) custom-call(bf16[512,4096]{1,0:T(8,128)(2,1)S(1)} %get-tuple-element.69.refs_0_.grads_other, bf16[704,256]{1,0:T(8,128)(2,1)S(1)} %collective-permute-done.10.refs_1_.refs_5_, ...), custom_call_target="tpu_custom_call", output_to_operand_aliasing={{0}: (3, {}), {1}: (9, {})} | custom-call | flops 1 | bytes 1 | tf_op jit(solution)/shard_map/pallas_call | solution.py:215
  66.0 0.0 collective-permute-done.14.refs_0_
  66.0 0.0 collective-permute-done.15.refs_1_
  66.0 0.0 copy-start.3
  66.1 1.0 %collective-permute-done.18.refs_2_ = bf16[352,256]{1,0:T(8,128)(2,1)S(1)} collective-permute-done((bf16[352,256]{1,0:T(8,128)(2,1)S(1)}, bf16[352,256]{1,0:T(8,128)(2,1)S(1)}, u32[]{:S(2)}, u32[]{:S(2)}) %collective-permute-start.18) | collective-permute-done | bytes 180256 | tf_op jit(solution)/shard_map/ppermute | solution.py:34
  67.0 1.5 %collective-permute-done.19.refs_3_ = bf16[352,256]{1,0:T(8,128)(2,1)S(1)} collective-permute-done((bf16[352,256]{1,0:T(8,128)(2,1)S(1)}, bf16[352,256]{1,0:T(8,128)(2,1)S(1)}, u32[]{:S(2)}, u32[]{:S(2)}) %collective-permute-start.19) | collective-permute-done | bytes 180256 | tf_op jit(solution)/shard_map/ppermute | solution.py:34
  68.5 0.0 copy-done.4
  68.5 1.9 %shard_map.81 = f32[16,1,128]{2,1,0:T(1,128)S(1)} custom-call(s32[2]{0:T(128)S(1)} %copy-done.4, s32[2]{0:T(128)S(1)} %collective-permute-done.5.seq_index_other, bf16[512,4096]{1,0:T(8,128)(2,1)S(1)} %bitcast.8, bf16[512,7168]{1,0:T(8,128)(2,1)S(1)} %bitcast_select_fusion.acts.refs_8_.refs_4_, bf16[512,4096]{1,0:T(8,128)(2,1)S(1)} %get-tuple-element.69.refs_0_.grads_other, ...), custom_call_target="tpu_custom_call" | custom-call | flops 1 | bytes 1 | tf_op jit(solution)/shard_map/pallas_call | solution.py:301
  70.4 9.9 %all_to_all.5.parts = f32[16,1,128]{2,1,0:T(1,128)S(1)} all-to-all(f32[16,1,128]{2,1,0:T(1,128)S(1)} %shard_map.81), channel_id=1, replica_groups=mesh['groups'=2,'dp'=16] {'dp'}, dimensions={0} | all-to-all | bytes 16384 | tf_op jit(solution)/shard_map/all_to_all | solution.py:459
  80.3 0.0 copy-done.3
  80.3 0.8 %shard_map.82 = f32[2,16]{1,0:T(2,128)} custom-call(f32[16,1,128]{2,1,0:T(1,128)S(1)} %all_to_all.5.parts, s32[16,64]{1,0:T(8,128)S(1)} %copy-done.3), custom_call_target="tpu_custom_call" | custom-call | flops 1 | bytes 1 | tf_op jit(solution)/shard_map/pallas_call | solution.py:288
  (7 shorter events, 0.2 us)
Async XLA Ops:
  0.0 1.0 %copy-start.1 = (bf16[448,512]{1,0:T(8,128)(2,1)S(1)}, bf16[448,512]{1,0:T(8,128)(2,1)}, u32[]{:S(2)}) copy-start(bf16[448,512]{1,0:T(8,128)(2,1)} %right.1) | copy-start | bytes 1376260
  1.0 0.9 %copy-start.2 = (bf16[256,512]{1,0:T(8,128)(2,1)S(1)}, bf16[256,512]{1,0:T(8,128)(2,1)}, u32[]{:S(2)}) copy-start(bf16[256,512]{1,0:T(8,128)(2,1)} %left.1) | copy-start | bytes 786436
  2.0 1.8 %collective-permute-start = (bf16[704,256]{1,0:T(8,128)(2,1)S(1)}, bf16[704,256]{1,0:T(8,128)(2,1)S(1)}, u32[]{:S(2)}, u32[]{:S(2)}) collective-permute-start(bf16[704,256]{1,0:T(8,128)(2,1)S(1)} %get-tuple-element.54), channel_id=1, source_target_pairs={{0,1},{1,0},{2,3},{3,2},{4,5},{5,4},{6,7},{7,6},{8,9},{9,8},{10,11... | collective-permute-start | bytes 1081352 | tf_op jit(solution)/shard_map/ppermute | solution.py:34
  3.9 21.4 %collective-permute-start.6 = (bf16[512,4096]{1,0:T(8,128)(2,1)}, bf16[512,4096]{1,0:T(8,128)(2,1)}, u32[]{:S(2)}, u32[]{:S(2)}) collective-permute-start(bf16[512,4096]{1,0:T(8,128)(2,1)} %bitcast.3), channel_id=1, source_target_pairs={{0,1},{1,0},{2,3},{3,2},{4,5},{5,4},{6,7},{7,6},{8,9},{9,8},{10,11... | collective-permute-start | bytes 12582920 | tf_op jit(solution)/shard_map/ppermute | solution.py:34
  4.3 16.7 %collective-permute-start.1 = (bf16[704,256]{1,0:T(8,128)(2,1)S(1)}, bf16[704,256]{1,0:T(8,128)(2,1)S(1)}, u32[]{:S(2)}, u32[]{:S(2)}) collective-permute-start(bf16[704,256]{1,0:T(8,128)(2,1)S(1)} %get-tuple-element.57.refs_1_.refs_5_.refs_9_), channel_id=1, source_target_pairs={{0,4},{1,5},{4,8},{5,9},{8,12},{9,13},{12,14},{13,15},{14,10},{15,... | collective-permute-start | bytes 1081352 | tf_op jit(solution)/shard_map/ppermute | solution.py:34
  7.1 14.0 %collective-permute-start.2 = (bf16[704,256]{1,0:T(8,128)(2,1)S(1)}, bf16[704,256]{1,0:T(8,128)(2,1)S(1)}, u32[]{:S(2)}, u32[]{:S(2)}) collective-permute-start(bf16[704,256]{1,0:T(8,128)(2,1)S(1)} %get-tuple-element.57.refs_1_.refs_5_.refs_9_), channel_id=1, source_target_pairs={{0,2},{1,3},{4,0},{5,1},{8,4},{9,5},{12,8},{13,9},{14,12},{15,13},... | collective-permute-start | bytes 1081352 | tf_op jit(solution)/shard_map/ppermute | solution.py:34
  7.8 10.0 %copy-start = (bf16[2,256,4096]{2,1,0:T(8,128)(2,1)S(1)}, bf16[2,256,4096]{2,1,0:T(8,128)(2,1)}, u32[]{:S(2)}) copy-start(bf16[2,256,4096]{2,1,0:T(8,128)(2,1)} %param.7) | copy-start | bytes 12582916
  7.8 16.0 %collective-permute-start.3 = (bf16[704,256]{1,0:T(8,128)(2,1)S(1)}, bf16[704,256]{1,0:T(8,128)(2,1)}, u32[]{:S(2)}, u32[]{:S(2)}) collective-permute-start(bf16[704,256]{1,0:T(8,128)(2,1)S(1)} %get-tuple-element.58.refs_10_.refs_2_), channel_id=1, source_target_pairs={{0,4},{1,5},{4,8},{5,9},{8,12},{9,13},{12,14},{13,15},{14,10},{15,... | collective-permute-start | bytes 1081352 | tf_op jit(solution)/shard_map/ppermute | solution.py:34
  9.8 1.4 %collective-permute-start.5 = (s32[2]{0:T(128)}, s32[2]{0:T(128)S(1)}, u32[]{:S(2)}, u32[]{:S(2)}) collective-permute-start(s32[2]{0:T(128)} %seq_index), channel_id=1, source_target_pairs={{0,1},{1,0},{2,3},{3,2},{4,5},{5,4},{6,7},{7,6},{8,9},{9,8},{10,11... | collective-permute-start | bytes 32 | tf_op jit(solution)/shard_map/ppermute | solution.py:34
  11.3 14.0 %collective-permute-start.4 = (bf16[704,256]{1,0:T(8,128)(2,1)S(1)}, bf16[704,256]{1,0:T(8,128)(2,1)}, u32[]{:S(2)}, u32[]{:S(2)}) collective-permute-start(bf16[704,256]{1,0:T(8,128)(2,1)S(1)} %get-tuple-element.58.refs_10_.refs_2_), channel_id=1, source_target_pairs={{0,2},{1,3},{4,0},{5,1},{8,4},{9,5},{12,8},{13,9},{14,12},{15,13},... | collective-permute-start | bytes 1081352 | tf_op jit(solution)/shard_map/ppermute | solution.py:34
  25.3 30.4 %collective-permute-start.7 = (bf16[512,7168]{1,0:T(8,128)(2,1)S(1)}, bf16[512,7168]{1,0:T(8,128)(2,1)S(1)}, u32[]{:S(2)}, u32[]{:S(2)}) collective-permute-start(bf16[512,7168]{1,0:T(8,128)(2,1)S(1)} %bitcast_select_fusion.acts.refs_8_.refs_4_), channel_id=1, source_target_pairs={{0,1},{1,0},{2,3},{3,2},{4,5},{5,4},{6,7},{7,6},{8,9},{9,8},{10,11... | collective-permute-start | bytes 22020104 | tf_op jit(solution)/shard_map/ppermute | solution.py:34
  25.3 11.2 %collective-permute-start.8 = (bf16[704,256]{1,0:T(8,128)(2,1)S(1)}, bf16[704,256]{1,0:T(8,128)(2,1)S(1)}, u32[]{:S(2)}, u32[]{:S(2)}) collective-permute-start(bf16[704,256]{1,0:T(8,128)(2,1)S(1)} %collective-permute-done.1.refs_2_.refs_6_.refs_11_.refs_3_), channel_id=1, source_target_pairs={{0,4},{1,5},{4,8},{5,9},{8,12},{9,13},{12,14},{13,15},{14,10},{15,... | collective-permute-start | bytes 1081352 | tf_op jit(solution)/shard_map/ppermute | solution.py:34
  26.9 11.2 %collective-permute-start.9 = (bf16[704,256]{1,0:T(8,128)(2,1)S(1)}, bf16[704,256]{1,0:T(8,128)(2,1)S(1)}, u32[]{:S(2)}, u32[]{:S(2)}) collective-permute-start(bf16[704,256]{1,0:T(8,128)(2,1)S(1)} %collective-permute-done.2.refs_3_.refs_7_.refs_13_.refs_5_), channel_id=1, source_target_pairs={{0,2},{1,3},{4,0},{5,1},{8,4},{9,5},{12,8},{13,9},{14,12},{15,13},... | collective-permute-start | bytes 1081352 | tf_op jit(solution)/shard_map/ppermute | solution.py:34
  27.3 16.9 %collective-permute-start.12 = (bf16[704,256]{1,0:T(8,128)(2,1)}, bf16[704,256]{1,0:T(8,128)(2,1)S(1)}, u32[]{:S(2)}, u32[]{:S(2)}) collective-permute-start(bf16[704,256]{1,0:T(8,128)(2,1)} %collective-permute-done.3.refs_12_.refs_4_), channel_id=1, source_target_pairs={{0,4},{1,5},{4,8},{5,9},{8,12},{9,13},{12,14},{13,15},{14,10},{15,... | collective-permute-start | bytes 1081352 | tf_op jit(solution)/shard_map/ppermute | solution.py:34
  28.9 16.9 %collective-permute-start.13 = (bf16[704,256]{1,0:T(8,128)(2,1)}, bf16[704,256]{1,0:T(8,128)(2,1)S(1)}, u32[]{:S(2)}, u32[]{:S(2)}) collective-permute-start(bf16[704,256]{1,0:T(8,128)(2,1)} %collective-permute-done.4.refs_14_.refs_6_), channel_id=1, source_target_pairs={{0,2},{1,3},{4,0},{5,1},{8,4},{9,5},{12,8},{13,9},{14,12},{15,13},... | collective-permute-start | bytes 1081352 | tf_op jit(solution)/shard_map/ppermute | solution.py:34
  38.1 13.8 %collective-permute-start.10 = (bf16[704,256]{1,0:T(8,128)(2,1)S(1)}, bf16[704,256]{1,0:T(8,128)(2,1)S(1)}, u32[]{:S(2)}, u32[]{:S(2)}) collective-permute-start(bf16[704,256]{1,0:T(8,128)(2,1)S(1)} %collective-permute-done.8.refs_1_.refs_5_.refs_9_.refs_7_), channel_id=1, source_target_pairs={{0,4},{1,5},{4,8},{5,9},{8,12},{9,13},{12,14},{13,15},{14,10},{15,... | collective-permute-start | bytes 1081352 | tf_op jit(solution)/shard_map/ppermute | solution.py:34
  39.7 13.9 %collective-permute-start.11 = (bf16[704,256]{1,0:T(8,128)(2,1)S(1)}, bf16[704,256]{1,0:T(8,128)(2,1)S(1)}, u32[]{:S(2)}, u32[]{:S(2)}) collective-permute-start(bf16[704,256]{1,0:T(8,128)(2,1)S(1)} %collective-permute-done.9.refs_2_.refs_6_.refs_11_.refs_9_), channel_id=1, source_target_pairs={{0,2},{1,3},{4,0},{5,1},{8,4},{9,5},{12,8},{13,9},{14,12},{15,13},... | collective-permute-start | bytes 1081352 | tf_op jit(solution)/shard_map/ppermute | solution.py:34
  44.2 15.4 %collective-permute-start.16 = (bf16[704,256]{1,0:T(8,128)(2,1)S(1)}, bf16[704,256]{1,0:T(8,128)(2,1)S(1)}, u32[]{:S(2)}, u32[]{:S(2)}) collective-permute-start(bf16[704,256]{1,0:T(8,128)(2,1)S(1)} %collective-permute-done.12.refs_10_.refs_8_), channel_id=1, source_target_pairs={{0,4},{1,5},{4,8},{5,9},{8,12},{9,13},{12,14},{13,15},{14,10},{15,... | collective-permute-start | bytes 1081352 | tf_op jit(solution)/shard_map/ppermute | solution.py:34
  45.8 15.4 %collective-permute-start.17 = (bf16[704,256]{1,0:T(8,128)(2,1)S(1)}, bf16[704,256]{1,0:T(8,128)(2,1)S(1)}, u32[]{:S(2)}, u32[]{:S(2)}) collective-permute-start(bf16[704,256]{1,0:T(8,128)(2,1)S(1)} %collective-permute-done.13.refs_12_.refs_10_), channel_id=1, source_target_pairs={{0,2},{1,3},{4,0},{5,1},{8,4},{9,5},{12,8},{13,9},{14,12},{15,13},... | collective-permute-start | bytes 1081352 | tf_op jit(solution)/shard_map/ppermute | solution.py:34
  53.6 12.4 %collective-permute-start.14 = (bf16[352,256]{1,0:T(8,128)(2,1)S(1)}, bf16[352,256]{1,0:T(8,128)(2,1)S(1)}, u32[]{:S(2)}, u32[]{:S(2)}) collective-permute-start(bf16[352,256]{1,0:T(8,128)(2,1)S(1)} %slice.12), channel_id=1, source_target_pairs={{0,4},{1,5},{4,8},{5,9},{8,12},{9,13},{12,14},{13,15},{14,10},{15,... | collective-permute-start | bytes 540680 | tf_op jit(solution)/shard_map/ppermute | solution.py:34
  55.2 10.8 %collective-permute-start.15 = (bf16[352,256]{1,0:T(8,128)(2,1)S(1)}, bf16[352,256]{1,0:T(8,128)(2,1)S(1)}, u32[]{:S(2)}, u32[]{:S(2)}) collective-permute-start(bf16[352,256]{1,0:T(8,128)(2,1)S(1)} %slice.13), channel_id=1, source_target_pairs={{0,2},{1,3},{4,0},{5,1},{8,4},{9,5},{12,8},{13,9},{14,12},{15,13},... | collective-permute-start | bytes 540680 | tf_op jit(solution)/shard_map/ppermute | solution.py:34
  61.3 5.7 %collective-permute-start.18 = (bf16[352,256]{1,0:T(8,128)(2,1)S(1)}, bf16[352,256]{1,0:T(8,128)(2,1)S(1)}, u32[]{:S(2)}, u32[]{:S(2)}) collective-permute-start(bf16[352,256]{1,0:T(8,128)(2,1)S(1)} %slice.14), channel_id=1, source_target_pairs={{0,4},{1,5},{4,8},{5,9},{8,12},{9,13},{12,14},{13,15},{14,10},{15,... | collective-permute-start | bytes 540680 | tf_op jit(solution)/shard_map/ppermute | solution.py:34
  63.0 5.5 %collective-permute-start.19 = (bf16[352,256]{1,0:T(8,128)(2,1)S(1)}, bf16[352,256]{1,0:T(8,128)(2,1)S(1)}, u32[]{:S(2)}, u32[]{:S(2)}) collective-permute-start(bf16[352,256]{1,0:T(8,128)(2,1)S(1)} %slice.15), channel_id=1, source_target_pairs={{0,2},{1,3},{4,0},{5,1},{8,4},{9,5},{12,8},{13,9},{14,12},{15,13},... | collective-permute-start | bytes 540680 | tf_op jit(solution)/shard_map/ppermute | solution.py:34
  64.7 3.8 %copy-start.4 = (s32[2]{0:T(128)S(1)}, s32[2]{0:T(128)}, u32[]{:S(2)}) copy-start(s32[2]{0:T(128)} %seq_index) | copy-start | bytes 28
  66.0 14.3 %copy-start.3 = (s32[16,64]{1,0:T(8,128)S(1)}, s32[16,64]{1,0:T(8,128)}, u32[]{:S(2)}) copy-start(s32[16,64]{1,0:T(8,128)} %query_ids.1) | copy-start | bytes 12292

commit v5 on v4

--- a/solution.py
+++ b/solution.py
@@ -224,34 +224,54 @@
     )(*[x for job in jobs for x in job.operands()])
 
 
+def far_left_kernel(shift, chips, *refs):
+    features, refs = refs[0:2], refs[2:]
+    pieces, refs = refs[0:2], refs[2:]
+    before, sums, stack = refs[0:2], refs[2:4], refs[4]
+    first, split = pieces[0].shape[0], stack.shape[0]
+    stack[0:first, :] = pieces[0][...]
+    stack[first:, :] = pieces[1][0 : split - first, :]
+    for x, old, new in zip(features, before, sums):
+        new[...] = old[...] + dot(block_of(chips, shift, x), stack[...])
+
+
+def far_left(chips, shift, features, pieces, sums):
+    split, columns = features[0].shape[1] // chips, pieces[0].shape[1]
+    return pl.pallas_call(
+        functools.partial(far_left_kernel, shift, chips),
+        in_specs=[VMEM] * 6,
+        out_specs=[VMEM] * 2,
+        out_shape=[jax.ShapeDtypeStruct(x.shape, x.dtype) for x in sums],
+        scratch_shapes=[pltpu.VMEM((split, columns), pieces[0].dtype)],
+        input_output_aliases={4: 0, 5: 1},
+        compiler_params=params(8),
+        cost_estimate=small_cost(),
+    )(*features, *pieces, *sums)
+
+
 def finish_kernel(
-    shift, chips, rank, queries, seq_index, seq_index_other, grads, acts, grads_other,
-    acts_other, *refs,
+    shift, chips, rank, queries, skip, seq_index, seq_index_other, acts, acts_other, *refs
 ):
     pieces, refs = refs[:-8], refs[-8:]
     sums, sums_other = refs[0:2], refs[2:4]
     norms, dense, per_column, stack = refs[4:]
     columns = stack.shape[1]
     sequences = seq_index.shape[0]
-    length = grads.shape[0] // sequences
+    length = acts.shape[0] // sequences
     lanes = dense.shape[2] // sequences
-    split = grads.shape[1] // chips
     core = device_index() % 2
     column = lax.broadcasted_iota(jnp.int32, (columns, dense.shape[2]), 0)
     query = lax.broadcasted_iota(jnp.int32, (columns, dense.shape[2]), 1) % lanes
     member = (column // rank + core * (columns // rank) == query).astype(FLOAT)
     first = 0
     for piece in pieces:
-        stack[first : first + piece.shape[0], :] = piece[...]
-        first += piece.shape[0]
-    sides = (
-        (block_of(chips, shift, grads), block_of(chips, shift, acts), sums),
-        (block_of(chips, shift, grads_other), block_of(chips, shift, acts_other), sums_other),
-    )
-    for side, (lefts, rights, total) in enumerate(sides):
-        product = (total[0][...] + dot(lefts, stack[0:split, :])) * (
-            total[1][...] + dot(rights, stack[split:, :])
-        )
+        count = piece.shape[0] - skip
+        stack[first : first + count, :] = piece[skip:, :]
+        first, skip = first + count, 0
+    sides = ((acts, sums), (acts_other, sums_other))
+    for side, (features, total) in enumerate(sides):
+        right = total[1][...] + dot(block_of(chips, shift, features), stack[...])
+        product = total[0][...] * right
         for s in range(sequences):
             n = side * sequences + s
             per_column[n : n + 1, :] = jnp.sum(
@@ -295,17 +315,17 @@
     )(parts, query_ids)
 
 
-def finish(chips, shift, places, features, pieces, sums, norms, queries, rank):
+def finish(chips, shift, places, features, pieces, skip, sums, norms, queries, rank):
     columns = pieces[0].shape[1]
     lanes = -(-places[0].shape[0] * (queries + 1) // 128) * 128
     return pl.pallas_call(
-        functools.partial(finish_kernel, shift, chips, rank, queries),
-        in_specs=[SMEM] * 2 + [VMEM] * (9 + len(pieces)),
+        functools.partial(finish_kernel, shift, chips, rank, queries, skip),
+        in_specs=[SMEM] * 2 + [VMEM] * (7 + len(pieces)),
         out_specs=VMEM,
         out_shape=jax.ShapeDtypeStruct((2 * chips, 1, lanes), FLOAT),
         scratch_shapes=[
             pltpu.VMEM((2 * places[0].shape[0], columns), FLOAT),
-            pltpu.VMEM((sum(p.shape[0] for p in pieces), columns), pieces[0].dtype),
+            pltpu.VMEM((features[0].shape[1] // chips, columns), pieces[0].dtype),
         ],
         compiler_params=params(12),
         cost_estimate=small_cost(),
@@ -399,13 +419,13 @@
 
     mine, other = split_columns(left_factor, input_side_factor)
     came = send(other, swap)
+    places = [seq_index, send(seq_index, swap)]
     pieces = list(merge_rows(low, mine, came))
-    pieces, grads_sent, train_ids, seq_index = in_order(pieces, grads, train_ids, seq_index)
+    pieces, places, grads_sent, train_ids = in_order(pieces, places, grads, train_ids)
     moving = [[send(x, forward), send(x, backward)] for x in pieces]
     acts = jnp.where((train_ids != 0).reshape(-1, 1), acts, jnp.zeros_like(acts))
     features = [grads, acts]
     grads_other = send(grads_sent, swap)
-    places = [seq_index, send(seq_index, swap)]
     norms = squared_norms_of(seq_count, grads, acts)
     middle = pieces[0].shape[0] // 2
     split = width // chips
@@ -450,10 +470,13 @@
                 other = project(chips, split, jobs[:1] + jobs[3:])
     upper, lower = moving
     upper, own, other = in_order(upper, own, other)
-    last = [*upper, *lower]
+    own, other = list(own), list(other)
+    own[LEFT], other[LEFT] = far_left(
+        chips, hops, [grads, grads_other], upper, [own[LEFT], other[LEFT]]
+    )
     dense = finish(
-        chips, hops, places, [*features, grads_other, acts_other], last, [*own, *other], norms,
-        queries, rank,
+        chips, hops, places, [acts, acts_other], [upper[1], *lower], split - middle,
+        [*own, *other], norms, queries, rank,
     )
     factor = query_ids.shape[1] * math.sqrt(width * hidden / rank)
     return settle(lax.all_to_all(dense, AXIS, 0, 0), query_ids, seq_count, factor)
@@ -464,6 +487,8 @@
     devices = lax.axis_size(AXIS)
     fits = (
         devices % 4 == 0
+        and devices >= 12
+        and left_rows + right_rows <= 4 * left_rows <= 2 * (left_rows + right_rows)
         and left_rows % 64 == 0
         and right_rows % 64 == 0
         and args[4].shape[1] % 256 == 0

time: 81.5 us -> 81 us (level)
  starting transfers between devices: 20.9 us -> 18.1 us
  waiting for transfers between devices: 25.7 us -> 27.6 us
    ppermute x20, starting transfers between devices: 20.9 us -> 18.1 us  [send(): return lax.ppermute(x, AXIS, pairs)]
    ppermute x20, waiting for transfers between devices: 25.7 us -> 27.6 us  [send(): return lax.ppermute(x, AXIS, pairs)]
  transfers between devices with their start and end apart: 20 -> 20, of which waited for: 13 -> 14; matrix products, arithmetic and copies ran while one was open for 5% -> 6% of each run, Pallas kernels for 19% -> 19%
where the time goes in v5:
time: 81 us; the launch traced here: 80.7 us
  waiting for transfers between devices  27.6 us (34%)
  starting transfers between devices  18.1 us (22%)
  Pallas kernels  18 us (22%)
  blocking collectives  9.91 us (12%)
  other arithmetic  4.47 us (6%)
  local copies, waits for them, and re-layouts  2.53 us (3%)
    ppermute x20, waiting for transfers between devices, send(): return lax.ppermute(x, AXIS, pairs)  27.6 us
    ppermute x20, starting transfers between devices, send(): return lax.ppermute(x, AXIS, pairs)  18.1 us
    pallas_call x5, Pallas kernels, project(): pl.pallas_call(functools.partial(project_kernel, jobs, split, chips, keep...  11.9 us
    all_to_all x1, blocking collectives, by_ring(): lax.all_to_all(dense, AXIS, 0, 0)  9.91 us
    select_n x1, other arithmetic, by_ring(): jnp.where((train_ids != 0).reshape(-1, 1), acts, jnp.zeros_like(acts))  3.78 us
    pallas_call x1, Pallas kernels, squared_norms_of(): pl.pallas_call(functools.partial(norms_kernel, sequences), in_specs=[VMEM...  3.31 us
    unnamed x10, local copies, waits for them, and re-layouts  2.46 us
  transfers between devices with their start and end apart: 20, of which 14 were waited for; matrix products, arithmetic and copies ran while one was open for 6% of the time, Pallas kernels for 19%

profile of v5, /device:TPU:0, one launch (start us, length us, event | category | flops | bytes accessed | tf_op | source)
XLA Modules:
  0.0 80.7 jit_solution(2460084265850517349)
XLA Ops:
  0.0 0.0 copy-start.1
  0.0 1.0 %copy-done.1 = bf16[448,512]{1,0:T(8,128)(2,1)S(1)} copy-done((bf16[448,512]{1,0:T(8,128)(2,1)S(1)}, bf16[448,512]{1,0:T(8,128)(2,1)}, u32[]{:S(2)}) %copy-start.1) | copy-done | bytes 458776
  1.0 0.0 copy-start.2
  1.0 0.9 %copy-done.2 = bf16[256,512]{1,0:T(8,128)(2,1)S(1)} copy-done((bf16[256,512]{1,0:T(8,128)(2,1)S(1)}, bf16[256,512]{1,0:T(8,128)(2,1)}, u32[]{:S(2)}) %copy-start.2) | copy-done | bytes 262168
  2.0 0.5 collective-permute-start
  2.5 0.1 collective-permute-start.1
  2.6 1.2 %collective-permute-done.came = bf16[704,256]{1,0:T(8,128)(2,1)S(1)} collective-permute-done((bf16[704,256]{1,0:T(8,128)(2,1)S(1)}, bf16[704,256]{1,0:T(8,128)(2,1)S(1)}, u32[]{:S(2)}, u32[]{:S(2)}) %collective-permute-start) | collective-permute-done | bytes 360480 | tf_op jit(solution)/shard_map/ppermute | solution.py:34
  3.9 0.1 collective-permute-done.1.seq_index_other
  4.0 0.4 collective-permute-start.6
  4.3 2.7 %collective-permute-start.2 = (bf16[704,256]{1,0:T(8,128)(2,1)S(1)}, bf16[704,256]{1,0:T(8,128)(2,1)S(1)}, u32[]{:S(2)}, u32[]{:S(2)}) collective-permute-start(bf16[704,256]{1,0:T(8,128)(2,1)S(1)} %get-tuple-element.60.refs_1_.refs_5_.refs_9_), channel_id=1, source_target_pairs={{0,4},{1,5},{4,8},{5,9},{8,12},{9,13},{12,14},{13,15},{14,10},{15,... | collective-permute-start | bytes 1081352 | tf_op jit(solution)/shard_map/ppermute | solution.py:34
  7.1 0.0 collective-permute-start.3
  7.1 2.0 %collective-permute-start.4 = (bf16[704,256]{1,0:T(8,128)(2,1)S(1)}, bf16[704,256]{1,0:T(8,128)(2,1)}, u32[]{:S(2)}, u32[]{:S(2)}) collective-permute-start(bf16[704,256]{1,0:T(8,128)(2,1)S(1)} %get-tuple-element.61.refs_10_.refs_2_), channel_id=1, source_target_pairs={{0,4},{1,5},{4,8},{5,9},{8,12},{9,13},{12,14},{13,15},{14,10},{15,... | collective-permute-start | bytes 1081352 | tf_op jit(solution)/shard_map/ppermute | solution.py:34
  9.1 0.0 collective-permute-start.5
  9.1 0.7 broadcast_compare_fusion
  9.8 0.0 copy-start
  9.8 3.8 %bitcast_select_fusion.acts.refs_8_.refs_4_ = bf16[512,7168]{1,0:T(8,128)(2,1)S(1)} fusion(bf16[2,256,7168]{2,1,0:T(8,128)(2,1)} %param.8, pred[512]{0:T(512)(128)(4,1)S(1)} %broadcast_in_dim.13), kind=kLoop, calls=%fused_computation | loop fusion | flops 3670016 | bytes 14680576 | tf_op jit(solution)/shard_map/jit(_where)/select_n | solution.py:426
  13.6 0.5 copy-done
  14.1 3.3 %shard_map.75.refs_7_ = f32[2,8,128]{2,1,0:T(8,128)S(1)} custom-call(bf16[512,4096]{1,0:T(8,128)(2,1)S(1)} %bitcast.4, bf16[512,7168]{1,0:T(8,128)(2,1)S(1)} %bitcast_select_fusion.acts.refs_8_.refs_4_), custom_call_target="tpu_custom_call" | custom-call | flops 1 | bytes 1 | tf_op jit(solution)/shard_map/pallas_call | solution.py:344
  17.4 0.0 collective-permute-done.2.refs_2_.refs_6_.refs_11_.refs_3_
  17.4 0.9 %collective-permute-done.3.refs_3_.refs_7_.refs_13_.refs_5_ = bf16[704,256]{1,0:T(8,128)(2,1)S(1)} collective-permute-done((bf16[704,256]{1,0:T(8,128)(2,1)S(1)}, bf16[704,256]{1,0:T(8,128)(2,1)S(1)}, u32[]{:S(2)}, u32[]{:S(2)}) %collective-permute-start.3) | collective-permute-done | bytes 360480 | tf_op jit(solution)/shard_map/ppermute | solution.py:34
  18.3 5.4 %collective-permute-done.4.refs_12_.refs_4_ = bf16[704,256]{1,0:T(8,128)(2,1)} collective-permute-done((bf16[704,256]{1,0:T(8,128)(2,1)S(1)}, bf16[704,256]{1,0:T(8,128)(2,1)}, u32[]{:S(2)}, u32[]{:S(2)}) %collective-permute-start.4) | collective-permute-done | bytes 360480 | tf_op jit(solution)/shard_map/ppermute | solution.py:34
  23.8 1.5 %collective-permute-done.5.refs_14_.refs_6_ = bf16[704,256]{1,0:T(8,128)(2,1)} collective-permute-done((bf16[704,256]{1,0:T(8,128)(2,1)S(1)}, bf16[704,256]{1,0:T(8,128)(2,1)}, u32[]{:S(2)}, u32[]{:S(2)}) %collective-permute-start.5) | collective-permute-done | bytes 360480 | tf_op jit(solution)/shard_map/ppermute | solution.py:34
  25.3 0.0 collective-permute-done.6.refs_0_
  25.3 0.0 collective-permute-start.7
  25.3 1.6 %collective-permute-start.8 = (bf16[704,256]{1,0:T(8,128)(2,1)S(1)}, bf16[704,256]{1,0:T(8,128)(2,1)S(1)}, u32[]{:S(2)}, u32[]{:S(2)}) collective-permute-start(bf16[704,256]{1,0:T(8,128)(2,1)S(1)} %collective-permute-done.2.refs_2_.refs_6_.refs_11_.refs_3_), channel_id=1, source_target_pairs={{0,4},{1,5},{4,8},{5,9},{8,12},{9,13},{12,14},{13,15},{14,10},{15,... | collective-permute-start | bytes 1081352 | tf_op jit(solution)/shard_map/ppermute | solution.py:34
  26.9 0.4 collective-permute-start.9
  27.3 1.6 %collective-permute-start.12 = (bf16[704,256]{1,0:T(8,128)(2,1)}, bf16[704,256]{1,0:T(8,128)(2,1)S(1)}, u32[]{:S(2)}, u32[]{:S(2)}) collective-permute-start(bf16[704,256]{1,0:T(8,128)(2,1)} %collective-permute-done.4.refs_12_.refs_4_), channel_id=1, source_target_pairs={{0,4},{1,5},{4,8},{5,9},{8,12},{9,13},{12,14},{13,15},{14,10},{15,... | collective-permute-start | bytes 1081352 | tf_op jit(solution)/shard_map/ppermute | solution.py:34
  28.9 0.4 collective-permute-start.13
  29.4 4.8 %shard_map.76 = (f32[512,256]{1,0:T(8,128)S(1)}, f32[512,256]{1,0:T(8,128)S(1)}, f32[512,256]{1,0:T(8,128)S(1)}, bf16[512,4096]{1,0:T(8,128)(2,1)S(1)}) custom-call(bf16[512,4096]{1,0:T(8,128)(2,1)} %collective-permute-done.6.refs_0_, bf16[704,256]{1,0:T(8,128)(2,1)S(1)} %get-tuple-element.60.refs_1_.refs_5_.refs_9_, ...), custom_call_target="tpu_custom_call" | custom-call | flops 1 | bytes 1 | tf_op jit(solution)/shard_map/pallas_call | solution.py:215
  34.1 2.4 %collective-permute-done.8.refs_1_.refs_5_.refs_9_.refs_7_ = bf16[704,256]{1,0:T(8,128)(2,1)S(1)} collective-permute-done((bf16[704,256]{1,0:T(8,128)(2,1)S(1)}, bf16[704,256]{1,0:T(8,128)(2,1)S(1)}, u32[]{:S(2)}, u32[]{:S(2)}) %collective-permute-start.8) | collective-permute-done | bytes 360480 | tf_op jit(solution)/shard_map/ppermute | solution.py:34
  36.5 1.6 %collective-permute-done.9.refs_2_.refs_6_.refs_11_.refs_9_ = bf16[704,256]{1,0:T(8,128)(2,1)S(1)} collective-permute-done((bf16[704,256]{1,0:T(8,128)(2,1)S(1)}, bf16[704,256]{1,0:T(8,128)(2,1)S(1)}, u32[]{:S(2)}, u32[]{:S(2)}) %collective-permute-start.9) | collective-permute-done | bytes 360480 | tf_op jit(solution)/shard_map/ppermute | solution.py:34
  38.1 1.6 %collective-permute-start.10 = (bf16[704,256]{1,0:T(8,128)(2,1)S(1)}, bf16[704,256]{1,0:T(8,128)(2,1)S(1)}, u32[]{:S(2)}, u32[]{:S(2)}) collective-permute-start(bf16[704,256]{1,0:T(8,128)(2,1)S(1)} %collective-permute-done.8.refs_1_.refs_5_.refs_9_.refs_7_), channel_id=1, source_target_pairs={{0,4},{1,5},{4,8},{5,9},{8,12},{9,13},{12,14},{13,15},{14,10},{15,... | collective-permute-start | bytes 1081352 | tf_op jit(solution)/shard_map/ppermute | solution.py:34
  39.7 0.4 collective-permute-start.11
  40.2 4.1 %collective-permute-done.12.refs_10_.refs_8_ = bf16[704,256]{1,0:T(8,128)(2,1)S(1)} collective-permute-done((bf16[704,256]{1,0:T(8,128)(2,1)}, bf16[704,256]{1,0:T(8,128)(2,1)S(1)}, u32[]{:S(2)}, u32[]{:S(2)}) %collective-permute-start.12) | collective-permute-done | bytes 360480 | tf_op jit(solution)/shard_map/ppermute | solution.py:34
  44.2 1.6 %collective-permute-start.16 = (bf16[704,256]{1,0:T(8,128)(2,1)S(1)}, bf16[704,256]{1,0:T(8,128)(2,1)S(1)}, u32[]{:S(2)}, u32[]{:S(2)}) collective-permute-start(bf16[704,256]{1,0:T(8,128)(2,1)S(1)} %collective-permute-done.12.refs_10_.refs_8_), channel_id=1, source_target_pairs={{0,4},{1,5},{4,8},{5,9},{8,12},{9,13},{12,14},{13,15},{14,10},{15,... | collective-permute-start | bytes 1081352 | tf_op jit(solution)/shard_map/ppermute | solution.py:34
  45.8 0.0 collective-permute-done.13.refs_12_.refs_10_
  45.9 0.4 collective-permute-start.17
  46.3 1.5 %shard_map.77 = (f32[512,256]{1,0:T(8,128)S(1)}, f32[512,256]{1,0:T(8,128)S(1)}, f32[512,256]{1,0:T(8,128)S(1)}) custom-call(bf16[512,4096]{1,0:T(8,128)(2,1)S(1)} %get-tuple-element.79.refs_0_.refs_1_, bf16[704,256]{1,0:T(8,128)(2,1)S(1)} %collective-permute-done.8.refs_1_.refs_5_.refs_9_.refs_7_, ...), custom_call_target="tpu_custom_call", output_to_operand_aliasing={{0}: (3, {}), {1}: (7, {}), {2}: (13, {})} | custom-call | flops 1 | bytes 1 | tf_op jit(solution)/shard_map/pallas_call | solution.py:215
  47.8 4.1 %collective-permute-done.10.refs_1_.refs_5_ = bf16[704,256]{1,0:T(8,128)(2,1)S(1)} collective-permute-done((bf16[704,256]{1,0:T(8,128)(2,1)S(1)}, bf16[704,256]{1,0:T(8,128)(2,1)S(1)}, u32[]{:S(2)}, u32[]{:S(2)}) %collective-permute-start.10) | collective-permute-done | bytes 360480 | tf_op jit(solution)/shard_map/ppermute | solution.py:34
  52.0 1.6 %collective-permute-done.11.refs_2_.refs_7_ = bf16[704,256]{1,0:T(8,128)(2,1)S(1)} collective-permute-done((bf16[704,256]{1,0:T(8,128)(2,1)S(1)}, bf16[704,256]{1,0:T(8,128)(2,1)S(1)}, u32[]{:S(2)}, u32[]{:S(2)}) %collective-permute-start.11) | collective-permute-done | bytes 360480 | tf_op jit(solution)/shard_map/ppermute | solution.py:34
  53.6 1.6 %collective-permute-start.14 = (bf16[352,256]{1,0:T(8,128)(2,1)S(1)}, bf16[352,256]{1,0:T(8,128)(2,1)S(1)}, u32[]{:S(2)}, u32[]{:S(2)}) collective-permute-start(bf16[352,256]{1,0:T(8,128)(2,1)S(1)} %slice.12), channel_id=1, source_target_pairs={{0,4},{1,5},{4,8},{5,9},{8,12},{9,13},{12,14},{13,15},{14,10},{15,... | collective-permute-start | bytes 540680 | tf_op jit(solution)/shard_map/ppermute | solution.py:34
  55.2 0.5 collective-permute-start.15
  55.7 0.0 collective-permute-done.7.refs_0_.refs_4_.acts_other
  55.7 3.0 %shard_map.78.refs_9_ = f32[512,256]{1,0:T(8,128)S(1)} custom-call(bf16[512,7168]{1,0:T(8,128)(2,1)S(1)} %collective-permute-done.7.refs_0_.refs_4_.acts_other, bf16[704,256]{1,0:T(8,128)(2,1)S(1)} %get-tuple-element.60.refs_1_.refs_5_.refs_9_, bf16[704,256]{1,0:T(8,128)(2,1)S(1)} %get-tuple-element.61.refs_10_.refs_2_, ...), custom_call_target="tpu_custom_call" | custom-call | flops 1 | bytes 1 | tf_op jit(solution)/shard_map/pallas_call | solution.py:215
  58.8 0.9 %collective-permute-done.16.refs_6_ = bf16[704,256]{1,0:T(8,128)(2,1)S(1)} collective-permute-done((bf16[704,256]{1,0:T(8,128)(2,1)S(1)}, bf16[704,256]{1,0:T(8,128)(2,1)S(1)}, u32[]{:S(2)}, u32[]{:S(2)}) %collective-permute-start.16) | collective-permute-done | bytes 360480 | tf_op jit(solution)/shard_map/ppermute | solution.py:34
  59.7 1.6 %collective-permute-done.17.refs_8_ = bf16[704,256]{1,0:T(8,128)(2,1)S(1)} collective-permute-done((bf16[704,256]{1,0:T(8,128)(2,1)S(1)}, bf16[704,256]{1,0:T(8,128)(2,1)S(1)}, u32[]{:S(2)}, u32[]{:S(2)}) %collective-permute-start.17) | collective-permute-done | bytes 360480 | tf_op jit(solution)/shard_map/ppermute | solution.py:34
  61.3 1.6 %collective-permute-start.18 = (bf16[352,256]{1,0:T(8,128)(2,1)S(1)}, bf16[352,256]{1,0:T(8,128)(2,1)S(1)}, u32[]{:S(2)}, u32[]{:S(2)}) collective-permute-start(bf16[352,256]{1,0:T(8,128)(2,1)S(1)} %slice.14), channel_id=1, source_target_pairs={{0,4},{1,5},{4,8},{5,9},{8,12},{9,13},{12,14},{13,15},{14,10},{15,... | collective-permute-start | bytes 540680 | tf_op jit(solution)/shard_map/ppermute | solution.py:34
  63.0 0.5 collective-permute-start.19
  63.5 1.3 %shard_map.79 = (f32[512,256]{1,0:T(8,128)S(1)}, f32[512,256]{1,0:T(8,128)S(1)}) custom-call(bf16[512,4096]{1,0:T(8,128)(2,1)S(1)} %bitcast.7, bf16[704,256]{1,0:T(8,128)(2,1)S(1)} %collective-permute-done.10.refs_1_.refs_5_, bf16[704,256]{1,0:T(8,128)(2,1)S(1)} %collective-permute-done.11.refs_2_.refs_7_, ...), custom_call_target="tpu_custom_call", output_to_operand_aliasing={{0}: (3, {}), {1}: (9, {})} | custom-call | flops 1 | bytes 1 | tf_op jit(solution)/shard_map/pallas_call | solution.py:215
  64.8 1.3 %shard_map.80 = (f32[512,256]{1,0:T(8,128)S(1)}, f32[512,256]{1,0:T(8,128)S(1)}) custom-call(bf16[512,4096]{1,0:T(8,128)(2,1)S(1)} %get-tuple-element.79.refs_0_.refs_1_, bf16[704,256]{1,0:T(8,128)(2,1)S(1)} %collective-permute-done.10.refs_1_.refs_5_, ...), custom_call_target="tpu_custom_call", output_to_operand_aliasing={{0}: (3, {}), {1}: (9, {})} | custom-call | flops 1 | bytes 1 | tf_op jit(solution)/shard_map/pallas_call | solution.py:215
  66.0 0.0 copy-start.4
  66.0 0.0 collective-permute-done.14.refs_2_
  66.1 0.0 collective-permute-done.15.refs_3_.refs_0_
  66.1 0.5 shard_map.81
  66.5 0.5 collective-permute-done.18.refs_1_
  67.0 1.5 %collective-permute-done.19.refs_2_ = bf16[352,256]{1,0:T(8,128)(2,1)S(1)} collective-permute-done((bf16[352,256]{1,0:T(8,128)(2,1)S(1)}, bf16[352,256]{1,0:T(8,128)(2,1)S(1)}, u32[]{:S(2)}, u32[]{:S(2)}) %collective-permute-start.19) | collective-permute-done | bytes 180256 | tf_op jit(solution)/shard_map/ppermute | solution.py:34
  68.5 0.0 copy-done.4
  68.5 0.0 copy-start.3
  68.5 1.5 %shard_map.82 = f32[16,1,128]{2,1,0:T(1,128)S(1)} custom-call(s32[2]{0:T(128)S(1)} %copy-done.4, s32[2]{0:T(128)S(1)} %collective-permute-done.1.seq_index_other, bf16[512,7168]{1,0:T(8,128)(2,1)S(1)} %bitcast_select_fusion.acts.refs_8_.refs_4_, bf16[512,7168]{1,0:T(8,128)(2,1)S(1)} %collective-permute-done.7.refs_0_.refs_4_.acts_other, ...), custom_call_target="tpu_custom_call" | custom-call | flops 1 | bytes 1 | tf_op jit(solution)/shard_map/pallas_call | solution.py:321
  70.0 9.9 %all_to_all.5.parts = f32[16,1,128]{2,1,0:T(1,128)S(1)} all-to-all(f32[16,1,128]{2,1,0:T(1,128)S(1)} %shard_map.82), channel_id=1, replica_groups=mesh['groups'=2,'dp'=16] {'dp'}, dimensions={0} | all-to-all | bytes 16384 | tf_op jit(solution)/shard_map/all_to_all | solution.py:482
  79.9 0.0 copy-done.3
  79.9 0.8 %shard_map.83 = f32[2,16]{1,0:T(2,128)} custom-call(f32[16,1,128]{2,1,0:T(1,128)S(1)} %all_to_all.5.parts, s32[16,64]{1,0:T(8,128)S(1)} %copy-done.3), custom_call_target="tpu_custom_call" | custom-call | flops 1 | bytes 1 | tf_op jit(solution)/shard_map/pallas_call | solution.py:308
  (7 shorter events, 0.2 us)
Async XLA Ops:
  0.0 1.0 %copy-start.1 = (bf16[448,512]{1,0:T(8,128)(2,1)S(1)}, bf16[448,512]{1,0:T(8,128)(2,1)}, u32[]{:S(2)}) copy-start(bf16[448,512]{1,0:T(8,128)(2,1)} %right.1) | copy-start | bytes 1376260
  1.0 0.9 %copy-start.2 = (bf16[256,512]{1,0:T(8,128)(2,1)S(1)}, bf16[256,512]{1,0:T(8,128)(2,1)}, u32[]{:S(2)}) copy-start(bf16[256,512]{1,0:T(8,128)(2,1)} %left.1) | copy-start | bytes 786436
  2.0 1.8 %collective-permute-start = (bf16[704,256]{1,0:T(8,128)(2,1)S(1)}, bf16[704,256]{1,0:T(8,128)(2,1)S(1)}, u32[]{:S(2)}, u32[]{:S(2)}) collective-permute-start(bf16[704,256]{1,0:T(8,128)(2,1)S(1)} %get-tuple-element.57), channel_id=1, source_target_pairs={{0,1},{1,0},{2,3},{3,2},{4,5},{5,4},{6,7},{7,6},{8,9},{9,8},{10,11... | collective-permute-start | bytes 1081352 | tf_op jit(solution)/shard_map/ppermute | solution.py:34
  2.5 1.4 %collective-permute-start.1 = (s32[2]{0:T(128)}, s32[2]{0:T(128)S(1)}, u32[]{:S(2)}, u32[]{:S(2)}) collective-permute-start(s32[2]{0:T(128)} %seq_index), channel_id=1, source_target_pairs={{0,1},{1,0},{2,3},{3,2},{4,5},{5,4},{6,7},{7,6},{8,9},{9,8},{10,11... | collective-permute-start | bytes 32 | tf_op jit(solution)/shard_map/ppermute | solution.py:34
  4.0 21.3 %collective-permute-start.6 = (bf16[512,4096]{1,0:T(8,128)(2,1)}, bf16[512,4096]{1,0:T(8,128)(2,1)}, u32[]{:S(2)}, u32[]{:S(2)}) collective-permute-start(bf16[512,4096]{1,0:T(8,128)(2,1)} %bitcast.3), channel_id=1, source_target_pairs={{0,1},{1,0},{2,3},{3,2},{4,5},{5,4},{6,7},{7,6},{8,9},{9,8},{10,11... | collective-permute-start | bytes 12582920 | tf_op jit(solution)/shard_map/ppermute | solution.py:34
  4.3 13.1 %collective-permute-start.2 = (bf16[704,256]{1,0:T(8,128)(2,1)S(1)}, bf16[704,256]{1,0:T(8,128)(2,1)S(1)}, u32[]{:S(2)}, u32[]{:S(2)}) collective-permute-start(bf16[704,256]{1,0:T(8,128)(2,1)S(1)} %get-tuple-element.60.refs_1_.refs_5_.refs_9_), channel_id=1, source_target_pairs={{0,4},{1,5},{4,8},{5,9},{8,12},{9,13},{12,14},{13,15},{14,10},{15,... | collective-permute-start | bytes 1081352 | tf_op jit(solution)/shard_map/ppermute | solution.py:34
  7.1 11.3 %collective-permute-start.3 = (bf16[704,256]{1,0:T(8,128)(2,1)S(1)}, bf16[704,256]{1,0:T(8,128)(2,1)S(1)}, u32[]{:S(2)}, u32[]{:S(2)}) collective-permute-start(bf16[704,256]{1,0:T(8,128)(2,1)S(1)} %get-tuple-element.60.refs_1_.refs_5_.refs_9_), channel_id=1, source_target_pairs={{0,2},{1,3},{4,0},{5,1},{8,4},{9,5},{12,8},{13,9},{14,12},{15,13},... | collective-permute-start | bytes 1081352 | tf_op jit(solution)/shard_map/ppermute | solution.py:34
  7.1 16.7 %collective-permute-start.4 = (bf16[704,256]{1,0:T(8,128)(2,1)S(1)}, bf16[704,256]{1,0:T(8,128)(2,1)}, u32[]{:S(2)}, u32[]{:S(2)}) collective-permute-start(bf16[704,256]{1,0:T(8,128)(2,1)S(1)} %get-tuple-element.61.refs_10_.refs_2_), channel_id=1, source_target_pairs={{0,4},{1,5},{4,8},{5,9},{8,12},{9,13},{12,14},{13,15},{14,10},{15,... | collective-permute-start | bytes 1081352 | tf_op jit(solution)/shard_map/ppermute | solution.py:34
  9.1 16.2 %collective-permute-start.5 = (bf16[704,256]{1,0:T(8,128)(2,1)S(1)}, bf16[704,256]{1,0:T(8,128)(2,1)}, u32[]{:S(2)}, u32[]{:S(2)}) collective-permute-start(bf16[704,256]{1,0:T(8,128)(2,1)S(1)} %get-tuple-element.61.refs_10_.refs_2_), channel_id=1, source_target_pairs={{0,2},{1,3},{4,0},{5,1},{8,4},{9,5},{12,8},{13,9},{14,12},{15,13},... | collective-permute-start | bytes 1081352 | tf_op jit(solution)/shard_map/ppermute | solution.py:34
  9.8 4.3 %copy-start = (bf16[2,256,4096]{2,1,0:T(8,128)(2,1)S(1)}, bf16[2,256,4096]{2,1,0:T(8,128)(2,1)}, u32[]{:S(2)}) copy-start(bf16[2,256,4096]{2,1,0:T(8,128)(2,1)} %param.7) | copy-start | bytes 12582916
  25.3 30.4 %collective-permute-start.7 = (bf16[512,7168]{1,0:T(8,128)(2,1)S(1)}, bf16[512,7168]{1,0:T(8,128)(2,1)S(1)}, u32[]{:S(2)}, u32[]{:S(2)}) collective-permute-start(bf16[512,7168]{1,0:T(8,128)(2,1)S(1)} %bitcast_select_fusion.acts.refs_8_.refs_4_), channel_id=1, source_target_pairs={{0,1},{1,0},{2,3},{3,2},{4,5},{5,4},{6,7},{7,6},{8,9},{9,8},{10,11... | collective-permute-start | bytes 22020104 | tf_op jit(solution)/shard_map/ppermute | solution.py:34
  25.3 11.2 %collective-permute-start.8 = (bf16[704,256]{1,0:T(8,128)(2,1)S(1)}, bf16[704,256]{1,0:T(8,128)(2,1)S(1)}, u32[]{:S(2)}, u32[]{:S(2)}) collective-permute-start(bf16[704,256]{1,0:T(8,128)(2,1)S(1)} %collective-permute-done.2.refs_2_.refs_6_.refs_11_.refs_3_), channel_id=1, source_target_pairs={{0,4},{1,5},{4,8},{5,9},{8,12},{9,13},{12,14},{13,15},{14,10},{15,... | collective-permute-start | bytes 1081352 | tf_op jit(solution)/shard_map/ppermute | solution.py:34
  26.9 11.2 %collective-permute-start.9 = (bf16[704,256]{1,0:T(8,128)(2,1)S(1)}, bf16[704,256]{1,0:T(8,128)(2,1)S(1)}, u32[]{:S(2)}, u32[]{:S(2)}) collective-permute-start(bf16[704,256]{1,0:T(8,128)(2,1)S(1)} %collective-permute-done.3.refs_3_.refs_7_.refs_13_.refs_5_), channel_id=1, source_target_pairs={{0,2},{1,3},{4,0},{5,1},{8,4},{9,5},{12,8},{13,9},{14,12},{15,13},... | collective-permute-start | bytes 1081352 | tf_op jit(solution)/shard_map/ppermute | solution.py:34
  27.3 16.9 %collective-permute-start.12 = (bf16[704,256]{1,0:T(8,128)(2,1)}, bf16[704,256]{1,0:T(8,128)(2,1)S(1)}, u32[]{:S(2)}, u32[]{:S(2)}) collective-permute-start(bf16[704,256]{1,0:T(8,128)(2,1)} %collective-permute-done.4.refs_12_.refs_4_), channel_id=1, source_target_pairs={{0,4},{1,5},{4,8},{5,9},{8,12},{9,13},{12,14},{13,15},{14,10},{15,... | collective-permute-start | bytes 1081352 | tf_op jit(solution)/shard_map/ppermute | solution.py:34
  28.9 16.9 %collective-permute-start.13 = (bf16[704,256]{1,0:T(8,128)(2,1)}, bf16[704,256]{1,0:T(8,128)(2,1)S(1)}, u32[]{:S(2)}, u32[]{:S(2)}) collective-permute-start(bf16[704,256]{1,0:T(8,128)(2,1)} %collective-permute-done.5.refs_14_.refs_6_), channel_id=1, source_target_pairs={{0,2},{1,3},{4,0},{5,1},{8,4},{9,5},{12,8},{13,9},{14,12},{15,13},... | collective-permute-start | bytes 1081352 | tf_op jit(solution)/shard_map/ppermute | solution.py:34
  38.1 13.8 %collective-permute-start.10 = (bf16[704,256]{1,0:T(8,128)(2,1)S(1)}, bf16[704,256]{1,0:T(8,128)(2,1)S(1)}, u32[]{:S(2)}, u32[]{:S(2)}) collective-permute-start(bf16[704,256]{1,0:T(8,128)(2,1)S(1)} %collective-permute-done.8.refs_1_.refs_5_.refs_9_.refs_7_), channel_id=1, source_target_pairs={{0,4},{1,5},{4,8},{5,9},{8,12},{9,13},{12,14},{13,15},{14,10},{15,... | collective-permute-start | bytes 1081352 | tf_op jit(solution)/shard_map/ppermute | solution.py:34
  39.7 13.9 %collective-permute-start.11 = (bf16[704,256]{1,0:T(8,128)(2,1)S(1)}, bf16[704,256]{1,0:T(8,128)(2,1)S(1)}, u32[]{:S(2)}, u32[]{:S(2)}) collective-permute-start(bf16[704,256]{1,0:T(8,128)(2,1)S(1)} %collective-permute-done.9.refs_2_.refs_6_.refs_11_.refs_9_), channel_id=1, source_target_pairs={{0,2},{1,3},{4,0},{5,1},{8,4},{9,5},{12,8},{13,9},{14,12},{15,13},... | collective-permute-start | bytes 1081352 | tf_op jit(solution)/shard_map/ppermute | solution.py:34
  44.2 15.4 %collective-permute-start.16 = (bf16[704,256]{1,0:T(8,128)(2,1)S(1)}, bf16[704,256]{1,0:T(8,128)(2,1)S(1)}, u32[]{:S(2)}, u32[]{:S(2)}) collective-permute-start(bf16[704,256]{1,0:T(8,128)(2,1)S(1)} %collective-permute-done.12.refs_10_.refs_8_), channel_id=1, source_target_pairs={{0,4},{1,5},{4,8},{5,9},{8,12},{9,13},{12,14},{13,15},{14,10},{15,... | collective-permute-start | bytes 1081352 | tf_op jit(solution)/shard_map/ppermute | solution.py:34
  45.9 15.4 %collective-permute-start.17 = (bf16[704,256]{1,0:T(8,128)(2,1)S(1)}, bf16[704,256]{1,0:T(8,128)(2,1)S(1)}, u32[]{:S(2)}, u32[]{:S(2)}) collective-permute-start(bf16[704,256]{1,0:T(8,128)(2,1)S(1)} %collective-permute-done.13.refs_12_.refs_10_), channel_id=1, source_target_pairs={{0,2},{1,3},{4,0},{5,1},{8,4},{9,5},{12,8},{13,9},{14,12},{15,13},... | collective-permute-start | bytes 1081352 | tf_op jit(solution)/shard_map/ppermute | solution.py:34
  53.6 12.4 %collective-permute-start.14 = (bf16[352,256]{1,0:T(8,128)(2,1)S(1)}, bf16[352,256]{1,0:T(8,128)(2,1)S(1)}, u32[]{:S(2)}, u32[]{:S(2)}) collective-permute-start(bf16[352,256]{1,0:T(8,128)(2,1)S(1)} %slice.12), channel_id=1, source_target_pairs={{0,4},{1,5},{4,8},{5,9},{8,12},{9,13},{12,14},{13,15},{14,10},{15,... | collective-permute-start | bytes 540680 | tf_op jit(solution)/shard_map/ppermute | solution.py:34
  55.2 10.8 %collective-permute-start.15 = (bf16[352,256]{1,0:T(8,128)(2,1)S(1)}, bf16[352,256]{1,0:T(8,128)(2,1)S(1)}, u32[]{:S(2)}, u32[]{:S(2)}) collective-permute-start(bf16[352,256]{1,0:T(8,128)(2,1)S(1)} %slice.13), channel_id=1, source_target_pairs={{0,2},{1,3},{4,0},{5,1},{8,4},{9,5},{12,8},{13,9},{14,12},{15,13},... | collective-permute-start | bytes 540680 | tf_op jit(solution)/shard_map/ppermute | solution.py:34
  61.3 5.7 %collective-permute-start.18 = (bf16[352,256]{1,0:T(8,128)(2,1)S(1)}, bf16[352,256]{1,0:T(8,128)(2,1)S(1)}, u32[]{:S(2)}, u32[]{:S(2)}) collective-permute-start(bf16[352,256]{1,0:T(8,128)(2,1)S(1)} %slice.14), channel_id=1, source_target_pairs={{0,4},{1,5},{4,8},{5,9},{8,12},{9,13},{12,14},{13,15},{14,10},{15,... | collective-permute-start | bytes 540680 | tf_op jit(solution)/shard_map/ppermute | solution.py:34
  63.0 5.5 %collective-permute-start.19 = (bf16[352,256]{1,0:T(8,128)(2,1)S(1)}, bf16[352,256]{1,0:T(8,128)(2,1)S(1)}, u32[]{:S(2)}, u32[]{:S(2)}) collective-permute-start(bf16[352,256]{1,0:T(8,128)(2,1)S(1)} %slice.15), channel_id=1, source_target_pairs={{0,2},{1,3},{4,0},{5,1},{8,4},{9,5},{12,8},{13,9},{14,12},{15,13},... | collective-permute-start | bytes 540680 | tf_op jit(solution)/shard_map/ppermute | solution.py:34
  66.0 2.5 %copy-start.4 = (s32[2]{0:T(128)S(1)}, s32[2]{0:T(128)}, u32[]{:S(2)}) copy-start(s32[2]{0:T(128)} %seq_index) | copy-start | bytes 28
  68.5 11.4 %copy-start.3 = (s32[16,64]{1,0:T(8,128)S(1)}, s32[16,64]{1,0:T(8,128)}, u32[]{:S(2)}) copy-start(s32[16,64]{1,0:T(8,128)} %query_ids.1) | copy-start | bytes 12292

commit v6 on v5

--- a/solution.py
+++ b/solution.py
@@ -262,7 +262,8 @@
     core = device_index() % 2
     column = lax.broadcasted_iota(jnp.int32, (columns, dense.shape[2]), 0)
     query = lax.broadcasted_iota(jnp.int32, (columns, dense.shape[2]), 1) % lanes
-    member = (column // rank + core * (columns // rank) == query).astype(FLOAT)
+    begin = (query - core * (columns // rank)) * rank
+    member = ((column >= begin) & (column < begin + rank)).astype(FLOAT)
     first = 0
     for piece in pieces:
         count = piece.shape[0] - skip
@@ -292,27 +293,26 @@
     dense[...] = placed
 
 
-def settle_kernel(factor, parts, query_ids, influence):
+def settle_kernel(parts, norms, influence):
     sequences, queries = influence.shape
     lanes = parts.shape[2] // sequences
     total = jnp.sum(parts[...], axis=0)
-    asked = (query_ids[...] != 0).astype(FLOAT)
-    count = dot_rows(jnp.ones((8, asked.shape[1]), FLOAT), asked, lax.Precision.HIGHEST)[0:1, :]
+    weight = norms[sequences, 0:1, 0:queries]
     for s in range(sequences):
         at = s * lanes
         norm = jnp.sqrt(total[:, at + queries : at + queries + 1] + 1e-06)
-        influence[s : s + 1, :] = total[:, at : at + queries] * factor / (count * norm)
-
-
-def settle(parts, query_ids, sequences, factor):
-    return pl.pallas_call(
-        functools.partial(settle_kernel, factor),
+        influence[s : s + 1, :] = total[:, at : at + queries] * weight / norm
+
+
+def settle(parts, norms, sequences, queries):
+    return pl.pallas_call(
+        settle_kernel,
         in_specs=[VMEM, VMEM],
         out_specs=VMEM,
-        out_shape=jax.ShapeDtypeStruct((sequences, query_ids.shape[0]), FLOAT),
+        out_shape=jax.ShapeDtypeStruct((sequences, queries), FLOAT),
         compiler_params=params(4),
         cost_estimate=small_cost(),
-    )(parts, query_ids)
+    )(parts, norms)
 
 
 def finish(chips, shift, places, features, pieces, skip, sums, norms, queries, rank):
@@ -332,23 +332,26 @@
     )(*places, *features, *pieces, *sums, norms)
 
 
-def norms_kernel(sequences, grads, acts, norms):
+def norms_kernel(sequences, factor, grads, acts, query_ids, norms):
     length = grads.shape[0] // sequences
     for s in range(sequences):
         rows = slice(s * length, (s + 1) * length)
         value = dot_rows(grads[rows, :], grads[rows, :]) * dot_rows(acts[rows, :], acts[rows, :])
         norms[s] = jnp.broadcast_to(jnp.sum(value, keepdims=True), norms.shape[1:])
-
-
-def squared_norms_of(sequences, grads, acts):
-    return pl.pallas_call(
-        functools.partial(norms_kernel, sequences),
-        in_specs=[VMEM, VMEM],
+    asked = (query_ids[...] != 0).astype(FLOAT)
+    count = dot_rows(jnp.ones((8, asked.shape[1]), FLOAT), asked, lax.Precision.HIGHEST)
+    norms[sequences, :, 0 : asked.shape[0]] = factor / count
+
+
+def squared_norms_of(sequences, factor, grads, acts, query_ids):
+    return pl.pallas_call(
+        functools.partial(norms_kernel, sequences, factor),
+        in_specs=[VMEM] * 3,
         out_specs=VMEM,
-        out_shape=jax.ShapeDtypeStruct((sequences, 8, 128), FLOAT),
+        out_shape=jax.ShapeDtypeStruct((sequences + 1, 8, 128), FLOAT),
         compiler_params=params(8),
         cost_estimate=small_cost(),
-    )(grads, acts)
+    )(grads, acts, query_ids)
 
 
 def squared_norms(live, grads, acts):
@@ -426,7 +429,8 @@
     acts = jnp.where((train_ids != 0).reshape(-1, 1), acts, jnp.zeros_like(acts))
     features = [grads, acts]
     grads_other = send(grads_sent, swap)
-    norms = squared_norms_of(seq_count, grads, acts)
+    factor = query_ids.shape[1] * math.sqrt(width * hidden / rank)
+    norms = squared_norms_of(seq_count, factor, grads, acts, query_ids)
     middle = pieces[0].shape[0] // 2
     split = width // chips
     shifts = [0]
@@ -478,8 +482,7 @@
         chips, hops, places, [acts, acts_other], [upper[1], *lower], split - middle,
         [*own, *other], norms, queries, rank,
     )
-    factor = query_ids.shape[1] * math.sqrt(width * hidden / rank)
-    return settle(lax.all_to_all(dense, AXIS, 0, 0), query_ids, seq_count, factor)
+    return settle(lax.all_to_all(dense, AXIS, 0, 0), norms, seq_count, queries)
 
 
 def on_device(*args):

time: 81 us -> 80.9 us (level)
  transfers between devices with their start and end apart: 20 -> 20, of which waited for: 14 -> 14; matrix products, arithmetic and copies ran while one was open for 6% -> 6% of each run, Pallas kernels for 19% -> 20%
where the time goes in v6:
time: 80.9 us; the launch traced here: 80.6 us
  waiting for transfers between devices  27.5 us (34%)
  starting transfers between devices  18.1 us (22%)
  Pallas kernels  18 us (22%)
  blocking collectives  9.91 us (12%)
  other arithmetic  4.47 us (6%)
  local copies, waits for them, and re-layouts  2.52 us (3%)
    ppermute x20, waiting for transfers between devices, send(): return lax.ppermute(x, AXIS, pairs)  27.5 us
    ppermute x20, starting transfers between devices, send(): return lax.ppermute(x, AXIS, pairs)  18.1 us
    pallas_call x5, Pallas kernels, project(): pl.pallas_call(functools.partial(project_kernel, jobs, split, chips, keep...  11.9 us
    all_to_all x1, blocking collectives, by_ring(): return settle(lax.all_to_all(dense, AXIS, 0, 0), norms, seq_count, queries)  9.91 us
    select_n x1, other arithmetic, by_ring(): jnp.where((train_ids != 0).reshape(-1, 1), acts, jnp.zeros_like(acts))  3.78 us
    pallas_call x1, Pallas kernels, squared_norms_of(): pl.pallas_call(functools.partial(norms_kernel, sequences, factor), in_spe...  3.33 us
    unnamed x10, local copies, waits for them, and re-layouts  2.45 us
  transfers between devices with their start and end apart: 20, of which 14 were waited for; matrix products, arithmetic and copies ran while one was open for 6% of the time, Pallas kernels for 20%

profile of v6, /device:TPU:0, one launch (start us, length us, event | category | flops | bytes accessed | tf_op | source)
XLA Modules:
  0.0 80.6 jit_solution(16161909372769445077)
XLA Ops:
  0.0 0.0 copy-start.1
  0.0 1.0 %copy-done.1 = bf16[448,512]{1,0:T(8,128)(2,1)S(1)} copy-done((bf16[448,512]{1,0:T(8,128)(2,1)S(1)}, bf16[448,512]{1,0:T(8,128)(2,1)}, u32[]{:S(2)}) %copy-start.1) | copy-done | bytes 458776
  1.0 0.0 copy-start.2
  1.0 0.9 %copy-done.2 = bf16[256,512]{1,0:T(8,128)(2,1)S(1)} copy-done((bf16[256,512]{1,0:T(8,128)(2,1)S(1)}, bf16[256,512]{1,0:T(8,128)(2,1)}, u32[]{:S(2)}) %copy-start.2) | copy-done | bytes 262168
  2.0 0.5 collective-permute-start
  2.5 0.1 collective-permute-start.1
  2.6 1.2 %collective-permute-done.came = bf16[704,256]{1,0:T(8,128)(2,1)S(1)} collective-permute-done((bf16[704,256]{1,0:T(8,128)(2,1)S(1)}, bf16[704,256]{1,0:T(8,128)(2,1)S(1)}, u32[]{:S(2)}, u32[]{:S(2)}) %collective-permute-start) | collective-permute-done | bytes 360480 | tf_op jit(solution)/shard_map/ppermute | solution.py:34
  3.9 0.1 collective-permute-done.1.seq_index_other
  4.0 0.4 collective-permute-start.6
  4.3 2.7 %collective-permute-start.2 = (bf16[704,256]{1,0:T(8,128)(2,1)S(1)}, bf16[704,256]{1,0:T(8,128)(2,1)S(1)}, u32[]{:S(2)}, u32[]{:S(2)}) collective-permute-start(bf16[704,256]{1,0:T(8,128)(2,1)S(1)} %get-tuple-element.60.refs_1_.refs_5_.refs_9_), channel_id=1, source_target_pairs={{0,4},{1,5},{4,8},{5,9},{8,12},{9,13},{12,14},{13,15},{14,10},{15,... | collective-permute-start | bytes 1081352 | tf_op jit(solution)/shard_map/ppermute | solution.py:34
  7.1 0.0 collective-permute-start.3
  7.1 2.0 %collective-permute-start.4 = (bf16[704,256]{1,0:T(8,128)(2,1)S(1)}, bf16[704,256]{1,0:T(8,128)(2,1)}, u32[]{:S(2)}, u32[]{:S(2)}) collective-permute-start(bf16[704,256]{1,0:T(8,128)(2,1)S(1)} %get-tuple-element.61.refs_10_.refs_2_), channel_id=1, source_target_pairs={{0,4},{1,5},{4,8},{5,9},{8,12},{9,13},{12,14},{13,15},{14,10},{15,... | collective-permute-start | bytes 1081352 | tf_op jit(solution)/shard_map/ppermute | solution.py:34
  9.1 0.0 collective-permute-start.5
  9.1 0.7 broadcast_compare_fusion
  9.8 0.0 copy-start
  9.8 0.0 copy-start.3
  9.8 3.8 %bitcast_select_fusion.acts.refs_8_.refs_4_ = bf16[512,7168]{1,0:T(8,128)(2,1)S(1)} fusion(bf16[2,256,7168]{2,1,0:T(8,128)(2,1)} %param.8, pred[512]{0:T(512)(128)(4,1)S(1)} %broadcast_in_dim.13), kind=kLoop, calls=%fused_computation | loop fusion | flops 3670016 | bytes 14680576 | tf_op jit(solution)/shard_map/jit(_where)/select_n | solution.py:429
  13.6 0.5 copy-done
  14.1 0.0 copy-done.3
  14.1 3.3 %shard_map.75.refs_7_.norms = f32[3,8,128]{2,1,0:T(8,128)S(1)} custom-call(bf16[512,4096]{1,0:T(8,128)(2,1)S(1)} %bitcast.4, bf16[512,7168]{1,0:T(8,128)(2,1)S(1)} %bitcast_select_fusion.acts.refs_8_.refs_4_, s32[16,64]{1,0:T(8,128)S(1)} %copy-done.3), custom_call_target="tpu_custom_call" | custom-call | flops 1 | bytes 1 | tf_op jit(solution)/shard_map/pallas_call | solution.py:347
  17.4 0.0 collective-permute-done.2.refs_2_.refs_6_.refs_11_.refs_3_
  17.4 0.9 %collective-permute-done.3.refs_3_.refs_7_.refs_13_.refs_5_ = bf16[704,256]{1,0:T(8,128)(2,1)S(1)} collective-permute-done((bf16[704,256]{1,0:T(8,128)(2,1)S(1)}, bf16[704,256]{1,0:T(8,128)(2,1)S(1)}, u32[]{:S(2)}, u32[]{:S(2)}) %collective-permute-start.3) | collective-permute-done | bytes 360480 | tf_op jit(solution)/shard_map/ppermute | solution.py:34
  18.3 5.4 %collective-permute-done.4.refs_12_.refs_4_ = bf16[704,256]{1,0:T(8,128)(2,1)} collective-permute-done((bf16[704,256]{1,0:T(8,128)(2,1)S(1)}, bf16[704,256]{1,0:T(8,128)(2,1)}, u32[]{:S(2)}, u32[]{:S(2)}) %collective-permute-start.4) | collective-permute-done | bytes 360480 | tf_op jit(solution)/shard_map/ppermute | solution.py:34
  23.8 1.5 %collective-permute-done.5.refs_14_.refs_6_ = bf16[704,256]{1,0:T(8,128)(2,1)} collective-permute-done((bf16[704,256]{1,0:T(8,128)(2,1)S(1)}, bf16[704,256]{1,0:T(8,128)(2,1)}, u32[]{:S(2)}, u32[]{:S(2)}) %collective-permute-start.5) | collective-permute-done | bytes 360480 | tf_op jit(solution)/shard_map/ppermute | solution.py:34
  25.3 0.0 collective-permute-done.6.refs_0_
  25.3 0.0 collective-permute-start.7
  25.3 1.6 %collective-permute-start.8 = (bf16[704,256]{1,0:T(8,128)(2,1)S(1)}, bf16[704,256]{1,0:T(8,128)(2,1)S(1)}, u32[]{:S(2)}, u32[]{:S(2)}) collective-permute-start(bf16[704,256]{1,0:T(8,128)(2,1)S(1)} %collective-permute-done.2.refs_2_.refs_6_.refs_11_.refs_3_), channel_id=1, source_target_pairs={{0,4},{1,5},{4,8},{5,9},{8,12},{9,13},{12,14},{13,15},{14,10},{15,... | collective-permute-start | bytes 1081352 | tf_op jit(solution)/shard_map/ppermute | solution.py:34
  26.9 0.4 collective-permute-start.9
  27.3 1.6 %collective-permute-start.12 = (bf16[704,256]{1,0:T(8,128)(2,1)}, bf16[704,256]{1,0:T(8,128)(2,1)S(1)}, u32[]{:S(2)}, u32[]{:S(2)}) collective-permute-start(bf16[704,256]{1,0:T(8,128)(2,1)} %collective-permute-done.4.refs_12_.refs_4_), channel_id=1, source_target_pairs={{0,4},{1,5},{4,8},{5,9},{8,12},{9,13},{12,14},{13,15},{14,10},{15,... | collective-permute-start | bytes 1081352 | tf_op jit(solution)/shard_map/ppermute | solution.py:34
  28.9 0.4 collective-permute-start.13
  29.4 4.8 %shard_map.76 = (f32[512,256]{1,0:T(8,128)S(1)}, f32[512,256]{1,0:T(8,128)S(1)}, f32[512,256]{1,0:T(8,128)S(1)}, bf16[512,4096]{1,0:T(8,128)(2,1)S(1)}) custom-call(bf16[512,4096]{1,0:T(8,128)(2,1)} %collective-permute-done.6.refs_0_, bf16[704,256]{1,0:T(8,128)(2,1)S(1)} %get-tuple-element.60.refs_1_.refs_5_.refs_9_, ...), custom_call_target="tpu_custom_call" | custom-call | flops 1 | bytes 1 | tf_op jit(solution)/shard_map/pallas_call | solution.py:215
  34.1 2.4 %collective-permute-done.8.refs_1_.refs_5_.refs_9_.refs_7_ = bf16[704,256]{1,0:T(8,128)(2,1)S(1)} collective-permute-done((bf16[704,256]{1,0:T(8,128)(2,1)S(1)}, bf16[704,256]{1,0:T(8,128)(2,1)S(1)}, u32[]{:S(2)}, u32[]{:S(2)}) %collective-permute-start.8) | collective-permute-done | bytes 360480 | tf_op jit(solution)/shard_map/ppermute | solution.py:34
  36.5 1.6 %collective-permute-done.9.refs_2_.refs_6_.refs_11_.refs_9_ = bf16[704,256]{1,0:T(8,128)(2,1)S(1)} collective-permute-done((bf16[704,256]{1,0:T(8,128)(2,1)S(1)}, bf16[704,256]{1,0:T(8,128)(2,1)S(1)}, u32[]{:S(2)}, u32[]{:S(2)}) %collective-permute-start.9) | collective-permute-done | bytes 360480 | tf_op jit(solution)/shard_map/ppermute | solution.py:34
  38.1 1.6 %collective-permute-start.10 = (bf16[704,256]{1,0:T(8,128)(2,1)S(1)}, bf16[704,256]{1,0:T(8,128)(2,1)S(1)}, u32[]{:S(2)}, u32[]{:S(2)}) collective-permute-start(bf16[704,256]{1,0:T(8,128)(2,1)S(1)} %collective-permute-done.8.refs_1_.refs_5_.refs_9_.refs_7_), channel_id=1, source_target_pairs={{0,4},{1,5},{4,8},{5,9},{8,12},{9,13},{12,14},{13,15},{14,10},{15,... | collective-permute-start | bytes 1081352 | tf_op jit(solution)/shard_map/ppermute | solution.py:34
  39.7 0.4 collective-permute-start.11
  40.2 4.1 %collective-permute-done.12.refs_10_.refs_8_ = bf16[704,256]{1,0:T(8,128)(2,1)S(1)} collective-permute-done((bf16[704,256]{1,0:T(8,128)(2,1)}, bf16[704,256]{1,0:T(8,128)(2,1)S(1)}, u32[]{:S(2)}, u32[]{:S(2)}) %collective-permute-start.12) | collective-permute-done | bytes 360480 | tf_op jit(solution)/shard_map/ppermute | solution.py:34
  44.2 1.6 %collective-permute-start.16 = (bf16[704,256]{1,0:T(8,128)(2,1)S(1)}, bf16[704,256]{1,0:T(8,128)(2,1)S(1)}, u32[]{:S(2)}, u32[]{:S(2)}) collective-permute-start(bf16[704,256]{1,0:T(8,128)(2,1)S(1)} %collective-permute-done.12.refs_10_.refs_8_), channel_id=1, source_target_pairs={{0,4},{1,5},{4,8},{5,9},{8,12},{9,13},{12,14},{13,15},{14,10},{15,... | collective-permute-start | bytes 1081352 | tf_op jit(solution)/shard_map/ppermute | solution.py:34
  45.8 0.0 collective-permute-done.13.refs_12_.refs_10_
  45.9 0.4 collective-permute-start.17
  46.3 1.6 %shard_map.77 = (f32[512,256]{1,0:T(8,128)S(1)}, f32[512,256]{1,0:T(8,128)S(1)}, f32[512,256]{1,0:T(8,128)S(1)}) custom-call(bf16[512,4096]{1,0:T(8,128)(2,1)S(1)} %get-tuple-element.79.refs_0_.refs_1_, bf16[704,256]{1,0:T(8,128)(2,1)S(1)} %collective-permute-done.8.refs_1_.refs_5_.refs_9_.refs_7_, ...), custom_call_target="tpu_custom_call", output_to_operand_aliasing={{0}: (3, {}), {1}: (7, {}), {2}: (13, {})} | custom-call | flops 1 | bytes 1 | tf_op jit(solution)/shard_map/pallas_call | solution.py:215
  47.9 4.1 %collective-permute-done.10.refs_1_.refs_5_ = bf16[704,256]{1,0:T(8,128)(2,1)S(1)} collective-permute-done((bf16[704,256]{1,0:T(8,128)(2,1)S(1)}, bf16[704,256]{1,0:T(8,128)(2,1)S(1)}, u32[]{:S(2)}, u32[]{:S(2)}) %collective-permute-start.10) | collective-permute-done | bytes 360480 | tf_op jit(solution)/shard_map/ppermute | solution.py:34
  52.0 1.6 %collective-permute-done.11.refs_2_.refs_7_ = bf16[704,256]{1,0:T(8,128)(2,1)S(1)} collective-permute-done((bf16[704,256]{1,0:T(8,128)(2,1)S(1)}, bf16[704,256]{1,0:T(8,128)(2,1)S(1)}, u32[]{:S(2)}, u32[]{:S(2)}) %collective-permute-start.11) | collective-permute-done | bytes 360480 | tf_op jit(solution)/shard_map/ppermute | solution.py:34
  53.6 1.6 %collective-permute-start.14 = (bf16[352,256]{1,0:T(8,128)(2,1)S(1)}, bf16[352,256]{1,0:T(8,128)(2,1)S(1)}, u32[]{:S(2)}, u32[]{:S(2)}) collective-permute-start(bf16[352,256]{1,0:T(8,128)(2,1)S(1)} %slice.12), channel_id=1, source_target_pairs={{0,4},{1,5},{4,8},{5,9},{8,12},{9,13},{12,14},{13,15},{14,10},{15,... | collective-permute-start | bytes 540680 | tf_op jit(solution)/shard_map/ppermute | solution.py:34
  55.2 0.5 collective-permute-start.15
  55.7 0.0 collective-permute-done.7.refs_0_.refs_4_.acts_other
  55.7 3.0 %shard_map.78.refs_9_ = f32[512,256]{1,0:T(8,128)S(1)} custom-call(bf16[512,7168]{1,0:T(8,128)(2,1)S(1)} %collective-permute-done.7.refs_0_.refs_4_.acts_other, bf16[704,256]{1,0:T(8,128)(2,1)S(1)} %get-tuple-element.60.refs_1_.refs_5_.refs_9_, bf16[704,256]{1,0:T(8,128)(2,1)S(1)} %get-tuple-element.61.refs_10_.refs_2_, ...), custom_call_target="tpu_custom_call" | custom-call | flops 1 | bytes 1 | tf_op jit(solution)/shard_map/pallas_call | solution.py:215
  58.8 0.9 %collective-permute-done.16.refs_6_ = bf16[704,256]{1,0:T(8,128)(2,1)S(1)} collective-permute-done((bf16[704,256]{1,0:T(8,128)(2,1)S(1)}, bf16[704,256]{1,0:T(8,128)(2,1)S(1)}, u32[]{:S(2)}, u32[]{:S(2)}) %collective-permute-start.16) | collective-permute-done | bytes 360480 | tf_op jit(solution)/shard_map/ppermute | solution.py:34
  59.7 1.6 %collective-permute-done.17.refs_8_ = bf16[704,256]{1,0:T(8,128)(2,1)S(1)} collective-permute-done((bf16[704,256]{1,0:T(8,128)(2,1)S(1)}, bf16[704,256]{1,0:T(8,128)(2,1)S(1)}, u32[]{:S(2)}, u32[]{:S(2)}) %collective-permute-start.17) | collective-permute-done | bytes 360480 | tf_op jit(solution)/shard_map/ppermute | solution.py:34
  61.3 1.6 %collective-permute-start.18 = (bf16[352,256]{1,0:T(8,128)(2,1)S(1)}, bf16[352,256]{1,0:T(8,128)(2,1)S(1)}, u32[]{:S(2)}, u32[]{:S(2)}) collective-permute-start(bf16[352,256]{1,0:T(8,128)(2,1)S(1)} %slice.14), channel_id=1, source_target_pairs={{0,4},{1,5},{4,8},{5,9},{8,12},{9,13},{12,14},{13,15},{14,10},{15,... | collective-permute-start | bytes 540680 | tf_op jit(solution)/shard_map/ppermute | solution.py:34
  63.0 0.5 collective-permute-start.19
  63.5 1.3 %shard_map.79 = (f32[512,256]{1,0:T(8,128)S(1)}, f32[512,256]{1,0:T(8,128)S(1)}) custom-call(bf16[512,4096]{1,0:T(8,128)(2,1)S(1)} %bitcast.7, bf16[704,256]{1,0:T(8,128)(2,1)S(1)} %collective-permute-done.10.refs_1_.refs_5_, bf16[704,256]{1,0:T(8,128)(2,1)S(1)} %collective-permute-done.11.refs_2_.refs_7_, ...), custom_call_target="tpu_custom_call", output_to_operand_aliasing={{0}: (3, {}), {1}: (9, {})} | custom-call | flops 1 | bytes 1 | tf_op jit(solution)/shard_map/pallas_call | solution.py:215
  64.8 1.3 %shard_map.80 = (f32[512,256]{1,0:T(8,128)S(1)}, f32[512,256]{1,0:T(8,128)S(1)}) custom-call(bf16[512,4096]{1,0:T(8,128)(2,1)S(1)} %get-tuple-element.79.refs_0_.refs_1_, bf16[704,256]{1,0:T(8,128)(2,1)S(1)} %collective-permute-done.10.refs_1_.refs_5_, ...), custom_call_target="tpu_custom_call", output_to_operand_aliasing={{0}: (3, {}), {1}: (9, {})} | custom-call | flops 1 | bytes 1 | tf_op jit(solution)/shard_map/pallas_call | solution.py:215
  66.0 0.0 copy-start.4
  66.1 0.0 collective-permute-done.14.refs_2_
  66.1 0.0 collective-permute-done.15.refs_3_.refs_0_
  66.1 0.5 shard_map.81
  66.5 0.5 collective-permute-done.18.refs_1_
  67.0 1.5 %collective-permute-done.19.refs_2_ = bf16[352,256]{1,0:T(8,128)(2,1)S(1)} collective-permute-done((bf16[352,256]{1,0:T(8,128)(2,1)S(1)}, bf16[352,256]{1,0:T(8,128)(2,1)S(1)}, u32[]{:S(2)}, u32[]{:S(2)}) %collective-permute-start.19) | collective-permute-done | bytes 180256 | tf_op jit(solution)/shard_map/ppermute | solution.py:34
  68.5 0.0 copy-done.4
  68.5 1.5 %shard_map.82 = f32[16,1,128]{2,1,0:T(1,128)S(1)} custom-call(s32[2]{0:T(128)S(1)} %copy-done.4, s32[2]{0:T(128)S(1)} %collective-permute-done.1.seq_index_other, bf16[512,7168]{1,0:T(8,128)(2,1)S(1)} %bitcast_select_fusion.acts.refs_8_.refs_4_, bf16[512,7168]{1,0:T(8,128)(2,1)S(1)} %collective-permute-done.7.refs_0_.refs_4_.acts_other, ...), custom_call_target="tpu_custom_call" | custom-call | flops 1 | bytes 1 | tf_op jit(solution)/shard_map/pallas_call | solution.py:321
  70.0 9.9 %all_to_all.5.parts = f32[16,1,128]{2,1,0:T(1,128)S(1)} all-to-all(f32[16,1,128]{2,1,0:T(1,128)S(1)} %shard_map.82), channel_id=1, replica_groups=mesh['groups'=2,'dp'=16] {'dp'}, dimensions={0} | all-to-all | bytes 16384 | tf_op jit(solution)/shard_map/all_to_all | solution.py:485
  79.9 0.7 shard_map.83
  (7 shorter events, 0.2 us)
Async XLA Ops:
  0.0 1.0 %copy-start.1 = (bf16[448,512]{1,0:T(8,128)(2,1)S(1)}, bf16[448,512]{1,0:T(8,128)(2,1)}, u32[]{:S(2)}) copy-start(bf16[448,512]{1,0:T(8,128)(2,1)} %right.1) | copy-start | bytes 1376260
  1.0 0.9 %copy-start.2 = (bf16[256,512]{1,0:T(8,128)(2,1)S(1)}, bf16[256,512]{1,0:T(8,128)(2,1)}, u32[]{:S(2)}) copy-start(bf16[256,512]{1,0:T(8,128)(2,1)} %left.1) | copy-start | bytes 786436
  2.0 1.8 %collective-permute-start = (bf16[704,256]{1,0:T(8,128)(2,1)S(1)}, bf16[704,256]{1,0:T(8,128)(2,1)S(1)}, u32[]{:S(2)}, u32[]{:S(2)}) collective-permute-start(bf16[704,256]{1,0:T(8,128)(2,1)S(1)} %get-tuple-element.57), channel_id=1, source_target_pairs={{0,1},{1,0},{2,3},{3,2},{4,5},{5,4},{6,7},{7,6},{8,9},{9,8},{10,11... | collective-permute-start | bytes 1081352 | tf_op jit(solution)/shard_map/ppermute | solution.py:34
  2.5 1.4 %collective-permute-start.1 = (s32[2]{0:T(128)}, s32[2]{0:T(128)S(1)}, u32[]{:S(2)}, u32[]{:S(2)}) collective-permute-start(s32[2]{0:T(128)} %seq_index), channel_id=1, source_target_pairs={{0,1},{1,0},{2,3},{3,2},{4,5},{5,4},{6,7},{7,6},{8,9},{9,8},{10,11... | collective-permute-start | bytes 32 | tf_op jit(solution)/shard_map/ppermute | solution.py:34
  4.0 21.3 %collective-permute-start.6 = (bf16[512,4096]{1,0:T(8,128)(2,1)}, bf16[512,4096]{1,0:T(8,128)(2,1)}, u32[]{:S(2)}, u32[]{:S(2)}) collective-permute-start(bf16[512,4096]{1,0:T(8,128)(2,1)} %bitcast.3), channel_id=1, source_target_pairs={{0,1},{1,0},{2,3},{3,2},{4,5},{5,4},{6,7},{7,6},{8,9},{9,8},{10,11... | collective-permute-start | bytes 12582920 | tf_op jit(solution)/shard_map/ppermute | solution.py:34
  4.3 13.1 %collective-permute-start.2 = (bf16[704,256]{1,0:T(8,128)(2,1)S(1)}, bf16[704,256]{1,0:T(8,128)(2,1)S(1)}, u32[]{:S(2)}, u32[]{:S(2)}) collective-permute-start(bf16[704,256]{1,0:T(8,128)(2,1)S(1)} %get-tuple-element.60.refs_1_.refs_5_.refs_9_), channel_id=1, source_target_pairs={{0,4},{1,5},{4,8},{5,9},{8,12},{9,13},{12,14},{13,15},{14,10},{15,... | collective-permute-start | bytes 1081352 | tf_op jit(solution)/shard_map/ppermute | solution.py:34
  7.1 11.3 %collective-permute-start.3 = (bf16[704,256]{1,0:T(8,128)(2,1)S(1)}, bf16[704,256]{1,0:T(8,128)(2,1)S(1)}, u32[]{:S(2)}, u32[]{:S(2)}) collective-permute-start(bf16[704,256]{1,0:T(8,128)(2,1)S(1)} %get-tuple-element.60.refs_1_.refs_5_.refs_9_), channel_id=1, source_target_pairs={{0,2},{1,3},{4,0},{5,1},{8,4},{9,5},{12,8},{13,9},{14,12},{15,13},... | collective-permute-start | bytes 1081352 | tf_op jit(solution)/shard_map/ppermute | solution.py:34
  7.1 16.7 %collective-permute-start.4 = (bf16[704,256]{1,0:T(8,128)(2,1)S(1)}, bf16[704,256]{1,0:T(8,128)(2,1)}, u32[]{:S(2)}, u32[]{:S(2)}) collective-permute-start(bf16[704,256]{1,0:T(8,128)(2,1)S(1)} %get-tuple-element.61.refs_10_.refs_2_), channel_id=1, source_target_pairs={{0,4},{1,5},{4,8},{5,9},{8,12},{9,13},{12,14},{13,15},{14,10},{15,... | collective-permute-start | bytes 1081352 | tf_op jit(solution)/shard_map/ppermute | solution.py:34
  9.1 16.2 %collective-permute-start.5 = (bf16[704,256]{1,0:T(8,128)(2,1)S(1)}, bf16[704,256]{1,0:T(8,128)(2,1)}, u32[]{:S(2)}, u32[]{:S(2)}) collective-permute-start(bf16[704,256]{1,0:T(8,128)(2,1)S(1)} %get-tuple-element.61.refs_10_.refs_2_), channel_id=1, source_target_pairs={{0,2},{1,3},{4,0},{5,1},{8,4},{9,5},{12,8},{13,9},{14,12},{15,13},... | collective-permute-start | bytes 1081352 | tf_op jit(solution)/shard_map/ppermute | solution.py:34
  9.8 4.3 %copy-start = (bf16[2,256,4096]{2,1,0:T(8,128)(2,1)S(1)}, bf16[2,256,4096]{2,1,0:T(8,128)(2,1)}, u32[]{:S(2)}) copy-start(bf16[2,256,4096]{2,1,0:T(8,128)(2,1)} %param.7) | copy-start | bytes 12582916
  9.8 4.3 %copy-start.3 = (s32[16,64]{1,0:T(8,128)S(1)}, s32[16,64]{1,0:T(8,128)}, u32[]{:S(2)}) copy-start(s32[16,64]{1,0:T(8,128)} %query_ids.1) | copy-start | bytes 12292
  25.3 30.4 %collective-permute-start.7 = (bf16[512,7168]{1,0:T(8,128)(2,1)S(1)}, bf16[512,7168]{1,0:T(8,128)(2,1)S(1)}, u32[]{:S(2)}, u32[]{:S(2)}) collective-permute-start(bf16[512,7168]{1,0:T(8,128)(2,1)S(1)} %bitcast_select_fusion.acts.refs_8_.refs_4_), channel_id=1, source_target_pairs={{0,1},{1,0},{2,3},{3,2},{4,5},{5,4},{6,7},{7,6},{8,9},{9,8},{10,11... | collective-permute-start | bytes 22020104 | tf_op jit(solution)/shard_map/ppermute | solution.py:34
  25.3 11.2 %collective-permute-start.8 = (bf16[704,256]{1,0:T(8,128)(2,1)S(1)}, bf16[704,256]{1,0:T(8,128)(2,1)S(1)}, u32[]{:S(2)}, u32[]{:S(2)}) collective-permute-start(bf16[704,256]{1,0:T(8,128)(2,1)S(1)} %collective-permute-done.2.refs_2_.refs_6_.refs_11_.refs_3_), channel_id=1, source_target_pairs={{0,4},{1,5},{4,8},{5,9},{8,12},{9,13},{12,14},{13,15},{14,10},{15,... | collective-permute-start | bytes 1081352 | tf_op jit(solution)/shard_map/ppermute | solution.py:34
  26.9 11.2 %collective-permute-start.9 = (bf16[704,256]{1,0:T(8,128)(2,1)S(1)}, bf16[704,256]{1,0:T(8,128)(2,1)S(1)}, u32[]{:S(2)}, u32[]{:S(2)}) collective-permute-start(bf16[704,256]{1,0:T(8,128)(2,1)S(1)} %collective-permute-done.3.refs_3_.refs_7_.refs_13_.refs_5_), channel_id=1, source_target_pairs={{0,2},{1,3},{4,0},{5,1},{8,4},{9,5},{12,8},{13,9},{14,12},{15,13},... | collective-permute-start | bytes 1081352 | tf_op jit(solution)/shard_map/ppermute | solution.py:34
  27.3 16.9 %collective-permute-start.12 = (bf16[704,256]{1,0:T(8,128)(2,1)}, bf16[704,256]{1,0:T(8,128)(2,1)S(1)}, u32[]{:S(2)}, u32[]{:S(2)}) collective-permute-start(bf16[704,256]{1,0:T(8,128)(2,1)} %collective-permute-done.4.refs_12_.refs_4_), channel_id=1, source_target_pairs={{0,4},{1,5},{4,8},{5,9},{8,12},{9,13},{12,14},{13,15},{14,10},{15,... | collective-permute-start | bytes 1081352 | tf_op jit(solution)/shard_map/ppermute | solution.py:34
  28.9 16.9 %collective-permute-start.13 = (bf16[704,256]{1,0:T(8,128)(2,1)}, bf16[704,256]{1,0:T(8,128)(2,1)S(1)}, u32[]{:S(2)}, u32[]{:S(2)}) collective-permute-start(bf16[704,256]{1,0:T(8,128)(2,1)} %collective-permute-done.5.refs_14_.refs_6_), channel_id=1, source_target_pairs={{0,2},{1,3},{4,0},{5,1},{8,4},{9,5},{12,8},{13,9},{14,12},{15,13},... | collective-permute-start | bytes 1081352 | tf_op jit(solution)/shard_map/ppermute | solution.py:34
  38.1 13.8 %collective-permute-start.10 = (bf16[704,256]{1,0:T(8,128)(2,1)S(1)}, bf16[704,256]{1,0:T(8,128)(2,1)S(1)}, u32[]{:S(2)}, u32[]{:S(2)}) collective-permute-start(bf16[704,256]{1,0:T(8,128)(2,1)S(1)} %collective-permute-done.8.refs_1_.refs_5_.refs_9_.refs_7_), channel_id=1, source_target_pairs={{0,4},{1,5},{4,8},{5,9},{8,12},{9,13},{12,14},{13,15},{14,10},{15,... | collective-permute-start | bytes 1081352 | tf_op jit(solution)/shard_map/ppermute | solution.py:34
  39.7 13.9 %collective-permute-start.11 = (bf16[704,256]{1,0:T(8,128)(2,1)S(1)}, bf16[704,256]{1,0:T(8,128)(2,1)S(1)}, u32[]{:S(2)}, u32[]{:S(2)}) collective-permute-start(bf16[704,256]{1,0:T(8,128)(2,1)S(1)} %collective-permute-done.9.refs_2_.refs_6_.refs_11_.refs_9_), channel_id=1, source_target_pairs={{0,2},{1,3},{4,0},{5,1},{8,4},{9,5},{12,8},{13,9},{14,12},{15,13},... | collective-permute-start | bytes 1081352 | tf_op jit(solution)/shard_map/ppermute | solution.py:34
  44.2 15.4 %collective-permute-start.16 = (bf16[704,256]{1,0:T(8,128)(2,1)S(1)}, bf16[704,256]{1,0:T(8,128)(2,1)S(1)}, u32[]{:S(2)}, u32[]{:S(2)}) collective-permute-start(bf16[704,256]{1,0:T(8,128)(2,1)S(1)} %collective-permute-done.12.refs_10_.refs_8_), channel_id=1, source_target_pairs={{0,4},{1,5},{4,8},{5,9},{8,12},{9,13},{12,14},{13,15},{14,10},{15,... | collective-permute-start | bytes 1081352 | tf_op jit(solution)/shard_map/ppermute | solution.py:34
  45.9 15.4 %collective-permute-start.17 = (bf16[704,256]{1,0:T(8,128)(2,1)S(1)}, bf16[704,256]{1,0:T(8,128)(2,1)S(1)}, u32[]{:S(2)}, u32[]{:S(2)}) collective-permute-start(bf16[704,256]{1,0:T(8,128)(2,1)S(1)} %collective-permute-done.13.refs_12_.refs_10_), channel_id=1, source_target_pairs={{0,2},{1,3},{4,0},{5,1},{8,4},{9,5},{12,8},{13,9},{14,12},{15,13},... | collective-permute-start | bytes 1081352 | tf_op jit(solution)/shard_map/ppermute | solution.py:34
  53.6 12.5 %collective-permute-start.14 = (bf16[352,256]{1,0:T(8,128)(2,1)S(1)}, bf16[352,256]{1,0:T(8,128)(2,1)S(1)}, u32[]{:S(2)}, u32[]{:S(2)}) collective-permute-start(bf16[352,256]{1,0:T(8,128)(2,1)S(1)} %slice.12), channel_id=1, source_target_pairs={{0,4},{1,5},{4,8},{5,9},{8,12},{9,13},{12,14},{13,15},{14,10},{15,... | collective-permute-start | bytes 540680 | tf_op jit(solution)/shard_map/ppermute | solution.py:34
  55.2 10.8 %collective-permute-start.15 = (bf16[352,256]{1,0:T(8,128)(2,1)S(1)}, bf16[352,256]{1,0:T(8,128)(2,1)S(1)}, u32[]{:S(2)}, u32[]{:S(2)}) collective-permute-start(bf16[352,256]{1,0:T(8,128)(2,1)S(1)} %slice.13), channel_id=1, source_target_pairs={{0,2},{1,3},{4,0},{5,1},{8,4},{9,5},{12,8},{13,9},{14,12},{15,13},... | collective-permute-start | bytes 540680 | tf_op jit(solution)/shard_map/ppermute | solution.py:34
  61.3 5.7 %collective-permute-start.18 = (bf16[352,256]{1,0:T(8,128)(2,1)S(1)}, bf16[352,256]{1,0:T(8,128)(2,1)S(1)}, u32[]{:S(2)}, u32[]{:S(2)}) collective-permute-start(bf16[352,256]{1,0:T(8,128)(2,1)S(1)} %slice.14), channel_id=1, source_target_pairs={{0,4},{1,5},{4,8},{5,9},{8,12},{9,13},{12,14},{13,15},{14,10},{15,... | collective-permute-start | bytes 540680 | tf_op jit(solution)/shard_map/ppermute | solution.py:34
  63.0 5.5 %collective-permute-start.19 = (bf16[352,256]{1,0:T(8,128)(2,1)S(1)}, bf16[352,256]{1,0:T(8,128)(2,1)S(1)}, u32[]{:S(2)}, u32[]{:S(2)}) collective-permute-start(bf16[352,256]{1,0:T(8,128)(2,1)S(1)} %slice.15), channel_id=1, source_target_pairs={{0,2},{1,3},{4,0},{5,1},{8,4},{9,5},{12,8},{13,9},{14,12},{15,13},... | collective-permute-start | bytes 540680 | tf_op jit(solution)/shard_map/ppermute | solution.py:34
  66.0 2.5 %copy-start.4 = (s32[2]{0:T(128)S(1)}, s32[2]{0:T(128)}, u32[]{:S(2)}) copy-start(s32[2]{0:T(128)} %seq_index) | copy-start | bytes 28
